TPU v7x, 256 devices: a whole 4x4x8 slice. The times are simulated.
256 devices in a mesh: pipe: 8 (over z_hi, x), edp: 32 (over y, z_lo, core).
Axes of the slice: x: 4, y: 4, z: 8 (z_hi: 2, z_lo: 4; z = z_hi * 4 + z_lo), core: 2. Of those that a mesh axis runs over, the one named last changes fastest.
Arguments:
- hidden_act: bfloat16 [65536, 1024], P(('pipe', 'edp')), may hold values from -24 to 24
- grad_out: bfloat16 [65536, 7168], P(('pipe', 'edp')), may hold values from -0.08984375 to 0.08984375
- live_tokens: int32 [8, 32], replicated, may hold values from 1 to 256, 2730 in all within a row
- block_count: int32 [8, 32], replicated, may hold values from 1 to 4, 64 in all within a row
- master: float32 [8, 1024, 7168], P('pipe', 'edp'), may hold values from -6 to 6
- moment1: bfloat16 [8, 1024, 7168], P('pipe', 'edp'), may hold values from -1.796875 to 1.796875
- moment2: bfloat16 [8, 1024, 7168], P('pipe', 'edp'), may hold values from 0.0099487305 to 1
Outputs:
- new_master: float32 [8, 1024, 7168], P('pipe', 'edp')
- new_first: bfloat16 [8, 1024, 7168], P('pipe', 'edp')
- new_second: bfloat16 [8, 1024, 7168], P('pipe', 'edp')
Inputs may be any that keep to these rules, and one draw needn't show every extreme that they name: live_tokens[p, e] counts the leading token slots of device (p, e) that hold routed tokens. Each row sums to 2730, and its largest entry is exactly 256. block_count[p, o] is the number of consecutive blocks of rank p's half that owner o holds, owners in order. Each row sums to 64, and its largest entry is exactly 4.
All inputs are finite; a program needn't handle non-finite values.
Results may differ from a plain program's by a relative error of at most 0.0085.
Values may be sent and summed in bfloat16 or wider, within the bound.
No kernel may reach another device: no remote copies, remote signals or barrier semaphores. Data moves between devices by JAX's collectives and lax.ppermute only.
A program may use at most 128 MiB of HBM per device.

v0:
```python
import functools
import jax
import jax.numpy as jnp
from jax import lax
from jax.experimental import pallas as pl
from jax.experimental.pallas import tpu as pltpu
from jax.sharding import Mesh, PartitionSpec as P

BLK = 8
CHUNKS = (512, 384)
NY, NZ, NC = 4, 4, 2
OFFSETS = tuple((dy, dc) for dy in range(NY) for dc in range(NC))

beta_first = 0.9
beta_second = 0.95
learn_rate = 0.00022
weight_decay = 0.1
adam_eps = 1e-08
bias_first = 1.0 - 0.9**20
bias_second = 1.0 - 0.95**20

bf16 = jnp.bfloat16
f32 = jnp.float32
VMEM = pl.BlockSpec(memory_space=pltpu.VMEM)
SMEM = pl.BlockSpec(memory_space=pltpu.SMEM)
ANY = pl.BlockSpec(memory_space=pl.ANY)
PARAMS = pltpu.CompilerParams(vmem_limit_bytes=40 * 1024 * 1024)


def send_group(value, dy, dc):
    if dy == 0 and dc == 0:
        return value
    pairs = []
    for y in range(NY):
        for c in range(NC):
            pairs.append((y * NC + c, (y + dy) % NY * NC + (c ^ dc)))
    return lax.ppermute(value, ("y", "c"), pairs)


def send_ring(value, steps):
    pairs = []
    for z in range(NZ):
        pairs.append((z, (z + steps) % NZ))
        pairs.append((NZ + z, NZ + (z + NZ - steps) % NZ))
    return lax.ppermute(value, ("zh", "z"), pairs)


def send_mirror(value):
    pairs = []
    for zh in range(2):
        for x in range(4):
            for z in range(NZ):
                source = (zh * 4 + x) * NZ + z
                target = ((1 - zh) * 4 + 3 - x) * NZ + NZ - 1 - z
                pairs.append((source, target))
    return lax.ppermute(value, ("zh", "x", "z"), pairs)


def ring_rank():
    z = lax.axis_index("z")
    return jnp.where(lax.axis_index("zh") == 0, z, NZ - 1 - z)


def prepare_kernel(live_ref, hidden_ref, out_ref):
    zh, x = lax.axis_index("zh"), lax.axis_index("x")
    y, z, c = lax.axis_index("y"), lax.axis_index("z"), lax.axis_index("c")
    live = live_ref[zh * 4 + x, (y * NZ + z) * NC + c]
    rank = jnp.where(zh == 0, z, NZ - 1 - z)
    rows = hidden_ref.shape[0]
    keep = lax.broadcasted_iota(jnp.int32, (128, rows), 1) < live
    for step in range(NZ):
        part = lax.rem(rank + 2 * NZ - 1 - step, NZ)
        for other in range(2):
            half = zh if other == 0 else 1 - zh
            block = (half * NZ + part) * 128
            cols = hidden_ref[:, pl.ds(pl.multiple_of(block, 128), 128)]
            turned = jnp.where(keep, cols.astype(f32).T, 0.0).astype(bf16)
            at = (step * 2 + other) * 128
            out_ref[at:at + 128, :] = turned


def prepare(hidden, live_tokens):
    return pl.pallas_call(
        prepare_kernel,
        out_shape=jax.ShapeDtypeStruct((hidden.shape[1], hidden.shape[0]), bf16),
        in_specs=[SMEM, VMEM],
        out_specs=VMEM,
        compiler_params=PARAMS,
        name="prepare",
    )(live_tokens, hidden)


def columns_of(y, c, base, cols):
    return pl.ds(pl.multiple_of((y * NC + c) * sum(CHUNKS) + base, 128), cols)


def pack_kernel(base, cols, grad_ref, after_ref, *rest):
    out_refs, sem = rest[:-1], rest[-1]
    y, c = lax.axis_index("y"), lax.axis_index("c")
    copies = []
    for i, out_ref in enumerate(out_refs):
        for other in range(NC):
            source = columns_of(lax.rem(y + i + 1, NY), lax.rem(c + other, NC), base, cols)
            copies.append(
                pltpu.make_async_copy(
                    grad_ref.at[:, source],
                    out_ref.at[:, other * cols:(other + 1) * cols],
                    sem.at[i * NC + other],
                )
            )
    for copy in copies:
        copy.start()
    for copy in copies:
        copy.wait()


def pack(grad, base, cols, after):
    shapes = [jax.ShapeDtypeStruct((grad.shape[0], NC * cols), bf16)] * (NY - 1)
    return pl.pallas_call(
        functools.partial(pack_kernel, base, cols),
        out_shape=shapes,
        in_specs=[ANY, ANY],
        out_specs=[ANY] * len(shapes),
        scratch_shapes=[pltpu.SemaphoreType.DMA((NC * len(shapes),))],
        compiler_params=PARAMS,
        name="pack",
    )(grad, after)


def product_kernel(base, cols, *refs):
    hidden, grad_ref, grads = refs[:NY], refs[NY], refs[NY + 1:2 * NY]
    outs, other_ref = refs[2 * NY:2 * NY + NZ], refs[2 * NY + NZ]
    left, right, sem = refs[2 * NY + NZ + 1:]
    y, c = lax.axis_index("y"), lax.axis_index("c")
    rows, depth = outs[0].shape[0], grad_ref.shape[0]
    copies = []
    for i in range(NY):
        tokens = slice(i * depth, (i + 1) * depth)
        copies.append((hidden[i], left.at[:, tokens]))
        if i:
            copies.append((grads[i - 1], right.at[tokens, :]))
        else:
            for other in range(NC):
                source = columns_of(y, lax.rem(c + other, NC), base, cols)
                target = right.at[tokens, other * cols:(other + 1) * cols]
                copies.append((grad_ref.at[:, source], target))
    copies = [pltpu.make_async_copy(a, b, sem.at[i]) for i, (a, b) in enumerate(copies)]
    for copy in copies:
        copy.start()
    for copy in copies:
        copy.wait()
    for step, out_ref in enumerate(outs):
        at = slice(step * rows, (step + 1) * rows)
        total = jnp.dot(left[at, :], right[...], preferred_element_type=f32)
        out_ref[...] = total[:, :cols].astype(bf16)
        other_ref[at, :] = total[:, cols:].astype(bf16)


def product(hidden, grad, grads, base, cols):
    width, tokens = hidden[0].shape
    depth = NY * tokens
    shapes = [jax.ShapeDtypeStruct((width // NZ, cols), bf16)] * NZ
    shapes.append(jax.ShapeDtypeStruct((width, cols), bf16))
    return pl.pallas_call(
        functools.partial(product_kernel, base, cols),
        out_shape=shapes,
        in_specs=[ANY] * (2 * NY),
        out_specs=[VMEM] * len(shapes),
        scratch_shapes=[
            pltpu.VMEM((width, depth), bf16),
            pltpu.VMEM((depth, NC * cols), bf16),
            pltpu.SemaphoreType.DMA((2 * NY + 1,)),
        ],
        compiler_params=PARAMS,
        cost_estimate=pl.CostEstimate(
            flops=2 * width * NC * cols * depth,
            bytes_accessed=2 * (width * (depth + NC * cols) + depth * NC * cols),
            transcendentals=0,
        ),
        name="product",
    )(*hidden, grad, *grads)


def adamw_kernel(*refs):
    counts_ref, owned_refs = refs[0], refs[1:1 + NY]
    master_ref, first_ref, second_ref, new_master_ref, new_first_ref, new_second_ref = refs[1 + NY:]
    zh, x = lax.axis_index("zh"), lax.axis_index("x")
    y, z, c = lax.axis_index("y"), lax.axis_index("z"), lax.axis_index("c")
    held = counts_ref[zh * 4 + x, (y * NZ + z) * NC + c]
    slots, cols = master_ref.shape[0], sum(CHUNKS)
    valid = lax.broadcasted_iota(jnp.int32, (slots, cols), 0) < held * BLK
    for dy in range(NY):
        for other in range(NC):
            at = columns_of(lax.rem(y + NY - dy, NY), lax.rem(c + other, NC), 0, cols)
            owned = owned_refs[dy][other].astype(f32)
            param = master_ref[:, at]
            first = beta_first * first_ref[:, at].astype(f32) + (1.0 - beta_first) * owned
            second = beta_second * second_ref[:, at].astype(f32) + (1.0 - beta_second) * owned * owned
            direction = first / bias_first / (jnp.sqrt(second / bias_second) + adam_eps)
            updated = param - learn_rate * (direction + weight_decay * param)
            new_master_ref[:, at] = jnp.where(valid, updated, 0.0)
            new_first_ref[:, at] = jnp.where(valid, first, 0.0).astype(bf16)
            new_second_ref[:, at] = jnp.where(valid, second, 0.0).astype(bf16)


def adamw(block_count, owned, master, moment1, moment2):
    shapes = [jax.ShapeDtypeStruct(a.shape, a.dtype) for a in (master, moment1, moment2)]
    return pl.pallas_call(
        adamw_kernel,
        out_shape=shapes,
        in_specs=[SMEM] + [VMEM] * (len(owned) + 3),
        out_specs=[VMEM] * 3,
        compiler_params=PARAMS,
        name="adamw",
    )(block_count, *owned, master, moment1, moment2)


def slot_choice(block_count, hblk, cap):
    y, z, c = lax.axis_index("y"), lax.axis_index("z"), lax.axis_index("c")
    counts = block_count[lax.axis_index("zh") * 4 + lax.axis_index("x")]
    owners = []
    for dy, dc in OFFSETS:
        owners.append(((y + dy) % NY * NZ + z) * NC + (c ^ dc))
    owners = jnp.stack(owners)
    before = jnp.arange(counts.shape[0], dtype=jnp.int32)[None, :] < owners[:, None]
    starts = jnp.sum(jnp.where(before, counts[None, :], 0), axis=1)
    slot = jnp.arange(cap, dtype=jnp.int32)
    block = jnp.minimum(starts[:, None] + slot[None, :], hblk - 1)
    per = hblk // NZ
    place = (ring_rank() + NZ - block // per) % NZ * per + block % per
    rows = place[:, :, None] * BLK + jnp.arange(BLK, dtype=jnp.int32)
    rows = rows.reshape(-1)
    return (rows[:, None] == jnp.arange(hblk * BLK, dtype=jnp.int32)[None, :]).astype(bf16)


def per_device(hidden_act, grad_out, live_tokens, block_count, master, moment1, moment2):
    half = hidden_act.shape[1] // 2
    slots = master.shape[1]
    turned = prepare(hidden_act, live_tokens)
    hidden = [send_group(turned, dy, 0) for dy in range(NY)]
    choice = slot_choice(block_count, half // BLK, slots // BLK)
    mine, swapped = [], []
    base = 0
    for k, cols in enumerate(CHUNKS):
        packed = pack(grad_out, base, cols, turned if k == 0 else hidden[1])
        grads = [send_group(packed[dy - 1], dy, 0) for dy in range(1, NY)]
        parts = product(hidden, grad_out, grads, base, cols)
        base += cols
        rows = parts[0].shape[0]
        sibling = send_group(parts[NZ], 0, 1)
        moving = None
        for step in range(NZ):
            total = parts[step].astype(f32) + sibling[step * rows:(step + 1) * rows].astype(f32)
            if step:
                total = total + send_ring(moving, 1).astype(f32)
            moving = total.astype(bf16)
        rows = rows // 2
        tile = (total[:rows] + send_mirror(moving[rows:]).astype(f32)).astype(bf16)
        gathered = jnp.concatenate([tile] + [send_ring(tile, d) for d in range(1, NZ)], 0)
        picked = jnp.dot(choice, gathered, preferred_element_type=f32).astype(bf16)
        picked = picked.reshape(NY, NC, slots, cols)
        mine.append(picked[:, 0])
        swapped.append(send_group(picked[:, 1], 0, 1))
    mine, swapped = jnp.concatenate(mine, 2), jnp.concatenate(swapped, 2)
    both = jnp.stack([mine, swapped], 1)
    owned = [send_group(both[dy], dy, 0) for dy in range(NY)]
    outs = adamw(block_count, owned, master[0], moment1[0], moment2[0])
    return tuple(out[None] for out in outs)


def solution(mesh):
    fine = Mesh(mesh.devices.reshape(2, 4, NY, NZ, NC), ("zh", "x", "y", "z", "c"))
    pipe, edp = ("zh", "x"), ("y", "z", "c")
    shard = P(pipe, edp, None)
    tokens = P(pipe + edp, None)
    return jax.shard_map(
        per_device,
        mesh=fine,
        in_specs=(tokens, tokens, P(), P(), shard, shard, shard),
        out_specs=(shard, shard, shard),
        check_vma=False,
    )
```

profile of v0, /device:TPU:1, one launch (start us, length us, event | category | flops | bytes accessed | tf_op | source)
XLA Modules:
  0.0 172.4 jit_solution(2215023679851733695)
XLA Ops:
  5.5 2.2 %collective-permute-start.3 = (bf16[256,1024]{1,0:T(8,128)(2,1)S(1)}, bf16[256,1024]{1,0:T(8,128)(2,1)S(1)}, u32[]{:S(2)}, u32[]{:S(2)}) collective-permute-start(bf16[256,1024]{1,0:T(8,128)(2,1)S(1)} %get-tuple-element.22), channel_id=1, source_target_pairs={{0,8},{1,9},{8,16},{9,17},{16,24},{17,25},{24,0},{25,1},{2,10},{3,... | collective-permute-start | bytes 1572872 | tf_op jit(solution)/shard_map/ppermute | solution.py:37
  12.7 6.0 %collective-permute-done.3.refs_5_ = bf16[256,1024]{1,0:T(8,128)(2,1)S(1)} collective-permute-done((bf16[256,1024]{1,0:T(8,128)(2,1)S(1)}, bf16[256,1024]{1,0:T(8,128)(2,1)S(1)}, u32[]{:S(2)}, u32[]{:S(2)}) %collective-permute-start.3) | collective-permute-done | bytes 524320 | tf_op jit(solution)/shard_map/ppermute | solution.py:37
  18.7 3.2 %collective-permute-start.2 = (bf16[1024,256]{1,0:T(8,128)(2,1)S(1)}, bf16[1024,256]{1,0:T(8,128)(2,1)S(1)}, u32[]{:S(2)}, u32[]{:S(2)}) collective-permute-start(bf16[1024,256]{1,0:T(8,128)(2,1)S(1)} %prepare.1.after_ref.refs_0_), channel_id=1, source_target_pairs={{0,24},{1,25},{8,0},{9,1},{16,8},{17,9},{24,16},{25,17},{2,26},{3,... | collective-permute-start | bytes 1572872 | tf_op jit(solution)/shard_map/ppermute | solution.py:37
  21.9 22.2 %collective-permute-done.4.refs_6_ = bf16[256,1024]{1,0:T(8,128)(2,1)S(1)} collective-permute-done((bf16[256,1024]{1,0:T(8,128)(2,1)S(1)}, bf16[256,1024]{1,0:T(8,128)(2,1)S(1)}, u32[]{:S(2)}, u32[]{:S(2)}) %collective-permute-start.4) | collective-permute-done | bytes 524320 | tf_op jit(solution)/shard_map/ppermute | solution.py:37
  44.1 11.2 %collective-permute-done.1.refs_2_ = bf16[1024,256]{1,0:T(8,128)(2,1)S(1)} collective-permute-done((bf16[1024,256]{1,0:T(8,128)(2,1)S(1)}, bf16[1024,256]{1,0:T(8,128)(2,1)S(1)}, u32[]{:S(2)}, u32[]{:S(2)}) %collective-permute-start.1) | collective-permute-done | bytes 524320 | tf_op jit(solution)/shard_map/ppermute | solution.py:37
  56.0 2.9 %product.2 = (bf16[256,512]{1,0:T(8,128)(2,1)S(1)}, bf16[256,512]{1,0:T(8,128)(2,1)S(1)}, bf16[256,512]{1,0:T(8,128)(2,1)S(1)}, bf16[256,512]{1,0:T(8,128)(2,1)S(1)}, bf16[1024,512]{1,0:T(8,128)(2,1)S(1)}) custom-call(bf16[1024,256]{1,0:T(8,128)(2,1)S(1)} %prepare.1.after_ref.refs_0_, bf16[1024,256]{1,0:T(8,128)(2,1)S(1)} %collective-permute-done.refs_1_.after_ref, ...), custom_call_target="tpu_custom_call" | custom-call | flops 2147483648 | bytes 6291456 | tf_op jit(solution)/shard_map/product/pallas_call | solution.py:164
  62.3 2.1 %collective-permute-start.15 = (bf16[256,768]{1,0:T(8,128)(2,1)S(1)}, bf16[256,768]{1,0:T(8,128)(2,1)S(1)}, u32[]{:S(2)}, u32[]{:S(2)}) collective-permute-start(bf16[256,768]{1,0:T(8,128)(2,1)S(1)} %get-tuple-element.31), channel_id=1, source_target_pairs={{0,16},{1,17},{8,24},{9,25},{16,0},{17,1},{24,8},{25,9},{2,18},{3,... | collective-permute-start | bytes 1179656 | tf_op jit(solution)/shard_map/ppermute | solution.py:37
  65.6 7.2 %collective-permute-done.14.refs_5_ = bf16[256,768]{1,0:T(8,128)(2,1)S(1)} collective-permute-done((bf16[256,768]{1,0:T(8,128)(2,1)S(1)}, bf16[256,768]{1,0:T(8,128)(2,1)S(1)}, u32[]{:S(2)}, u32[]{:S(2)}) %collective-permute-start.14) | collective-permute-done | bytes 393248 | tf_op jit(solution)/shard_map/ppermute | solution.py:37
  72.8 9.2 %collective-permute-done.15.refs_6_ = bf16[256,768]{1,0:T(8,128)(2,1)S(1)} collective-permute-done((bf16[256,768]{1,0:T(8,128)(2,1)S(1)}, bf16[256,768]{1,0:T(8,128)(2,1)S(1)}, u32[]{:S(2)}, u32[]{:S(2)}) %collective-permute-start.15) | collective-permute-done | bytes 393248 | tf_op jit(solution)/shard_map/ppermute | solution.py:37
  82.0 3.7 %product.3 = (bf16[256,384]{1,0:T(8,128)(2,1)S(1)}, bf16[256,384]{1,0:T(8,128)(2,1)S(1)}, bf16[256,384]{1,0:T(8,128)(2,1)S(1)}, bf16[256,384]{1,0:T(8,128)(2,1)S(1)}, bf16[1024,384]{1,0:T(8,128)(2,1)}) custom-call(bf16[1024,256]{1,0:T(8,128)(2,1)S(1)} %prepare.1.after_ref.refs_0_, bf16[1024,256]{1,0:T(8,128)(2,1)S(1)} %collective-permute-done.refs_1_.after_ref, ...), custom_call_target="tpu_custom_call" | custom-call | flops 1610612736 | bytes 5242880 | tf_op jit(solution)/shard_map/product/pallas_call | solution.py:164
  92.5 6.4 %collective-permute-done.7 = bf16[256,512]{1,0:T(8,128)(2,1)S(1)} collective-permute-done((bf16[256,512]{1,0:T(8,128)(2,1)S(1)}, bf16[256,512]{1,0:T(8,128)(2,1)S(1)}, u32[]{:S(2)}, u32[]{:S(2)}) %collective-permute-start.7) | collective-permute-done | bytes 262176 | tf_op jit(solution)/shard_map/ppermute | solution.py:45
  100.2 3.0 %collective-permute-done.18 = bf16[256,384]{1,0:T(8,128)(2,1)S(1)} collective-permute-done((bf16[256,384]{1,0:T(8,128)(2,1)S(1)}, bf16[256,384]{1,0:T(8,128)(2,1)S(1)}, u32[]{:S(2)}, u32[]{:S(2)}) %collective-permute-start.18) | collective-permute-done | bytes 196640 | tf_op jit(solution)/shard_map/ppermute | solution.py:45
  104.3 4.5 %collective-permute-done.8 = bf16[256,512]{1,0:T(8,128)(2,1)S(1)} collective-permute-done((bf16[256,512]{1,0:T(8,128)(2,1)S(1)}, bf16[256,512]{1,0:T(8,128)(2,1)S(1)}, u32[]{:S(2)}, u32[]{:S(2)}) %collective-permute-start.8) | collective-permute-done | bytes 262176 | tf_op jit(solution)/shard_map/ppermute | solution.py:45
  109.9 3.1 %collective-permute-done.19 = bf16[256,384]{1,0:T(8,128)(2,1)S(1)} collective-permute-done((bf16[256,384]{1,0:T(8,128)(2,1)S(1)}, bf16[256,384]{1,0:T(8,128)(2,1)S(1)}, u32[]{:S(2)}, u32[]{:S(2)}) %collective-permute-start.19) | collective-permute-done | bytes 196640 | tf_op jit(solution)/shard_map/ppermute | solution.py:45
  114.3 8.5 %collective-permute-done.20 = bf16[256,384]{1,0:T(8,128)(2,1)S(1)} collective-permute-done((bf16[256,384]{1,0:T(8,128)(2,1)S(1)}, bf16[256,384]{1,0:T(8,128)(2,1)S(1)}, u32[]{:S(2)}, u32[]{:S(2)}) %collective-permute-start.20) | collective-permute-done | bytes 196640 | tf_op jit(solution)/shard_map/ppermute | solution.py:45
  123.8 6.6 %collective-permute-start.21 = (bf16[128,384]{1,0:T(8,128)(2,1)S(1)}, bf16[128,384]{1,0:T(8,128)(2,1)S(1)}, u32[]{:S(2)}, u32[]{:S(2)}) collective-permute-start(bf16[128,384]{1,0:T(8,128)(2,1)S(1)} %slice.147), channel_id=1, source_target_pairs={{0,230},{2,228},{4,226},{6,224},{32,198},{34,196},{36,194},{38,192... | collective-permute-start | bytes 294920 | tf_op jit(solution)/shard_map/ppermute | solution.py:56
  131.5 4.6 %collective-permute-done.21 = bf16[128,384]{1,0:T(8,128)(2,1)S(1)} collective-permute-done((bf16[128,384]{1,0:T(8,128)(2,1)S(1)}, bf16[128,384]{1,0:T(8,128)(2,1)S(1)}, u32[]{:S(2)}, u32[]{:S(2)}) %collective-permute-start.21) | collective-permute-done | bytes 98336 | tf_op jit(solution)/shard_map/ppermute | solution.py:56
  136.4 3.2 %collective-permute-start.24 = (bf16[128,384]{1,0:T(8,128)(2,1)S(1)}, bf16[128,384]{1,0:T(8,128)(2,1)S(1)}, u32[]{:S(2)}, u32[]{:S(2)}) collective-permute-start(bf16[128,384]{1,0:T(8,128)(2,1)S(1)} %fusion.17), channel_id=1, source_target_pairs={{0,6},{128,130},{2,0},{130,132},{4,2},{132,134},{6,4},{134,128},{1... | collective-permute-start | bytes 294920 | tf_op jit(solution)/shard_map/ppermute | solution.py:45
  143.9 3.7 %collective-permute-done.11 = bf16[128,512]{1,0:T(8,128)(2,1)S(1)} collective-permute-done((bf16[128,512]{1,0:T(8,128)(2,1)S(1)}, bf16[128,512]{1,0:T(8,128)(2,1)S(1)}, u32[]{:S(2)}, u32[]{:S(2)}) %collective-permute-start.11) | collective-permute-done | bytes 131104 | tf_op jit(solution)/shard_map/ppermute | solution.py:45
  147.6 8.3 %collective-permute-done.12 = bf16[128,512]{1,0:T(8,128)(2,1)S(1)} collective-permute-done((bf16[128,512]{1,0:T(8,128)(2,1)S(1)}, bf16[128,512]{1,0:T(8,128)(2,1)S(1)}, u32[]{:S(2)}, u32[]{:S(2)}) %collective-permute-start.12) | collective-permute-done | bytes 131104 | tf_op jit(solution)/shard_map/ppermute | solution.py:45
  156.3 2.4 %collective-permute-start.25 = (bf16[4,32,512]{2,1,0:T(8,128)(2,1)S(1)}, bf16[4,32,512]{2,1,0:T(8,128)(2,1)S(1)}, u32[]{:S(2)}, u32[]{:S(2)}) collective-permute-start(bf16[4,32,512]{2,1,0:T(8,128)(2,1)S(1)} %get-tuple-element.45), channel_id=1, source_target_pairs={{0,1},{1,0},{8,9},{9,8},{16,17},{17,16},{24,25},{25,24},{2,3},{3,2... | collective-permute-start | bytes 393224 | tf_op jit(solution)/shard_map/ppermute | solution.py:37
  161.7 2.1 %collective-permute-start.28 = (bf16[2,32,896]{2,1,0:T(8,128)(2,1)S(1)}, bf16[2,32,896]{2,1,0:T(8,128)(2,1)S(1)}, u32[]{:S(2)}, u32[]{:S(2)}) collective-permute-start(bf16[2,32,896]{2,1,0:T(8,128)(2,1)S(1)} %get-tuple-element.44), channel_id=1, source_target_pairs={{0,16},{1,17},{8,24},{9,25},{16,0},{17,1},{24,8},{25,9},{2,18},{3,... | collective-permute-start | bytes 344072 | tf_op jit(solution)/shard_map/ppermute | solution.py:37
  166.3 3.1 %collective-permute-done.28.refs_3_ = bf16[2,32,896]{2,1,0:T(8,128)(2,1)S(1)} collective-permute-done((bf16[2,32,896]{2,1,0:T(8,128)(2,1)S(1)}, bf16[2,32,896]{2,1,0:T(8,128)(2,1)S(1)}, u32[]{:S(2)}, u32[]{:S(2)}) %collective-permute-start.28) | collective-permute-done | bytes 114720 | tf_op jit(solution)/shard_map/ppermute | solution.py:37
  169.4 3.0 %adamw.1 = (f32[32,7168]{1,0:T(8,128)}, bf16[32,7168]{1,0:T(8,128)(2,1)}, bf16[32,7168]{1,0:T(8,128)(2,1)}) custom-call(s32[8,32]{1,0:T(8,128)S(1)} %copy-done.7, bf16[2,32,896]{2,1,0:T(8,128)(2,1)S(1)} %get-tuple-element.42.refs_1_, bf16[2,32,896]{2,1,0:T(8,128)(2,1)S(1)} %collective-permute-done.27.refs_2_, ...), custom_call_target="tpu_custom_call" | custom-call | tf_op jit(solution)/shard_map/adamw/pallas_call | solution.py:208
  (83 shorter events, 39.2 us)
Async XLA Ops:
  5.5 13.3 %collective-permute-start.3 = (bf16[256,1024]{1,0:T(8,128)(2,1)S(1)}, bf16[256,1024]{1,0:T(8,128)(2,1)S(1)}, u32[]{:S(2)}, u32[]{:S(2)}) collective-permute-start(bf16[256,1024]{1,0:T(8,128)(2,1)S(1)} %get-tuple-element.22), channel_id=1, source_target_pairs={{0,8},{1,9},{8,16},{9,17},{16,24},{17,25},{24,0},{25,1},{2,10},{3,... | collective-permute-start | bytes 1572872 | tf_op jit(solution)/shard_map/ppermute | solution.py:37
  7.7 36.4 %collective-permute-start = (bf16[1024,256]{1,0:T(8,128)(2,1)S(1)}, bf16[1024,256]{1,0:T(8,128)(2,1)S(1)}, u32[]{:S(2)}, u32[]{:S(2)}) collective-permute-start(bf16[1024,256]{1,0:T(8,128)(2,1)S(1)} %prepare.1.after_ref.refs_0_), channel_id=1, source_target_pairs={{0,8},{1,9},{8,16},{9,17},{16,24},{17,25},{24,0},{25,1},{2,10},{3,... | collective-permute-start | bytes 1572872 | tf_op jit(solution)/shard_map/ppermute | solution.py:37
  9.0 35.1 %collective-permute-start.4 = (bf16[256,1024]{1,0:T(8,128)(2,1)S(1)}, bf16[256,1024]{1,0:T(8,128)(2,1)S(1)}, u32[]{:S(2)}, u32[]{:S(2)}) collective-permute-start(bf16[256,1024]{1,0:T(8,128)(2,1)S(1)} %get-tuple-element.23), channel_id=1, source_target_pairs={{0,16},{1,17},{8,24},{9,25},{16,0},{17,1},{24,8},{25,9},{2,18},{3,... | collective-permute-start | bytes 1572872 | tf_op jit(solution)/shard_map/ppermute | solution.py:37
  10.4 33.7 %collective-permute-start.5 = (bf16[256,1024]{1,0:T(8,128)(2,1)S(1)}, bf16[256,1024]{1,0:T(8,128)(2,1)S(1)}, u32[]{:S(2)}, u32[]{:S(2)}) collective-permute-start(bf16[256,1024]{1,0:T(8,128)(2,1)S(1)} %get-tuple-element.24), channel_id=1, source_target_pairs={{0,24},{1,25},{8,0},{9,1},{16,8},{17,9},{24,16},{25,17},{2,26},{3,... | collective-permute-start | bytes 1572872 | tf_op jit(solution)/shard_map/ppermute | solution.py:37
  12.4 43.0 %collective-permute-start.1 = (bf16[1024,256]{1,0:T(8,128)(2,1)S(1)}, bf16[1024,256]{1,0:T(8,128)(2,1)S(1)}, u32[]{:S(2)}, u32[]{:S(2)}) collective-permute-start(bf16[1024,256]{1,0:T(8,128)(2,1)S(1)} %prepare.1.after_ref.refs_0_), channel_id=1, source_target_pairs={{0,16},{1,17},{8,24},{9,25},{16,0},{17,1},{24,8},{25,9},{2,18},{3,... | collective-permute-start | bytes 1572872 | tf_op jit(solution)/shard_map/ppermute | solution.py:37
  18.7 37.3 %collective-permute-start.2 = (bf16[1024,256]{1,0:T(8,128)(2,1)S(1)}, bf16[1024,256]{1,0:T(8,128)(2,1)S(1)}, u32[]{:S(2)}, u32[]{:S(2)}) collective-permute-start(bf16[1024,256]{1,0:T(8,128)(2,1)S(1)} %prepare.1.after_ref.refs_0_), channel_id=1, source_target_pairs={{0,24},{1,25},{8,0},{9,1},{16,8},{17,9},{24,16},{25,17},{2,26},{3,... | collective-permute-start | bytes 1572872 | tf_op jit(solution)/shard_map/ppermute | solution.py:37
  58.9 27.8 %collective-permute-start.6 = (bf16[1024,512]{1,0:T(8,128)(2,1)S(1)}, bf16[1024,512]{1,0:T(8,128)(2,1)}, u32[]{:S(2)}, u32[]{:S(2)}) collective-permute-start(bf16[1024,512]{1,0:T(8,128)(2,1)S(1)} %get-tuple-element.26), channel_id=1, source_target_pairs={{0,1},{1,0},{8,9},{9,8},{16,17},{17,16},{24,25},{25,24},{2,3},{3,2... | collective-permute-start | bytes 3145736 | tf_op jit(solution)/shard_map/ppermute | solution.py:37
  60.8 12.0 %collective-permute-start.14 = (bf16[256,768]{1,0:T(8,128)(2,1)S(1)}, bf16[256,768]{1,0:T(8,128)(2,1)S(1)}, u32[]{:S(2)}, u32[]{:S(2)}) collective-permute-start(bf16[256,768]{1,0:T(8,128)(2,1)S(1)} %get-tuple-element.30), channel_id=1, source_target_pairs={{0,8},{1,9},{8,16},{9,17},{16,24},{17,25},{24,0},{25,1},{2,10},{3,... | collective-permute-start | bytes 1179656 | tf_op jit(solution)/shard_map/ppermute | solution.py:37
  62.3 19.8 %collective-permute-start.15 = (bf16[256,768]{1,0:T(8,128)(2,1)S(1)}, bf16[256,768]{1,0:T(8,128)(2,1)S(1)}, u32[]{:S(2)}, u32[]{:S(2)}) collective-permute-start(bf16[256,768]{1,0:T(8,128)(2,1)S(1)} %get-tuple-element.31), channel_id=1, source_target_pairs={{0,16},{1,17},{8,24},{9,25},{16,0},{17,1},{24,8},{25,9},{2,18},{3,... | collective-permute-start | bytes 1179656 | tf_op jit(solution)/shard_map/ppermute | solution.py:37
  64.4 17.7 %collective-permute-start.16 = (bf16[256,768]{1,0:T(8,128)(2,1)S(1)}, bf16[256,768]{1,0:T(8,128)(2,1)S(1)}, u32[]{:S(2)}, u32[]{:S(2)}) collective-permute-start(bf16[256,768]{1,0:T(8,128)(2,1)S(1)} %get-tuple-element.32), channel_id=1, source_target_pairs={{0,24},{1,25},{8,0},{9,1},{16,8},{17,9},{24,16},{25,17},{2,26},{3,... | collective-permute-start | bytes 1179656 | tf_op jit(solution)/shard_map/ppermute | solution.py:37
  87.7 11.2 %collective-permute-start.7 = (bf16[256,512]{1,0:T(8,128)(2,1)S(1)}, bf16[256,512]{1,0:T(8,128)(2,1)S(1)}, u32[]{:S(2)}, u32[]{:S(2)}) collective-permute-start(bf16[256,512]{1,0:T(8,128)(2,1)S(1)} %add_convert_fusion.2), channel_id=1, source_target_pairs={{0,2},{128,134},{2,4},{130,128},{4,6},{132,130},{6,0},{134,132},{1... | collective-permute-start | bytes 786440 | tf_op jit(solution)/shard_map/ppermute | solution.py:45
  90.8 12.4 %collective-permute-start.18 = (bf16[256,384]{1,0:T(8,128)(2,1)S(1)}, bf16[256,384]{1,0:T(8,128)(2,1)S(1)}, u32[]{:S(2)}, u32[]{:S(2)}) collective-permute-start(bf16[256,384]{1,0:T(8,128)(2,1)S(1)} %add_convert_fusion.5), channel_id=1, source_target_pairs={{0,2},{128,134},{2,4},{130,128},{4,6},{132,130},{6,0},{134,132},{1... | collective-permute-start | bytes 589832 | tf_op jit(solution)/shard_map/ppermute | solution.py:45
  100.0 8.8 %collective-permute-start.8 = (bf16[256,512]{1,0:T(8,128)(2,1)S(1)}, bf16[256,512]{1,0:T(8,128)(2,1)S(1)}, u32[]{:S(2)}, u32[]{:S(2)}) collective-permute-start(bf16[256,512]{1,0:T(8,128)(2,1)S(1)} %add_convert_fusion.1), channel_id=1, source_target_pairs={{0,2},{128,134},{2,4},{130,128},{4,6},{132,130},{6,0},{134,132},{1... | collective-permute-start | bytes 786440 | tf_op jit(solution)/shard_map/ppermute | solution.py:45
  104.2 8.8 %collective-permute-start.19 = (bf16[256,384]{1,0:T(8,128)(2,1)S(1)}, bf16[256,384]{1,0:T(8,128)(2,1)S(1)}, u32[]{:S(2)}, u32[]{:S(2)}) collective-permute-start(bf16[256,384]{1,0:T(8,128)(2,1)S(1)} %add_convert_fusion.4), channel_id=1, source_target_pairs={{0,2},{128,134},{2,4},{130,128},{4,6},{132,130},{6,0},{134,132},{1... | collective-permute-start | bytes 589832 | tf_op jit(solution)/shard_map/ppermute | solution.py:45
  109.9 20.5 %collective-permute-start.9 = (bf16[256,512]{1,0:T(8,128)(2,1)S(1)}, bf16[256,512]{1,0:T(8,128)(2,1)S(1)}, u32[]{:S(2)}, u32[]{:S(2)}) collective-permute-start(bf16[256,512]{1,0:T(8,128)(2,1)S(1)} %add_convert_fusion), channel_id=1, source_target_pairs={{0,2},{128,134},{2,4},{130,128},{4,6},{132,130},{6,0},{134,132},{1... | collective-permute-start | bytes 786440 | tf_op jit(solution)/shard_map/ppermute | solution.py:45
  114.0 8.7 %collective-permute-start.20 = (bf16[256,384]{1,0:T(8,128)(2,1)S(1)}, bf16[256,384]{1,0:T(8,128)(2,1)S(1)}, u32[]{:S(2)}, u32[]{:S(2)}) collective-permute-start(bf16[256,384]{1,0:T(8,128)(2,1)S(1)} %add_convert_fusion.3), channel_id=1, source_target_pairs={{0,2},{128,134},{2,4},{130,128},{4,6},{132,130},{6,0},{134,132},{1... | collective-permute-start | bytes 589832 | tf_op jit(solution)/shard_map/ppermute | solution.py:45
  123.8 12.4 %collective-permute-start.21 = (bf16[128,384]{1,0:T(8,128)(2,1)S(1)}, bf16[128,384]{1,0:T(8,128)(2,1)S(1)}, u32[]{:S(2)}, u32[]{:S(2)}) collective-permute-start(bf16[128,384]{1,0:T(8,128)(2,1)S(1)} %slice.147), channel_id=1, source_target_pairs={{0,230},{2,228},{4,226},{6,224},{32,198},{34,196},{36,194},{38,192... | collective-permute-start | bytes 294920 | tf_op jit(solution)/shard_map/ppermute | solution.py:56
  131.4 8.4 %collective-permute-start.10 = (bf16[128,512]{1,0:T(8,128)(2,1)S(1)}, bf16[128,512]{1,0:T(8,128)(2,1)S(1)}, u32[]{:S(2)}, u32[]{:S(2)}) collective-permute-start(bf16[128,512]{1,0:T(8,128)(2,1)S(1)} %slice.146), channel_id=1, source_target_pairs={{0,230},{2,228},{4,226},{6,224},{32,198},{34,196},{36,194},{38,192... | collective-permute-start | bytes 393224 | tf_op jit(solution)/shard_map/ppermute | solution.py:56
  136.3 7.3 %collective-permute-start.23 = (bf16[128,384]{1,0:T(8,128)(2,1)S(1)}, bf16[128,384]{1,0:T(8,128)(2,1)S(1)}, u32[]{:S(2)}, u32[]{:S(2)}) collective-permute-start(bf16[128,384]{1,0:T(8,128)(2,1)S(1)} %fusion.17), channel_id=1, source_target_pairs={{0,4},{128,132},{2,6},{130,134},{4,0},{132,128},{6,2},{134,130},{1... | collective-permute-start | bytes 294920 | tf_op jit(solution)/shard_map/ppermute | solution.py:45
  136.4 7.2 %collective-permute-start.24 = (bf16[128,384]{1,0:T(8,128)(2,1)S(1)}, bf16[128,384]{1,0:T(8,128)(2,1)S(1)}, u32[]{:S(2)}, u32[]{:S(2)}) collective-permute-start(bf16[128,384]{1,0:T(8,128)(2,1)S(1)} %fusion.17), channel_id=1, source_target_pairs={{0,6},{128,130},{2,0},{130,132},{4,2},{132,134},{6,4},{134,128},{1... | collective-permute-start | bytes 294920 | tf_op jit(solution)/shard_map/ppermute | solution.py:45
  139.8 7.8 %collective-permute-start.11 = (bf16[128,512]{1,0:T(8,128)(2,1)S(1)}, bf16[128,512]{1,0:T(8,128)(2,1)S(1)}, u32[]{:S(2)}, u32[]{:S(2)}) collective-permute-start(bf16[128,512]{1,0:T(8,128)(2,1)S(1)} %fusion.14), channel_id=1, source_target_pairs={{0,2},{128,134},{2,4},{130,128},{4,6},{132,130},{6,0},{134,132},{1... | collective-permute-start | bytes 393224 | tf_op jit(solution)/shard_map/ppermute | solution.py:45
  139.9 15.9 %collective-permute-start.12 = (bf16[128,512]{1,0:T(8,128)(2,1)S(1)}, bf16[128,512]{1,0:T(8,128)(2,1)S(1)}, u32[]{:S(2)}, u32[]{:S(2)}) collective-permute-start(bf16[128,512]{1,0:T(8,128)(2,1)S(1)} %fusion.14), channel_id=1, source_target_pairs={{0,4},{128,132},{2,6},{130,134},{4,0},{132,128},{6,2},{134,130},{1... | collective-permute-start | bytes 393224 | tf_op jit(solution)/shard_map/ppermute | solution.py:45
  141.9 14.0 %collective-permute-start.13 = (bf16[128,512]{1,0:T(8,128)(2,1)S(1)}, bf16[128,512]{1,0:T(8,128)(2,1)S(1)}, u32[]{:S(2)}, u32[]{:S(2)}) collective-permute-start(bf16[128,512]{1,0:T(8,128)(2,1)S(1)} %fusion.14), channel_id=1, source_target_pairs={{0,6},{128,130},{2,0},{130,132},{4,2},{132,134},{6,4},{134,128},{1... | collective-permute-start | bytes 393224 | tf_op jit(solution)/shard_map/ppermute | solution.py:45
  161.7 7.7 %collective-permute-start.28 = (bf16[2,32,896]{2,1,0:T(8,128)(2,1)S(1)}, bf16[2,32,896]{2,1,0:T(8,128)(2,1)S(1)}, u32[]{:S(2)}, u32[]{:S(2)}) collective-permute-start(bf16[2,32,896]{2,1,0:T(8,128)(2,1)S(1)} %get-tuple-element.44), channel_id=1, source_target_pairs={{0,16},{1,17},{8,24},{9,25},{16,0},{17,1},{24,8},{25,9},{2,18},{3,... | collective-permute-start | bytes 344072 | tf_op jit(solution)/shard_map/ppermute | solution.py:37
  (14 other events, 206.2 us)
where the time goes:
time: 173 us; the launch traced here: 172 us
  waiting for transfers between devices  105 us (61%)
  starting transfers between devices  42.1 us (24%)
  Pallas kernels  10.8 us (6%)
  other arithmetic  8.63 us (5%)
  local copies, waits for them, and re-layouts  4.04 us (2%)
    ppermute x16, waiting for transfers between devices, send_group(): return lax.ppermute(value, ('y', 'c'), pairs)  62.2 us
    ppermute x12, waiting for transfers between devices, send_ring(): return lax.ppermute(value, ('zh', 'z'), pairs)  38.2 us
    ppermute x16, starting transfers between devices, send_group(): return lax.ppermute(value, ('y', 'c'), pairs)  25.1 us
    ppermute x12, starting transfers between devices, send_ring(): return lax.ppermute(value, ('zh', 'z'), pairs)  10.3 us
    ppermute x2, starting transfers between devices, send_mirror(): return lax.ppermute(value, ('zh', 'x', 'z'), pairs)  6.69 us
    pallas_call x2, Pallas kernels, product(): pl.pallas_call(functools.partial(product_kernel, base, cols), out_shape=s...  6.53 us
    convert_element_type x6, other arithmetic, per_device(): moving = total.astype(bf16)  6.1 us
    ppermute x2, waiting for transfers between devices, send_mirror(): return lax.ppermute(value, ('zh', 'x', 'z'), pairs)  4.88 us
  transfers between devices with their start and end apart: 30, of which 20 were waited for; matrix products, arithmetic and copies ran while one was open for 5% of the time, Pallas kernels for 2%

commit v1 on v0

v1 whole, which is shorter than its diff:
```python
import functools
import jax
import jax.numpy as jnp
from jax import lax
from jax.experimental import pallas as pl
from jax.experimental.pallas import tpu as pltpu
from jax.sharding import Mesh, PartitionSpec as P

BLK = 8
NY, NZ, NC = 4, 4, 2
NEAR = (1, NY - 1)
COLS, LATE = 896, 256
EARLY = COLS - LATE
LAG, FORWARD = 1, 1
OFFSETS = tuple((dy, dc) for dy in range(NY) for dc in range(NC))

beta_first = 0.9
beta_second = 0.95
learn_rate = 0.00022
weight_decay = 0.1
adam_eps = 1e-08
bias_first = 1.0 - 0.9**20
bias_second = 1.0 - 0.95**20

bf16 = jnp.bfloat16
f32 = jnp.float32
VMEM = pl.BlockSpec(memory_space=pltpu.VMEM)
SMEM = pl.BlockSpec(memory_space=pltpu.SMEM)
ANY = pl.BlockSpec(memory_space=pl.ANY)
HBM = pl.BlockSpec(memory_space=pltpu.HBM)
PARAMS = pltpu.CompilerParams(vmem_limit_bytes=40 * 1024 * 1024)
SMALL = pltpu.CompilerParams(vmem_limit_bytes=8 * 1024 * 1024)
FULL = pltpu.CompilerParams(vmem_limit_bytes=62 * 1024 * 1024)


def send_group(value, dy, dc):
    if dy == 0 and dc == 0:
        return value
    pairs = []
    for y in range(NY):
        for c in range(NC):
            pairs.append((y * NC + c, (y + dy) % NY * NC + (c ^ dc)))
    return lax.ppermute(value, ("y", "c"), pairs)


def send_ring(value, steps):
    pairs = []
    for z in range(NZ):
        pairs.append((z, (z + steps) % NZ))
        pairs.append((NZ + z, NZ + (z + NZ - steps) % NZ))
    return lax.ppermute(value, ("zh", "z"), pairs)


def send_mirror(value):
    pairs = []
    for zh in range(2):
        for x in range(4):
            for z in range(NZ):
                source = (zh * 4 + x) * NZ + z
                target = ((1 - zh) * 4 + 3 - x) * NZ + NZ - 1 - z
                pairs.append((source, target))
    return lax.ppermute(value, ("zh", "x", "z"), pairs)


def columns_of(y, c, base=0, cols=COLS):
    return pl.ds(pl.multiple_of((y * NC + c) * COLS + base, 128), cols)


def run(copies):
    for copy in copies:
        copy.start()
    for copy in copies:
        copy.wait()


def prepare_kernel(live_hbm, hidden_hbm, grad_hbm, own_hbm, up_hbm, down_hbm, swap_hbm, late_hbm, *rest):
    live_ref, hidden_ref, turned_ref, near_ref, late_ref, in_sem, out_sem = rest
    zh, x = lax.axis_index("zh"), lax.axis_index("x")
    y, z, c = lax.axis_index("y"), lax.axis_index("z"), lax.axis_index("c")
    rows, width = hidden_ref.shape
    pairs = [(hidden_hbm, hidden_ref), (live_hbm, live_ref)]
    for i, dy in enumerate(NEAR):
        for other in range(NC):
            source = columns_of(lax.rem(y + dy, NY), lax.rem(c + other, NC), 0, EARLY)
            pairs.append((grad_hbm.at[:, source], near_ref.at[i, :, other * EARLY:(other + 1) * EARLY]))
    for other in range(NC):
        for there in range(NY):
            source = columns_of(there, lax.rem(c + other, NC), EARLY, LATE)
            pairs.append((grad_hbm.at[:, source], late_ref.at[other, :, there * LATE:(there + 1) * LATE]))
    loads = [pltpu.make_async_copy(a, b, in_sem.at[i]) for i, (a, b) in enumerate(pairs)]
    for copy in loads:
        copy.start()
    loads[0].wait()
    loads[1].wait()
    live = live_ref[zh * 4 + x, (y * NZ + z) * NC + c]
    rank = jnp.where(zh == 0, z, NZ - 1 - z)
    keep = lax.broadcasted_iota(jnp.int32, (128, rows), 1) < live
    for own in range(2):
        half = zh if own else 1 - zh
        for step in range(NZ):
            part = lax.rem(rank + 2 * NZ - 1 - step, NZ)
            block = (half * NZ + part) * 128
            cols = hidden_ref[:, pl.ds(pl.multiple_of(block, 128), 128)]
            turned = jnp.where(keep, cols.astype(f32).T, 0.0).astype(bf16)
            at = own * NZ + step
            down, across = slice(at % 2 * 128, (at % 2 + 1) * 128), at // 2 * rows
            turned_ref[down, across:across + rows] = turned
    for copy in loads[2:]:
        copy.wait()
    pairs = [(turned_ref, own_hbm), (late_ref.at[0], late_hbm)]
    for out, grad in ((swap_hbm, late_ref.at[1]), (up_hbm, near_ref.at[0]), (down_hbm, near_ref.at[1])):
        pairs += [(turned_ref, out.at[:, :width]), (grad, out.at[:, width:])]
    run([pltpu.make_async_copy(a, b, out_sem.at[i]) for i, (a, b) in enumerate(pairs)])


def prepare(live_tokens, hidden, grad):
    rows, width = hidden.shape
    early, late = NC * EARLY, NY * LATE
    widths = [width, width + early, width + early, width + late, late]
    return pl.pallas_call(
        prepare_kernel,
        out_shape=[jax.ShapeDtypeStruct((rows, cols), bf16) for cols in widths],
        in_specs=[HBM] * 3,
        out_specs=[HBM] * 5,
        scratch_shapes=[
            pltpu.SMEM(live_tokens.shape, live_tokens.dtype),
            pltpu.VMEM(hidden.shape, bf16),
            pltpu.VMEM(hidden.shape, bf16),
            pltpu.VMEM((2, rows, early), bf16),
            pltpu.VMEM((NC, rows, late), bf16),
            pltpu.SemaphoreType.DMA((2 + 2 * NC + NC * NY,)),
            pltpu.SemaphoreType.DMA((8,)),
        ],
        compiler_params=FULL,
        name="prepare",
    )(live_tokens, hidden, grad)


def pack_kernel(grad_hbm, after_ref, far_hbm, own_hbm, buffer, in_sem, out_sem):
    y, c = lax.axis_index("y"), lax.axis_index("c")
    pairs = []
    for i, dy in enumerate((2, 0)):
        for other in range(NC):
            source = columns_of(lax.rem(y + dy, NY), lax.rem(c + other, NC), 0, EARLY)
            pairs.append((grad_hbm.at[:, source], buffer.at[i, :, other * EARLY:(other + 1) * EARLY]))
    run([pltpu.make_async_copy(a, b, in_sem.at[i]) for i, (a, b) in enumerate(pairs)])
    pairs = [(buffer.at[0], far_hbm), (buffer.at[1], own_hbm)]
    run([pltpu.make_async_copy(a, b, out_sem.at[i]) for i, (a, b) in enumerate(pairs)])


def pack(grad, after):
    shape = (grad.shape[0], NC * EARLY)
    return pl.pallas_call(
        pack_kernel,
        out_shape=[jax.ShapeDtypeStruct(shape, bf16)] * 2,
        in_specs=[HBM] * 2,
        out_specs=[HBM] * 2,
        scratch_shapes=[
            pltpu.VMEM((2,) + shape, bf16),
            pltpu.SemaphoreType.DMA((2 * NC,)),
            pltpu.SemaphoreType.DMA((2,)),
        ],
        compiler_params=FULL,
        name="pack",
    )(grad, after)


def forward_kernel(up_ref, down_ref, after_ref, far_up_ref, far_down_ref, sem):
    half = far_up_ref.shape[1]
    pairs = [(up_ref.at[:, :half], far_up_ref), (down_ref.at[:, half:2 * half], far_down_ref)]
    run([pltpu.make_async_copy(a, b, sem.at[i]) for i, (a, b) in enumerate(pairs)])


def forward(up, down, half, after):
    return pl.pallas_call(
        forward_kernel,
        out_shape=[jax.ShapeDtypeStruct((up.shape[0], half), bf16)] * 2,
        in_specs=[ANY] * 3,
        out_specs=[VMEM] * 2,
        scratch_shapes=[pltpu.SemaphoreType.DMA((2,))],
        compiler_params=SMALL,
        name="forward",
    )(up, down, after)


def chip_product_kernel(own_ref, late_ref, swap_ref, *rest):
    outs, (left, right, sem) = rest[:NZ], rest[NZ:]
    rows, width = own_ref.shape
    pairs = [
        (own_ref, left.at[0]),
        (swap_ref.at[:, :width], left.at[1]),
        (late_ref, right.at[:rows, :]),
        (swap_ref.at[:, width:], right.at[rows:, :]),
    ]
    run([pltpu.make_async_copy(a, b, sem.at[i]) for i, (a, b) in enumerate(pairs)])
    for block in range(NZ):
        at = slice(block * rows, (block + 1) * rows)
        both = jnp.concatenate([left[0, :, at], left[1, :, at]], 1)
        total = jnp.dot(both, right[...], preferred_element_type=f32).astype(bf16)
        half, step = block // 2, block % 2 * 2
        for i in range(2):
            outs[step + i][half * 128:(half + 1) * 128, :] = total[i * 128:(i + 1) * 128]


def chip_product(own, late, swap):
    rows, width = own.shape
    cols = late.shape[1]
    return pl.pallas_call(
        chip_product_kernel,
        out_shape=[jax.ShapeDtypeStruct((256, cols), bf16)] * NZ,
        in_specs=[ANY] * 3,
        out_specs=[VMEM] * NZ,
        scratch_shapes=[
            pltpu.VMEM((NC, rows, width), bf16),
            pltpu.VMEM((NC * rows, cols), bf16),
            pltpu.SemaphoreType.DMA((4,)),
        ],
        compiler_params=PARAMS,
        name="chip_product",
    )(own, late, swap)


def split_kernel(part_ref, moved_ref, *outs):
    y = lax.axis_index("y")
    for dy, out_ref in enumerate(outs):
        at = pl.ds(pl.multiple_of(lax.rem(y + dy, NY) * LATE, 128), LATE)
        total = part_ref[:, at].astype(f32) + moved_ref[:, at].astype(f32)
        out_ref[...] = total.astype(bf16)


def split(part, moved):
    return pl.pallas_call(
        split_kernel,
        out_shape=[jax.ShapeDtypeStruct((part.shape[0], LATE), bf16)] * NY,
        in_specs=[VMEM] * 2,
        out_specs=[VMEM] * NY,
        compiler_params=SMALL,
        name="split",
    )(part, moved)


def product_kernel(part, n_after, *refs):
    hidden, grads = refs[:NY + 1], refs[NY + 1:2 * NY + 1]
    refs = refs[2 * NY + 1 + n_after:]
    outs, other_ref, (left, right, sem) = refs[:NZ], refs[NZ], refs[NZ + 1:]
    depth, width = hidden[0].shape
    rows, lead = outs[0].shape[0], part * width // 2
    pairs = []
    for dy in range(NY):
        if dy == 2:
            piece = hidden[NY] if part else hidden[2]
        else:
            piece = hidden[dy].at[:, lead:lead + width // 2]
        pairs.append((piece, left.at[dy]))
        first = grads[dy].shape[1] - NC * EARLY
        pairs.append((grads[dy].at[:, first:], right.at[dy * depth:(dy + 1) * depth, :]))
    run([pltpu.make_async_copy(a, b, sem.at[i]) for i, (a, b) in enumerate(pairs)])
    for pair in range(NZ // 2):
        at = slice(pair * depth, (pair + 1) * depth)
        block = jnp.concatenate([left[i, :, at] for i in range(NY)], 1)
        total = jnp.dot(block, right[...], preferred_element_type=f32)
        for i in range(2):
            outs[pair * 2 + i][...] = total[i * rows:(i + 1) * rows, :EARLY].astype(bf16)
        other_ref[pair * 2 * rows:(pair + 1) * 2 * rows, :] = total[:, EARLY:].astype(bf16)


def product(part, hidden, grads, after):
    tokens, width = hidden[0].shape
    depth, rows = NY * tokens, width // 2 // NZ
    shapes = [jax.ShapeDtypeStruct((rows, EARLY), bf16)] * NZ
    shapes.append(jax.ShapeDtypeStruct((rows * NZ, EARLY), bf16))
    return pl.pallas_call(
        functools.partial(product_kernel, part, len(after)),
        out_shape=shapes,
        in_specs=[ANY] * (2 * NY + 1 + len(after)),
        out_specs=[VMEM] * len(shapes),
        scratch_shapes=[
            pltpu.VMEM((NY, tokens, width // 2), bf16),
            pltpu.VMEM((depth, NC * EARLY), bf16),
            pltpu.SemaphoreType.DMA((2 * NY,)),
        ],
        compiler_params=PARAMS,
        cost_estimate=pl.CostEstimate(
            flops=width * NC * EARLY * depth,
            bytes_accessed=width * (depth + NC * EARLY) + 2 * depth * NC * EARLY,
            transcendentals=0,
        ),
        name="product",
    )(*hidden, *grads, *after)


def add_kernel(terms, pieces, *refs):
    out_ref, rows = refs[-1], refs[-1].shape[0]
    total = None
    for ref, at in zip(refs, terms):
        term = ref[at:at + rows, :].astype(f32)
        total = term if total is None else total + term
    out_ref[:, :total.shape[1]] = total.astype(out_ref.dtype)
    if pieces is not None:
        total = None
        for ref in refs[len(terms):len(terms) + NY]:
            term = ref[pieces:pieces + rows, :].astype(f32)
            total = term if total is None else total + term
        out_ref[:, out_ref.shape[1] - total.shape[1]:] = total.astype(out_ref.dtype)


def add(terms, dtype, after=(), late=(), at=None, rows=128):
    cols = terms[0][0].shape[1] + (late[0].shape[1] if late else 0)
    return pl.pallas_call(
        functools.partial(add_kernel, tuple(first for _, first in terms), at),
        out_shape=jax.ShapeDtypeStruct((rows, cols), dtype),
        in_specs=[VMEM] * (len(terms) + len(late)) + [ANY] * len(after),
        out_specs=VMEM,
        compiler_params=SMALL,
        name="add",
    )(*[value for value, _ in terms], *late, *after)


def adamw_kernel(*refs):
    counts_ref, owned_refs = refs[0], refs[1:1 + NY]
    master_ref, first_ref, second_ref, new_master_ref, new_first_ref, new_second_ref = refs[1 + NY:]
    zh, x = lax.axis_index("zh"), lax.axis_index("x")
    y, z, c = lax.axis_index("y"), lax.axis_index("z"), lax.axis_index("c")
    held = counts_ref[zh * 4 + x, (y * NZ + z) * NC + c]
    slots, cols = master_ref.shape[0], COLS
    valid = lax.broadcasted_iota(jnp.int32, (slots, cols), 0) < held * BLK
    for dy in range(NY):
        for other in range(NC):
            at = columns_of(lax.rem(y + NY - dy, NY), lax.rem(c + other, NC))
            owned = owned_refs[dy][other].astype(f32)
            param = master_ref[:, at]
            first = beta_first * first_ref[:, at].astype(f32) + (1.0 - beta_first) * owned
            second = beta_second * second_ref[:, at].astype(f32) + (1.0 - beta_second) * owned * owned
            direction = first / bias_first / (jnp.sqrt(second / bias_second) + adam_eps)
            updated = param - learn_rate * (direction + weight_decay * param)
            new_master_ref[:, at] = jnp.where(valid, updated, 0.0)
            new_first_ref[:, at] = jnp.where(valid, first, 0.0).astype(bf16)
            new_second_ref[:, at] = jnp.where(valid, second, 0.0).astype(bf16)


def adamw(block_count, owned, master, moment1, moment2):
    shapes = [jax.ShapeDtypeStruct(a.shape, a.dtype) for a in (master, moment1, moment2)]
    return pl.pallas_call(
        adamw_kernel,
        out_shape=shapes,
        in_specs=[SMEM] + [VMEM] * (len(owned) + 3),
        out_specs=[VMEM] * 3,
        compiler_params=PARAMS,
        name="adamw",
    )(block_count, *owned, master, moment1, moment2)


def slot_choice(block_count, hblk, cap):
    y, z, c = lax.axis_index("y"), lax.axis_index("z"), lax.axis_index("c")
    counts = block_count[lax.axis_index("zh") * 4 + lax.axis_index("x")]
    owners = []
    for dy, dc in OFFSETS:
        owners.append(((y + dy) % NY * NZ + z) * NC + (c ^ dc))
    owners = jnp.stack(owners)
    before = jnp.arange(counts.shape[0], dtype=jnp.int32)[None, :] < owners[:, None]
    starts = jnp.sum(jnp.where(before, counts[None, :], 0), axis=1)
    slot = jnp.arange(cap, dtype=jnp.int32)
    block = jnp.minimum(starts[:, None] + slot[None, :], hblk - 1)
    per = hblk // NZ
    chunk = block // per
    chunk = jnp.where(lax.axis_index("zh") == 0, chunk, NZ - 1 - chunk)
    place = chunk * per + block % per
    rows = place[:, :, None] * BLK + jnp.arange(BLK, dtype=jnp.int32)
    rows = rows.reshape(-1)
    return (rows[:, None] == jnp.arange(hblk * BLK, dtype=jnp.int32)[None, :]).astype(bf16)


def per_device(hidden_act, grad_out, live_tokens, block_count, master, moment1, moment2):
    half = hidden_act.shape[1] // 2
    slots = master.shape[1]
    own, up, down, swap, late = prepare(live_tokens, hidden_act, grad_out)
    choice = slot_choice(block_count, half // BLK, slots // BLK)
    near = [send_group(up, 1, 0), send_group(down, 3, 0)]
    opposite, mine = pack(grad_out, own)
    grads = [mine, near[0], send_group(opposite, 2, 0), near[1]]

    parts = chip_product(own, late, send_group(swap, 0, 1))
    moving, steps = parts[0], []
    for step in range(1, NZ - 1):
        moving = add([(parts[step], 0), (send_ring(moving, 1), 0)], bf16, rows=256)
        steps.append(moving)
    pieces = split(parts[NZ - 1], send_ring(moving, 1))
    late = [send_group(piece, dy, 0) for dy, piece in enumerate(pieces)]

    far = forward(near[0], near[1], half, steps[FORWARD])
    far = [send_group(far[0], 1, 0), send_group(far[1], 3, 0)]
    hidden = [own, near[0], far[0], near[1], far[1]]
    sums, after = [], [pieces[0]]
    for part in range(2):
        parts = product(part, hidden, grads, [] if part else after)
        sibling = send_group(parts[NZ], 0, 1)
        moved = []
        for step in range(NZ):
            terms = [(parts[step], 0), (sibling, step * 128)] + moved
            if step < NZ - 1:
                total = add(terms, bf16, after if part and not step else ())
                moved = [(send_ring(total, 1), 0)]
            else:
                total = add(terms, f32 if part else bf16, (), late, part * 128)
            if step == LAG:
                after = [total]
        sums.append(total)
    tile = (sums[1] + send_mirror(sums[0]).astype(f32)).astype(bf16)
    gathered = lax.all_gather(tile, "z", axis=0, tiled=True)
    picked = jnp.dot(choice, gathered, preferred_element_type=f32).astype(bf16)
    picked = picked.reshape(NY, NC, slots, COLS)
    both = jnp.stack([picked[:, 0], send_group(picked[:, 1], 0, 1)], 1)
    owned = [send_group(both[dy], dy, 0) for dy in range(NY)]
    outs = adamw(block_count, owned, master[0], moment1[0], moment2[0])
    return tuple(out[None] for out in outs)


def solution(mesh):
    fine = Mesh(mesh.devices.reshape(2, 4, NY, NZ, NC), ("zh", "x", "y", "z", "c"))
    pipe, edp = ("zh", "x"), ("y", "z", "c")
    shard = P(pipe, edp, None)
    tokens = P(pipe + edp, None)
    return jax.shard_map(
        per_device,
        mesh=fine,
        in_specs=(tokens, tokens, P(), P(), shard, shard, shard),
        out_specs=(shard, shard, shard),
        check_vma=False,
    )
```

time: 173 us -> 150 us (0.87)
  waiting for transfers between devices: 105 us -> 62.5 us
  blocking collectives: 0 us -> 15.6 us
  Pallas kernels: 10.8 us -> 22.7 us
  other arithmetic: 8.63 us -> 0.45 us
    ppermute x16 -> x15, waiting for transfers between devices: 62.2 us -> 9.21 us  [send_group(): return lax.ppermute(value, ('y', 'c'), pairs)]
    all_gather x0 -> x1, blocking collectives: none -> 15.6 us  [per_device(): gathered = lax.all_gather(tile, 'z', axis=0, tiled=True)]
    ppermute x12 -> x9, waiting for transfers between devices: 38.2 us -> 53.3 us  [send_ring(): return lax.ppermute(value, ('zh', 'z'), pairs)]
    pallas_call x5 -> x17, Pallas kernels: 7.8 us -> 19.7 us  [the longest x2 7.39 us: product(): pl.pallas_call(functools.partial(product_kernel, part, len(after)), out_s...]
    ppermute x16 -> x15, starting transfers between devices: 25.1 us -> 36.7 us  [send_group(): return lax.ppermute(value, ('y', 'c'), pairs)]
    ppermute x12 -> x9, starting transfers between devices: 10.3 us -> 2.44 us  [send_ring(): return lax.ppermute(value, ('zh', 'z'), pairs)]
    convert_element_type x8 -> x1, other arithmetic: 6.15 us -> 0.05 us  [per_device(): tile = (sums[1] + send_mirror(sums[0]).astype(f32)).astype(bf16)]
    ppermute x2 -> x1, waiting for transfers between devices: 4.88 us -> 0.01 us  [send_mirror(): return lax.ppermute(value, ('zh', 'x', 'z'), pairs)]
  transfers between devices with their start and end apart: 30 -> 25, of which waited for: 20 -> 13; matrix products, arithmetic and copies ran while one was open for 5% -> 0% of each run, Pallas kernels for 2% -> 7%
where the time goes in v1:
time: 150 us; the launch traced here: 149 us
  waiting for transfers between devices  62.5 us (42%)
  starting transfers between devices  43.7 us (29%)
  Pallas kernels  22.7 us (15%)
  blocking collectives  15.6 us (10%)
  local copies, waits for them, and re-layouts  3.03 us (2%)
    ppermute x9, waiting for transfers between devices, send_ring(): return lax.ppermute(value, ('zh', 'z'), pairs)  53.3 us
    ppermute x15, starting transfers between devices, send_group(): return lax.ppermute(value, ('y', 'c'), pairs)  36.7 us
    all_gather x1, blocking collectives, per_device(): gathered = lax.all_gather(tile, 'z', axis=0, tiled=True)  15.6 us
    ppermute x15, waiting for transfers between devices, send_group(): return lax.ppermute(value, ('y', 'c'), pairs)  9.21 us
    pallas_call x2, Pallas kernels, product(): pl.pallas_call(functools.partial(product_kernel, part, len(after)), out_s...  7.39 us
    ppermute x1, starting transfers between devices, send_mirror(): return lax.ppermute(value, ('zh', 'x', 'z'), pairs)  4.6 us
    pallas_call x1, Pallas kernels, prepare(): pl.pallas_call(prepare_kernel, out_shape=[jax.ShapeDtypeStruct((rows, col...  4.06 us
  transfers between devices with their start and end apart: 25, of which 13 were waited for; matrix products, arithmetic and copies ran while one was open for 0% of the time, Pallas kernels for 7%

profile of v1, /device:TPU:1, one launch (start us, length us, event | category | flops | bytes accessed | tf_op | source)
XLA Modules:
  0.0 149.5 jit_solution(3023276509538361428)
XLA Ops:
  0.6 4.1 %prepare.1 = (bf16[256,1024]{1,0:T(8,128)(2,1)}, bf16[256,2304]{1,0:T(8,128)(2,1)}, bf16[256,2304]{1,0:T(8,128)(2,1)}, bf16[256,2048]{1,0:T(8,128)(2,1)}, bf16[256,1024]{1,0:T(8,128)(2,1)}) custom-call(s32[8,32]{1,0:T(8,128)} %live_hbm.1, bf16[256,1024]{1,0:T(8,128)(2,1)} %hidden_hbm.1, bf16[256,7168]{1,0:T(8,128)(2,1)} %grad_hbm.3), custom_call_target="tpu_custom_call" | custom-call | tf_op jit(solution)/shard_map/prepare/pallas_call | solution.py:120
  4.7 3.3 %collective-permute-start.2 = (bf16[256,2048]{1,0:T(8,128)(2,1)}, bf16[256,2048]{1,0:T(8,128)(2,1)S(1)}, u32[]{:S(2)}, u32[]{:S(2)}) collective-permute-start(bf16[256,2048]{1,0:T(8,128)(2,1)} %get-tuple-element.37), channel_id=1, source_target_pairs={{0,1},{1,0},{8,9},{9,8},{16,17},{17,16},{24,25},{25,24},{2,3},{3,2... | collective-permute-start | bytes 3145736 | tf_op jit(solution)/shard_map/ppermute | solution.py:43
  8.0 2.5 %collective-permute-done.2.swap_ref = bf16[256,2048]{1,0:T(8,128)(2,1)S(1)} collective-permute-done((bf16[256,2048]{1,0:T(8,128)(2,1)}, bf16[256,2048]{1,0:T(8,128)(2,1)S(1)}, u32[]{:S(2)}, u32[]{:S(2)}) %collective-permute-start.2) | collective-permute-done | bytes 1048608 | tf_op jit(solution)/shard_map/ppermute | solution.py:43
  15.4 1.6 %collective-permute-start.1 = (bf16[256,2304]{1,0:T(8,128)(2,1)}, bf16[256,2304]{1,0:T(8,128)(2,1)}, u32[]{:S(2)}, u32[]{:S(2)}) collective-permute-start(bf16[256,2304]{1,0:T(8,128)(2,1)} %get-tuple-element.35), channel_id=1, source_target_pairs={{0,24},{1,25},{8,0},{9,1},{16,8},{17,9},{24,16},{25,17},{2,26},{3,... | collective-permute-start | bytes 3538952 | tf_op jit(solution)/shard_map/ppermute | solution.py:43
  16.9 12.2 %collective-permute-done.3.refs_1_ = bf16[256,1024]{1,0:T(8,128)(2,1)S(1)} collective-permute-done((bf16[256,1024]{1,0:T(8,128)(2,1)S(1)}, bf16[256,1024]{1,0:T(8,128)(2,1)S(1)}, u32[]{:S(2)}, u32[]{:S(2)}) %collective-permute-start.3) | collective-permute-done | bytes 524320 | tf_op jit(solution)/shard_map/ppermute | solution.py:51
  30.0 2.4 %pack.1 = (bf16[256,1280]{1,0:T(8,128)(2,1)}, bf16[256,1280]{1,0:T(8,128)(2,1)}) custom-call(bf16[256,7168]{1,0:T(8,128)(2,1)} %grad_hbm.3, bf16[256,1024]{1,0:T(8,128)(2,1)} %get-tuple-element.33.own_ref.after_ref.refs_0_), custom_call_target="tpu_custom_call" | custom-call | tf_op jit(solution)/shard_map/pack/pallas_call | solution.py:153
  32.4 2.7 %collective-permute-start.7 = (bf16[256,1280]{1,0:T(8,128)(2,1)}, bf16[256,1280]{1,0:T(8,128)(2,1)S(1)}, u32[]{:S(2)}, u32[]{:S(2)}) collective-permute-start(bf16[256,1280]{1,0:T(8,128)(2,1)} %get-tuple-element.44), channel_id=1, source_target_pairs={{0,16},{1,17},{8,24},{9,25},{16,0},{17,1},{24,8},{25,9},{2,18},{3,... | collective-permute-start | bytes 1966088 | tf_op jit(solution)/shard_map/ppermute | solution.py:43
  35.1 9.3 %collective-permute-done.4.refs_1_ = bf16[256,1024]{1,0:T(8,128)(2,1)} collective-permute-done((bf16[256,1024]{1,0:T(8,128)(2,1)}, bf16[256,1024]{1,0:T(8,128)(2,1)}, u32[]{:S(2)}, u32[]{:S(2)}) %collective-permute-start.4) | collective-permute-done | bytes 524320 | tf_op jit(solution)/shard_map/ppermute | solution.py:51
  48.1 1.5 %collective-permute-start.6 = (bf16[256,512]{1,0:T(8,128)(2,1)S(1)}, bf16[256,512]{1,0:T(8,128)(2,1)S(1)}, u32[]{:S(2)}, u32[]{:S(2)}) collective-permute-start(bf16[256,512]{1,0:T(8,128)(2,1)S(1)} %get-tuple-element.42), channel_id=1, source_target_pairs={{0,24},{1,25},{8,0},{9,1},{16,8},{17,9},{24,16},{25,17},{2,26},{3,... | collective-permute-start | bytes 786440 | tf_op jit(solution)/shard_map/ppermute | solution.py:43
  49.7 9.0 %collective-permute-done.9.moved_ref = bf16[256,1024]{1,0:T(8,128)(2,1)S(1)} collective-permute-done((bf16[256,1024]{1,0:T(8,128)(2,1)S(1)}, bf16[256,1024]{1,0:T(8,128)(2,1)S(1)}, u32[]{:S(2)}, u32[]{:S(2)}) %collective-permute-start.9) | collective-permute-done | bytes 524320 | tf_op jit(solution)/shard_map/ppermute | solution.py:51
  61.4 3.3 %product.3 = (bf16[128,640]{1,0:T(8,128)(2,1)S(1)}, bf16[128,640]{1,0:T(8,128)(2,1)S(1)}, bf16[128,640]{1,0:T(8,128)(2,1)S(1)}, bf16[128,640]{1,0:T(8,128)(2,1)S(1)}, bf16[512,640]{1,0:T(8,128)(2,1)S(1)}) custom-call(bf16[256,1024]{1,0:T(8,128)(2,1)S(1)} %copy-done.1, bf16[256,2304]{1,0:T(8,128)(2,1)S(1)} %collective-permute-done.up_ref.refs_1_.refs_6_, ...), custom_call_target="tpu_custom_call" | custom-call | flops 1342177280 | bytes 4980736 | tf_op jit(solution)/shard_map/product/pallas_call | solution.py:272
  64.7 4.7 %collective-permute-start.10 = (bf16[512,640]{1,0:T(8,128)(2,1)S(1)}, bf16[512,640]{1,0:T(8,128)(2,1)S(1)}, u32[]{:S(2)}, u32[]{:S(2)}) collective-permute-start(bf16[512,640]{1,0:T(8,128)(2,1)S(1)} %get-tuple-element.53), channel_id=1, source_target_pairs={{0,1},{1,0},{8,9},{9,8},{16,17},{17,16},{24,25},{25,24},{2,3},{3,2... | collective-permute-start | bytes 1966088 | tf_op jit(solution)/shard_map/ppermute | solution.py:43
  69.4 4.1 %product.2 = (bf16[128,640]{1,0:T(8,128)(2,1)S(1)}, bf16[128,640]{1,0:T(8,128)(2,1)S(1)}, bf16[128,640]{1,0:T(8,128)(2,1)S(1)}, bf16[128,640]{1,0:T(8,128)(2,1)S(1)}, bf16[512,640]{1,0:T(8,128)(2,1)}) custom-call(bf16[256,1024]{1,0:T(8,128)(2,1)S(1)} %copy-done.1, bf16[256,2304]{1,0:T(8,128)(2,1)S(1)} %collective-permute-done.up_ref.refs_1_.refs_6_, ...), custom_call_target="tpu_custom_call" | custom-call | flops 1342177280 | bytes 4980736 | tf_op jit(solution)/shard_map/product/pallas_call | solution.py:272
  75.1 7.4 %collective-permute-done.11.refs_2_ = bf16[128,640]{1,0:T(8,128)(2,1)S(1)} collective-permute-done((bf16[128,640]{1,0:T(8,128)(2,1)S(1)}, bf16[128,640]{1,0:T(8,128)(2,1)S(1)}, u32[]{:S(2)}, u32[]{:S(2)}) %collective-permute-start.11) | collective-permute-done | bytes 163872 | tf_op jit(solution)/shard_map/ppermute | solution.py:51
  83.9 3.1 %collective-permute-start.16 = (bf16[256,256]{1,0:T(8,128)(2,1)}, bf16[256,256]{1,0:T(8,128)(2,1)S(1)}, u32[]{:S(2)}, u32[]{:S(2)}) collective-permute-start(bf16[256,256]{1,0:T(8,128)(2,1)} %get-tuple-element.56), channel_id=1, source_target_pairs={{0,16},{1,17},{8,24},{9,25},{16,0},{17,1},{24,8},{25,9},{2,18},{3,... | collective-permute-start | bytes 393224 | tf_op jit(solution)/shard_map/ppermute | solution.py:43
  90.2 3.9 %collective-permute-done.12.refs_2_ = bf16[128,640]{1,0:T(8,128)(2,1)S(1)} collective-permute-done((bf16[128,640]{1,0:T(8,128)(2,1)S(1)}, bf16[128,640]{1,0:T(8,128)(2,1)S(1)}, u32[]{:S(2)}, u32[]{:S(2)}) %collective-permute-start.12) | collective-permute-done | bytes 163872 | tf_op jit(solution)/shard_map/ppermute | solution.py:51
  94.3 3.0 %collective-permute-done.19.refs_2_ = bf16[128,640]{1,0:T(8,128)(2,1)S(1)} collective-permute-done((bf16[128,640]{1,0:T(8,128)(2,1)S(1)}, bf16[128,640]{1,0:T(8,128)(2,1)S(1)}, u32[]{:S(2)}, u32[]{:S(2)}) %collective-permute-start.19) | collective-permute-done | bytes 163872 | tf_op jit(solution)/shard_map/ppermute | solution.py:51
  97.4 4.6 %collective-permute-start.20 = (bf16[128,896]{1,0:T(8,128)(2,1)S(1)}, bf16[128,896]{1,0:T(8,128)(2,1)S(1)}, u32[]{:S(2)}, u32[]{:S(2)}) collective-permute-start(bf16[128,896]{1,0:T(8,128)(2,1)S(1)} %add.248), channel_id=1, source_target_pairs={{0,230},{2,228},{4,226},{6,224},{32,198},{34,196},{36,194},{38,192... | collective-permute-start | bytes 688136 | tf_op jit(solution)/shard_map/ppermute | solution.py:62
  102.5 7.5 %collective-permute-done.14.refs_2_ = bf16[128,640]{1,0:T(8,128)(2,1)S(1)} collective-permute-done((bf16[128,640]{1,0:T(8,128)(2,1)S(1)}, bf16[128,640]{1,0:T(8,128)(2,1)S(1)}, u32[]{:S(2)}, u32[]{:S(2)}) %collective-permute-start.14) | collective-permute-done | bytes 163872 | tf_op jit(solution)/shard_map/ppermute | solution.py:51
  110.1 15.6 %all_gather.3 = bf16[512,896]{1,0:T(8,128)(2,1)S(1)} all-gather(bf16[128,896]{1,0:T(8,128)(2,1)S(1)} %add_convert_fusion), channel_id=1, replica_groups=mesh['zh'=2,'x'=4,'y'=4,'z'=4,'c'=2] {'z'}, dimensions={0}, use_global_device_ids=true | all-gather | bytes 1146880 | tf_op jit(solution)/shard_map/all_gather | solution.py:409
  126.3 7.8 %collective-permute-start.21 = (bf16[4,32,896]{2,1,0:T(8,128)(2,1)S(1)}, bf16[4,32,896]{2,1,0:T(8,128)(2,1)S(1)}, u32[]{:S(2)}, u32[]{:S(2)}) collective-permute-start(bf16[4,32,896]{2,1,0:T(8,128)(2,1)S(1)} %get-tuple-element.67), channel_id=1, source_target_pairs={{0,1},{1,0},{8,9},{9,8},{16,17},{17,16},{24,25},{25,24},{2,3},{3,2... | collective-permute-start | bytes 688136 | tf_op jit(solution)/shard_map/ppermute | solution.py:43
  135.4 5.7 %collective-permute-start.23 = (bf16[2,32,896]{2,1,0:T(8,128)(2,1)S(1)}, bf16[2,32,896]{2,1,0:T(8,128)(2,1)S(1)}, u32[]{:S(2)}, u32[]{:S(2)}) collective-permute-start(bf16[2,32,896]{2,1,0:T(8,128)(2,1)S(1)} %get-tuple-element.66), channel_id=1, source_target_pairs={{0,16},{1,17},{8,24},{9,25},{16,0},{17,1},{24,8},{25,9},{2,18},{3,... | collective-permute-start | bytes 344072 | tf_op jit(solution)/shard_map/ppermute | solution.py:43
  143.2 3.3 %collective-permute-done.23.refs_3_ = bf16[2,32,896]{2,1,0:T(8,128)(2,1)S(1)} collective-permute-done((bf16[2,32,896]{2,1,0:T(8,128)(2,1)S(1)}, bf16[2,32,896]{2,1,0:T(8,128)(2,1)S(1)}, u32[]{:S(2)}, u32[]{:S(2)}) %collective-permute-start.23) | collective-permute-done | bytes 114720 | tf_op jit(solution)/shard_map/ppermute | solution.py:43
  146.5 3.0 %adamw.1 = (f32[32,7168]{1,0:T(8,128)}, bf16[32,7168]{1,0:T(8,128)(2,1)}, bf16[32,7168]{1,0:T(8,128)(2,1)}) custom-call(s32[8,32]{1,0:T(8,128)S(1)} %copy-done.11, bf16[2,32,896]{2,1,0:T(8,128)(2,1)S(1)} %get-tuple-element.64.refs_1_, bf16[2,32,896]{2,1,0:T(8,128)(2,1)S(1)} %collective-permute-done.22.refs_2_, ...), custom_call_target="tpu_custom_call" | custom-call | tf_op jit(solution)/shard_map/adamw/pallas_call | solution.py:343
  (83 shorter events, 22.9 us)
Async XLA Ops:
  4.7 5.8 %collective-permute-start.2 = (bf16[256,2048]{1,0:T(8,128)(2,1)}, bf16[256,2048]{1,0:T(8,128)(2,1)S(1)}, u32[]{:S(2)}, u32[]{:S(2)}) collective-permute-start(bf16[256,2048]{1,0:T(8,128)(2,1)} %get-tuple-element.37), channel_id=1, source_target_pairs={{0,1},{1,0},{8,9},{9,8},{16,17},{17,16},{24,25},{25,24},{2,3},{3,2... | collective-permute-start | bytes 3145736 | tf_op jit(solution)/shard_map/ppermute | solution.py:43
  14.1 15.0 %collective-permute-start.3 = (bf16[256,1024]{1,0:T(8,128)(2,1)S(1)}, bf16[256,1024]{1,0:T(8,128)(2,1)S(1)}, u32[]{:S(2)}, u32[]{:S(2)}) collective-permute-start(bf16[256,1024]{1,0:T(8,128)(2,1)S(1)} %get-tuple-element.40), channel_id=1, source_target_pairs={{0,2},{128,134},{2,4},{130,128},{4,6},{132,130},{6,0},{134,132},{1... | collective-permute-start | bytes 1572872 | tf_op jit(solution)/shard_map/ppermute | solution.py:51
  14.2 31.4 %collective-permute-start = (bf16[256,2304]{1,0:T(8,128)(2,1)}, bf16[256,2304]{1,0:T(8,128)(2,1)S(1)}, u32[]{:S(2)}, u32[]{:S(2)}) collective-permute-start(bf16[256,2304]{1,0:T(8,128)(2,1)} %get-tuple-element.34), channel_id=1, source_target_pairs={{0,8},{1,9},{8,16},{9,17},{16,24},{17,25},{24,0},{25,1},{2,10},{3,... | collective-permute-start | bytes 3538952 | tf_op jit(solution)/shard_map/ppermute | solution.py:43
  15.4 30.3 %collective-permute-start.1 = (bf16[256,2304]{1,0:T(8,128)(2,1)}, bf16[256,2304]{1,0:T(8,128)(2,1)}, u32[]{:S(2)}, u32[]{:S(2)}) collective-permute-start(bf16[256,2304]{1,0:T(8,128)(2,1)} %get-tuple-element.35), channel_id=1, source_target_pairs={{0,24},{1,25},{8,0},{9,1},{16,8},{17,9},{24,16},{25,17},{2,26},{3,... | collective-permute-start | bytes 3538952 | tf_op jit(solution)/shard_map/ppermute | solution.py:43
  30.0 14.3 %collective-permute-start.4 = (bf16[256,1024]{1,0:T(8,128)(2,1)}, bf16[256,1024]{1,0:T(8,128)(2,1)}, u32[]{:S(2)}, u32[]{:S(2)}) collective-permute-start(bf16[256,1024]{1,0:T(8,128)(2,1)} %add.239), channel_id=1, source_target_pairs={{0,2},{128,134},{2,4},{130,128},{4,6},{132,130},{6,0},{134,132},{1... | collective-permute-start | bytes 1572872 | tf_op jit(solution)/shard_map/ppermute | solution.py:51
  32.4 27.7 %collective-permute-start.7 = (bf16[256,1280]{1,0:T(8,128)(2,1)}, bf16[256,1280]{1,0:T(8,128)(2,1)S(1)}, u32[]{:S(2)}, u32[]{:S(2)}) collective-permute-start(bf16[256,1280]{1,0:T(8,128)(2,1)} %get-tuple-element.44), channel_id=1, source_target_pairs={{0,16},{1,17},{8,24},{9,25},{16,0},{17,1},{24,8},{25,9},{2,18},{3,... | collective-permute-start | bytes 1966088 | tf_op jit(solution)/shard_map/ppermute | solution.py:43
  45.5 13.2 %collective-permute-start.9 = (bf16[256,1024]{1,0:T(8,128)(2,1)S(1)}, bf16[256,1024]{1,0:T(8,128)(2,1)S(1)}, u32[]{:S(2)}, u32[]{:S(2)}) collective-permute-start(bf16[256,1024]{1,0:T(8,128)(2,1)S(1)} %add.240.after_ref), channel_id=1, source_target_pairs={{0,2},{128,134},{2,4},{130,128},{4,6},{132,130},{6,0},{134,132},{1... | collective-permute-start | bytes 1572872 | tf_op jit(solution)/shard_map/ppermute | solution.py:51
  46.7 14.6 %collective-permute-start.5 = (bf16[256,512]{1,0:T(8,128)(2,1)S(1)}, bf16[256,512]{1,0:T(8,128)(2,1)S(1)}, u32[]{:S(2)}, u32[]{:S(2)}) collective-permute-start(bf16[256,512]{1,0:T(8,128)(2,1)S(1)} %get-tuple-element.41), channel_id=1, source_target_pairs={{0,8},{1,9},{8,16},{9,17},{16,24},{17,25},{24,0},{25,1},{2,10},{3,... | collective-permute-start | bytes 786440 | tf_op jit(solution)/shard_map/ppermute | solution.py:43
  48.1 13.2 %collective-permute-start.6 = (bf16[256,512]{1,0:T(8,128)(2,1)S(1)}, bf16[256,512]{1,0:T(8,128)(2,1)S(1)}, u32[]{:S(2)}, u32[]{:S(2)}) collective-permute-start(bf16[256,512]{1,0:T(8,128)(2,1)S(1)} %get-tuple-element.42), channel_id=1, source_target_pairs={{0,24},{1,25},{8,0},{9,1},{16,8},{17,9},{24,16},{25,17},{2,26},{3,... | collective-permute-start | bytes 786440 | tf_op jit(solution)/shard_map/ppermute | solution.py:43
  64.7 9.2 %collective-permute-start.10 = (bf16[512,640]{1,0:T(8,128)(2,1)S(1)}, bf16[512,640]{1,0:T(8,128)(2,1)S(1)}, u32[]{:S(2)}, u32[]{:S(2)}) collective-permute-start(bf16[512,640]{1,0:T(8,128)(2,1)S(1)} %get-tuple-element.53), channel_id=1, source_target_pairs={{0,1},{1,0},{8,9},{9,8},{16,17},{17,16},{24,25},{25,24},{2,3},{3,2... | collective-permute-start | bytes 1966088 | tf_op jit(solution)/shard_map/ppermute | solution.py:43
  73.5 14.5 %collective-permute-start.8 = (bf16[512,640]{1,0:T(8,128)(2,1)}, bf16[512,640]{1,0:T(8,128)(2,1)S(1)}, u32[]{:S(2)}, u32[]{:S(2)}) collective-permute-start(bf16[512,640]{1,0:T(8,128)(2,1)} %get-tuple-element.46), channel_id=1, source_target_pairs={{0,1},{1,0},{8,9},{9,8},{16,17},{17,16},{24,25},{25,24},{2,3},{3,2... | collective-permute-start | bytes 1966088 | tf_op jit(solution)/shard_map/ppermute | solution.py:43
  73.9 8.7 %collective-permute-start.11 = (bf16[128,640]{1,0:T(8,128)(2,1)S(1)}, bf16[128,640]{1,0:T(8,128)(2,1)S(1)}, u32[]{:S(2)}, u32[]{:S(2)}) collective-permute-start(bf16[128,640]{1,0:T(8,128)(2,1)S(1)} %add.241), channel_id=1, source_target_pairs={{0,2},{128,134},{2,4},{130,128},{4,6},{132,130},{6,0},{134,132},{1... | collective-permute-start | bytes 491528 | tf_op jit(solution)/shard_map/ppermute | solution.py:51
  82.6 6.6 %collective-permute-start.18 = (bf16[128,640]{1,0:T(8,128)(2,1)S(1)}, bf16[128,640]{1,0:T(8,128)(2,1)S(1)}, u32[]{:S(2)}, u32[]{:S(2)}) collective-permute-start(bf16[128,640]{1,0:T(8,128)(2,1)S(1)} %add.242.refs_2_), channel_id=1, source_target_pairs={{0,2},{128,134},{2,4},{130,128},{4,6},{132,130},{6,0},{134,132},{1... | collective-permute-start | bytes 491528 | tf_op jit(solution)/shard_map/ppermute | solution.py:51
  82.7 11.6 %collective-permute-start.15 = (bf16[256,256]{1,0:T(8,128)(2,1)}, bf16[256,256]{1,0:T(8,128)(2,1)S(1)}, u32[]{:S(2)}, u32[]{:S(2)}) collective-permute-start(bf16[256,256]{1,0:T(8,128)(2,1)} %get-tuple-element.55), channel_id=1, source_target_pairs={{0,8},{1,9},{8,16},{9,17},{16,24},{17,25},{24,0},{25,1},{2,10},{3,... | collective-permute-start | bytes 393224 | tf_op jit(solution)/shard_map/ppermute | solution.py:43
  83.9 10.4 %collective-permute-start.16 = (bf16[256,256]{1,0:T(8,128)(2,1)}, bf16[256,256]{1,0:T(8,128)(2,1)S(1)}, u32[]{:S(2)}, u32[]{:S(2)}) collective-permute-start(bf16[256,256]{1,0:T(8,128)(2,1)} %get-tuple-element.56), channel_id=1, source_target_pairs={{0,16},{1,17},{8,24},{9,25},{16,0},{17,1},{24,8},{25,9},{2,18},{3,... | collective-permute-start | bytes 393224 | tf_op jit(solution)/shard_map/ppermute | solution.py:43
  87.0 7.3 %collective-permute-start.17 = (bf16[256,256]{1,0:T(8,128)(2,1)S(1)}, bf16[256,256]{1,0:T(8,128)(2,1)S(1)}, u32[]{:S(2)}, u32[]{:S(2)}) collective-permute-start(bf16[256,256]{1,0:T(8,128)(2,1)S(1)} %copy-done.13), channel_id=1, source_target_pairs={{0,24},{1,25},{8,0},{9,1},{16,8},{17,9},{24,16},{25,17},{2,26},{3,... | collective-permute-start | bytes 393224 | tf_op jit(solution)/shard_map/ppermute | solution.py:43
  88.1 6.0 %collective-permute-start.12 = (bf16[128,640]{1,0:T(8,128)(2,1)S(1)}, bf16[128,640]{1,0:T(8,128)(2,1)S(1)}, u32[]{:S(2)}, u32[]{:S(2)}) collective-permute-start(bf16[128,640]{1,0:T(8,128)(2,1)S(1)} %add.243), channel_id=1, source_target_pairs={{0,2},{128,134},{2,4},{130,128},{4,6},{132,130},{6,0},{134,132},{1... | collective-permute-start | bytes 491528 | tf_op jit(solution)/shard_map/ppermute | solution.py:51
  89.2 8.1 %collective-permute-start.19 = (bf16[128,640]{1,0:T(8,128)(2,1)S(1)}, bf16[128,640]{1,0:T(8,128)(2,1)S(1)}, u32[]{:S(2)}, u32[]{:S(2)}) collective-permute-start(bf16[128,640]{1,0:T(8,128)(2,1)S(1)} %add.247), channel_id=1, source_target_pairs={{0,2},{128,134},{2,4},{130,128},{4,6},{132,130},{6,0},{134,132},{1... | collective-permute-start | bytes 491528 | tf_op jit(solution)/shard_map/ppermute | solution.py:51
  94.2 7.9 %collective-permute-start.13 = (bf16[128,640]{1,0:T(8,128)(2,1)S(1)}, bf16[128,640]{1,0:T(8,128)(2,1)S(1)}, u32[]{:S(2)}, u32[]{:S(2)}) collective-permute-start(bf16[128,640]{1,0:T(8,128)(2,1)S(1)} %add.244), channel_id=1, source_target_pairs={{0,2},{128,134},{2,4},{130,128},{4,6},{132,130},{6,0},{134,132},{1... | collective-permute-start | bytes 491528 | tf_op jit(solution)/shard_map/ppermute | solution.py:51
  97.4 12.6 %collective-permute-start.20 = (bf16[128,896]{1,0:T(8,128)(2,1)S(1)}, bf16[128,896]{1,0:T(8,128)(2,1)S(1)}, u32[]{:S(2)}, u32[]{:S(2)}) collective-permute-start(bf16[128,896]{1,0:T(8,128)(2,1)S(1)} %add.248), channel_id=1, source_target_pairs={{0,230},{2,228},{4,226},{6,224},{32,198},{34,196},{36,194},{38,192... | collective-permute-start | bytes 688136 | tf_op jit(solution)/shard_map/ppermute | solution.py:62
  102.2 7.8 %collective-permute-start.14 = (bf16[128,640]{1,0:T(8,128)(2,1)S(1)}, bf16[128,640]{1,0:T(8,128)(2,1)S(1)}, u32[]{:S(2)}, u32[]{:S(2)}) collective-permute-start(bf16[128,640]{1,0:T(8,128)(2,1)S(1)} %add.245), channel_id=1, source_target_pairs={{0,2},{128,134},{2,4},{130,128},{4,6},{132,130},{6,0},{134,132},{1... | collective-permute-start | bytes 491528 | tf_op jit(solution)/shard_map/ppermute | solution.py:51
  126.3 8.9 %collective-permute-start.21 = (bf16[4,32,896]{2,1,0:T(8,128)(2,1)S(1)}, bf16[4,32,896]{2,1,0:T(8,128)(2,1)S(1)}, u32[]{:S(2)}, u32[]{:S(2)}) collective-permute-start(bf16[4,32,896]{2,1,0:T(8,128)(2,1)S(1)} %get-tuple-element.67), channel_id=1, source_target_pairs={{0,1},{1,0},{8,9},{9,8},{16,17},{17,16},{24,25},{25,24},{2,3},{3,2... | collective-permute-start | bytes 688136 | tf_op jit(solution)/shard_map/ppermute | solution.py:43
  135.3 7.9 %collective-permute-start.22 = (bf16[2,32,896]{2,1,0:T(8,128)(2,1)S(1)}, bf16[2,32,896]{2,1,0:T(8,128)(2,1)S(1)}, u32[]{:S(2)}, u32[]{:S(2)}) collective-permute-start(bf16[2,32,896]{2,1,0:T(8,128)(2,1)S(1)} %get-tuple-element.65), channel_id=1, source_target_pairs={{0,8},{1,9},{8,16},{9,17},{16,24},{17,25},{24,0},{25,1},{2,10},{3,... | collective-permute-start | bytes 344072 | tf_op jit(solution)/shard_map/ppermute | solution.py:43
  135.4 11.1 %collective-permute-start.23 = (bf16[2,32,896]{2,1,0:T(8,128)(2,1)S(1)}, bf16[2,32,896]{2,1,0:T(8,128)(2,1)S(1)}, u32[]{:S(2)}, u32[]{:S(2)}) collective-permute-start(bf16[2,32,896]{2,1,0:T(8,128)(2,1)S(1)} %get-tuple-element.66), channel_id=1, source_target_pairs={{0,16},{1,17},{8,24},{9,25},{16,0},{17,1},{24,8},{25,9},{2,18},{3,... | collective-permute-start | bytes 344072 | tf_op jit(solution)/shard_map/ppermute | solution.py:43
  (15 other events, 166.3 us)

commit v2 on v1

--- a/solution.py
+++ b/solution.py
@@ -11,7 +11,8 @@
 NEAR = (1, NY - 1)
 COLS, LATE = 896, 256
 EARLY = COLS - LATE
-LAG, FORWARD = 1, 1
+LAG, FORWARD = 0, 1
+COST = 1
 OFFSETS = tuple((dy, dc) for dy in range(NY) for dc in range(NC))
 
 beta_first = 0.9
@@ -184,7 +185,7 @@
 
 
 def chip_product_kernel(own_ref, late_ref, swap_ref, *rest):
-    outs, (left, right, sem) = rest[:NZ], rest[NZ:]
+    outs, (left, right, sem) = rest[:2 * NZ], rest[2 * NZ:]
     rows, width = own_ref.shape
     pairs = [
         (own_ref, left.at[0]),
@@ -197,9 +198,8 @@
         at = slice(block * rows, (block + 1) * rows)
         both = jnp.concatenate([left[0, :, at], left[1, :, at]], 1)
         total = jnp.dot(both, right[...], preferred_element_type=f32).astype(bf16)
-        half, step = block // 2, block % 2 * 2
         for i in range(2):
-            outs[step + i][half * 128:(half + 1) * 128, :] = total[i * 128:(i + 1) * 128]
+            outs[block * 2 + i][...] = total[i * 128:(i + 1) * 128]
 
 
 def chip_product(own, late, swap):
@@ -207,9 +207,9 @@
     cols = late.shape[1]
     return pl.pallas_call(
         chip_product_kernel,
-        out_shape=[jax.ShapeDtypeStruct((256, cols), bf16)] * NZ,
+        out_shape=[jax.ShapeDtypeStruct((128, cols), bf16)] * (2 * NZ),
         in_specs=[ANY] * 3,
-        out_specs=[VMEM] * NZ,
+        out_specs=[VMEM] * (2 * NZ),
         scratch_shapes=[
             pltpu.VMEM((NC, rows, width), bf16),
             pltpu.VMEM((NC * rows, cols), bf16),
@@ -220,23 +220,25 @@
     )(own, late, swap)
 
 
-def split_kernel(part_ref, moved_ref, *outs):
+def split_kernel(*refs):
     y = lax.axis_index("y")
-    for dy, out_ref in enumerate(outs):
-        at = pl.ds(pl.multiple_of(lax.rem(y + dy, NY) * LATE, 128), LATE)
-        total = part_ref[:, at].astype(f32) + moved_ref[:, at].astype(f32)
-        out_ref[...] = total.astype(bf16)
-
-
-def split(part, moved):
+    for half in range(2):
+        part_ref, moved_ref = refs[2 * half], refs[2 * half + 1]
+        for dy, out_ref in enumerate(refs[4:]):
+            at = pl.ds(pl.multiple_of(lax.rem(y + dy, NY) * LATE, 128), LATE)
+            total = part_ref[:, at].astype(f32) + moved_ref[:, at].astype(f32)
+            out_ref[half * 128:(half + 1) * 128, :] = total.astype(bf16)
+
+
+def split(*terms):
     return pl.pallas_call(
         split_kernel,
-        out_shape=[jax.ShapeDtypeStruct((part.shape[0], LATE), bf16)] * NY,
-        in_specs=[VMEM] * 2,
+        out_shape=[jax.ShapeDtypeStruct((256, LATE), bf16)] * NY,
+        in_specs=[VMEM] * 4,
         out_specs=[VMEM] * NY,
         compiler_params=SMALL,
         name="split",
-    )(part, moved)
+    )(*terms)
 
 
 def product_kernel(part, n_after, *refs):
@@ -281,7 +283,7 @@
         ],
         compiler_params=PARAMS,
         cost_estimate=pl.CostEstimate(
-            flops=width * NC * EARLY * depth,
+            flops=COST * width * NC * EARLY * depth,
             bytes_accessed=width * (depth + NC * EARLY) + 2 * depth * NC * EARLY,
             transcendentals=0,
         ),
@@ -380,11 +382,16 @@
     grads = [mine, near[0], send_group(opposite, 2, 0), near[1]]
 
     parts = chip_product(own, late, send_group(swap, 0, 1))
-    moving, steps = parts[0], []
+    moving, steps = [parts[0], parts[NZ]], []
     for step in range(1, NZ - 1):
-        moving = add([(parts[step], 0), (send_ring(moving, 1), 0)], bf16, rows=256)
-        steps.append(moving)
-    pieces = split(parts[NZ - 1], send_ring(moving, 1))
+        moving = [
+            add([(parts[half * NZ + step], 0), (send_ring(moving[half], 1), 0)], bf16)
+            for half in range(2)
+        ]
+        steps.append(moving[1])
+    pieces = split(
+        parts[NZ - 1], send_ring(moving[0], 1), parts[2 * NZ - 1], send_ring(moving[1], 1)
+    )
     late = [send_group(piece, dy, 0) for dy, piece in enumerate(pieces)]
 
     far = forward(near[0], near[1], half, steps[FORWARD])

time: 150 us -> 144 us (0.960)
  waiting for transfers between devices: 62.5 us -> 55.8 us
  starting transfers between devices: 43.7 us -> 40.5 us
  local copies, waits for them, and re-layouts: 3.03 us -> 5.44 us
    ppermute x9 -> x12, waiting for transfers between devices: 53.3 us -> 38.4 us  [send_ring(): return lax.ppermute(value, ('zh', 'z'), pairs)]
    ppermute x15, waiting for transfers between devices: 9.21 us -> 17.4 us  [send_group(): return lax.ppermute(value, ('y', 'c'), pairs)]
    ppermute x15, starting transfers between devices: 36.7 us -> 33.3 us  [send_group(): return lax.ppermute(value, ('y', 'c'), pairs)]
    unnamed x28 -> x32, local copies, waits for them, and re-layouts: 2.81 us -> 5.21 us
  transfers between devices with their start and end apart: 25 -> 28, of which waited for: 13 -> 14; matrix products, arithmetic and copies ran while one was open for 0% -> 0% of each run, Pallas kernels for 7% -> 9%
where the time goes in v2:
time: 144 us; the launch traced here: 143 us
  waiting for transfers between devices  55.8 us (39%)
  starting transfers between devices  40.5 us (28%)
  Pallas kernels  23.2 us (16%)
  blocking collectives  16.2 us (11%)
  local copies, waits for them, and re-layouts  5.44 us (4%)
    ppermute x12, waiting for transfers between devices, send_ring(): return lax.ppermute(value, ('zh', 'z'), pairs)  38.4 us
    ppermute x15, starting transfers between devices, send_group(): return lax.ppermute(value, ('y', 'c'), pairs)  33.3 us
    ppermute x15, waiting for transfers between devices, send_group(): return lax.ppermute(value, ('y', 'c'), pairs)  17.4 us
    all_gather x1, blocking collectives, per_device(): gathered = lax.all_gather(tile, 'z', axis=0, tiled=True)  16.2 us
    pallas_call x2, Pallas kernels, product(): pl.pallas_call(functools.partial(product_kernel, part, len(after)), out_s...  7.39 us
    unnamed x32, local copies, waits for them, and re-layouts  5.21 us
    ppermute x1, starting transfers between devices, send_mirror(): return lax.ppermute(value, ('zh', 'x', 'z'), pairs)  4.84 us
    pallas_call x1, Pallas kernels, prepare(): pl.pallas_call(prepare_kernel, out_shape=[jax.ShapeDtypeStruct((rows, col...  4.09 us
  transfers between devices with their start and end apart: 28, of which 14 were waited for; matrix products, arithmetic and copies ran while one was open for 0% of the time, Pallas kernels for 9%

profile of v2, /device:TPU:1, one launch (start us, length us, event | category | flops | bytes accessed | tf_op | source)
XLA Modules:
  0.0 143.1 jit_solution(16415550186456959994)
XLA Ops:
  0.6 4.1 %prepare.1 = (bf16[256,1024]{1,0:T(8,128)(2,1)}, bf16[256,2304]{1,0:T(8,128)(2,1)}, bf16[256,2304]{1,0:T(8,128)(2,1)}, bf16[256,2048]{1,0:T(8,128)(2,1)}, bf16[256,1024]{1,0:T(8,128)(2,1)}) custom-call(s32[8,32]{1,0:T(8,128)} %live_hbm.1, bf16[256,1024]{1,0:T(8,128)(2,1)} %hidden_hbm.1, bf16[256,7168]{1,0:T(8,128)(2,1)} %grad_hbm.3), custom_call_target="tpu_custom_call" | custom-call | tf_op jit(solution)/shard_map/prepare/pallas_call | solution.py:121
  4.7 3.3 %collective-permute-start.2 = (bf16[256,2048]{1,0:T(8,128)(2,1)}, bf16[256,2048]{1,0:T(8,128)(2,1)S(1)}, u32[]{:S(2)}, u32[]{:S(2)}) collective-permute-start(bf16[256,2048]{1,0:T(8,128)(2,1)} %get-tuple-element.41), channel_id=1, source_target_pairs={{0,1},{1,0},{8,9},{9,8},{16,17},{17,16},{24,25},{25,24},{2,3},{3,2... | collective-permute-start | bytes 3145736 | tf_op jit(solution)/shard_map/ppermute | solution.py:44
  8.1 2.7 %collective-permute-start.1 = (bf16[256,2304]{1,0:T(8,128)(2,1)}, bf16[256,2304]{1,0:T(8,128)(2,1)}, u32[]{:S(2)}, u32[]{:S(2)}) collective-permute-start(bf16[256,2304]{1,0:T(8,128)(2,1)} %get-tuple-element.39), channel_id=1, source_target_pairs={{0,24},{1,25},{8,0},{9,1},{16,8},{17,9},{24,16},{25,17},{2,26},{3,... | collective-permute-start | bytes 3538952 | tf_op jit(solution)/shard_map/ppermute | solution.py:44
  18.4 2.4 %pack.1 = (bf16[256,1280]{1,0:T(8,128)(2,1)}, bf16[256,1280]{1,0:T(8,128)(2,1)}) custom-call(bf16[256,7168]{1,0:T(8,128)(2,1)} %grad_hbm.3, bf16[256,1024]{1,0:T(8,128)(2,1)} %get-tuple-element.37.own_ref.after_ref.refs_0_), custom_call_target="tpu_custom_call" | custom-call | tf_op jit(solution)/shard_map/pack/pallas_call | solution.py:154
  20.8 2.8 %collective-permute-start.7 = (bf16[256,1280]{1,0:T(8,128)(2,1)}, bf16[256,1280]{1,0:T(8,128)(2,1)S(1)}, u32[]{:S(2)}, u32[]{:S(2)}) collective-permute-start(bf16[256,1280]{1,0:T(8,128)(2,1)} %get-tuple-element.48), channel_id=1, source_target_pairs={{0,16},{1,17},{8,24},{9,25},{16,0},{17,1},{24,8},{25,9},{2,18},{3,... | collective-permute-start | bytes 1966088 | tf_op jit(solution)/shard_map/ppermute | solution.py:44
  23.6 2.6 %collective-permute-done.3.refs_1_ = bf16[128,1024]{1,0:T(8,128)(2,1)} collective-permute-done((bf16[128,1024]{1,0:T(8,128)(2,1)}, bf16[128,1024]{1,0:T(8,128)(2,1)}, u32[]{:S(2)}, u32[]{:S(2)}) %collective-permute-start.3) | collective-permute-done | bytes 262176 | tf_op jit(solution)/shard_map/ppermute | solution.py:52
  28.2 3.6 %collective-permute-done.9.refs_1_ = bf16[128,1024]{1,0:T(8,128)(2,1)} collective-permute-done((bf16[128,1024]{1,0:T(8,128)(2,1)}, bf16[128,1024]{1,0:T(8,128)(2,1)}, u32[]{:S(2)}, u32[]{:S(2)}) %collective-permute-start.9) | collective-permute-done | bytes 262176 | tf_op jit(solution)/shard_map/ppermute | solution.py:52
  32.9 2.4 %collective-permute-done.4.refs_1_ = bf16[128,1024]{1,0:T(8,128)(2,1)S(1)} collective-permute-done((bf16[128,1024]{1,0:T(8,128)(2,1)S(1)}, bf16[128,1024]{1,0:T(8,128)(2,1)S(1)}, u32[]{:S(2)}, u32[]{:S(2)}) %collective-permute-start.4) | collective-permute-done | bytes 262176 | tf_op jit(solution)/shard_map/ppermute | solution.py:52
  35.5 7.6 %collective-permute-done.10.refs_1_ = bf16[128,1024]{1,0:T(8,128)(2,1)S(1)} collective-permute-done((bf16[128,1024]{1,0:T(8,128)(2,1)S(1)}, bf16[128,1024]{1,0:T(8,128)(2,1)S(1)}, u32[]{:S(2)}, u32[]{:S(2)}) %collective-permute-start.10) | collective-permute-done | bytes 262176 | tf_op jit(solution)/shard_map/ppermute | solution.py:52
  43.3 6.7 %collective-permute-done.1.down_ref.refs_3_.refs_8_ = bf16[256,2304]{1,0:T(8,128)(2,1)} collective-permute-done((bf16[256,2304]{1,0:T(8,128)(2,1)}, bf16[256,2304]{1,0:T(8,128)(2,1)}, u32[]{:S(2)}, u32[]{:S(2)}) %collective-permute-start.1) | collective-permute-done | bytes 1179680 | tf_op jit(solution)/shard_map/ppermute | solution.py:44
  51.1 3.8 %collective-permute-start.6 = (bf16[256,512]{1,0:T(8,128)(2,1)S(1)}, bf16[256,512]{1,0:T(8,128)(2,1)S(1)}, u32[]{:S(2)}, u32[]{:S(2)}) collective-permute-start(bf16[256,512]{1,0:T(8,128)(2,1)S(1)} %get-tuple-element.46), channel_id=1, source_target_pairs={{0,24},{1,25},{8,0},{9,1},{16,8},{17,9},{24,16},{25,17},{2,26},{3,... | collective-permute-start | bytes 786440 | tf_op jit(solution)/shard_map/ppermute | solution.py:44
  55.7 4.2 %collective-permute-done.5.refs_2_ = bf16[256,512]{1,0:T(8,128)(2,1)S(1)} collective-permute-done((bf16[256,512]{1,0:T(8,128)(2,1)S(1)}, bf16[256,512]{1,0:T(8,128)(2,1)S(1)}, u32[]{:S(2)}, u32[]{:S(2)}) %collective-permute-start.5) | collective-permute-done | bytes 262176 | tf_op jit(solution)/shard_map/ppermute | solution.py:44
  59.9 3.3 %product.3 = (bf16[128,640]{1,0:T(8,128)(2,1)S(1)}, bf16[128,640]{1,0:T(8,128)(2,1)S(1)}, bf16[128,640]{1,0:T(8,128)(2,1)S(1)}, bf16[128,640]{1,0:T(8,128)(2,1)S(1)}, bf16[512,640]{1,0:T(8,128)(2,1)S(1)}) custom-call(bf16[256,1024]{1,0:T(8,128)(2,1)S(1)} %copy-done.1, bf16[256,2304]{1,0:T(8,128)(2,1)S(1)} %collective-permute-done.up_ref.refs_1_.refs_6_, ...), custom_call_target="tpu_custom_call" | custom-call | flops 1342177280 | bytes 4980736 | tf_op jit(solution)/shard_map/product/pallas_call | solution.py:274
  65.3 4.1 %product.2 = (bf16[128,640]{1,0:T(8,128)(2,1)S(1)}, bf16[128,640]{1,0:T(8,128)(2,1)S(1)}, bf16[128,640]{1,0:T(8,128)(2,1)S(1)}, bf16[128,640]{1,0:T(8,128)(2,1)S(1)}, bf16[512,640]{1,0:T(8,128)(2,1)}) custom-call(bf16[256,1024]{1,0:T(8,128)(2,1)S(1)} %copy-done.1, bf16[256,2304]{1,0:T(8,128)(2,1)S(1)} %collective-permute-done.up_ref.refs_1_.refs_6_, ...), custom_call_target="tpu_custom_call" | custom-call | flops 1342177280 | bytes 4980736 | tf_op jit(solution)/shard_map/product/pallas_call | solution.py:274
  69.7 7.1 %collective-permute-done.20.refs_2_ = bf16[128,640]{1,0:T(8,128)(2,1)S(1)} collective-permute-done((bf16[128,640]{1,0:T(8,128)(2,1)S(1)}, bf16[128,640]{1,0:T(8,128)(2,1)S(1)}, u32[]{:S(2)}, u32[]{:S(2)}) %collective-permute-start.20) | collective-permute-done | bytes 163872 | tf_op jit(solution)/shard_map/ppermute | solution.py:52
  77.9 3.3 %collective-permute-start.18 = (bf16[256,256]{1,0:T(8,128)(2,1)}, bf16[256,256]{1,0:T(8,128)(2,1)S(1)}, u32[]{:S(2)}, u32[]{:S(2)}) collective-permute-start(bf16[256,256]{1,0:T(8,128)(2,1)} %get-tuple-element.63), channel_id=1, source_target_pairs={{0,16},{1,17},{8,24},{9,25},{16,0},{17,1},{24,8},{25,9},{2,18},{3,... | collective-permute-start | bytes 393224 | tf_op jit(solution)/shard_map/ppermute | solution.py:44
  83.4 4.7 %collective-permute-done.14.refs_2_ = bf16[128,640]{1,0:T(8,128)(2,1)S(1)} collective-permute-done((bf16[128,640]{1,0:T(8,128)(2,1)S(1)}, bf16[128,640]{1,0:T(8,128)(2,1)S(1)}, u32[]{:S(2)}, u32[]{:S(2)}) %collective-permute-start.14) | collective-permute-done | bytes 163872 | tf_op jit(solution)/shard_map/ppermute | solution.py:52
  90.8 4.8 %collective-permute-start.23 = (bf16[128,896]{1,0:T(8,128)(2,1)S(1)}, bf16[128,896]{1,0:T(8,128)(2,1)S(1)}, u32[]{:S(2)}, u32[]{:S(2)}) collective-permute-start(bf16[128,896]{1,0:T(8,128)(2,1)S(1)} %add.252), channel_id=1, source_target_pairs={{0,230},{2,228},{4,226},{6,224},{32,198},{34,196},{36,194},{38,192... | collective-permute-start | bytes 688136 | tf_op jit(solution)/shard_map/ppermute | solution.py:63
  96.0 7.0 %collective-permute-done.16.refs_2_ = bf16[128,640]{1,0:T(8,128)(2,1)S(1)} collective-permute-done((bf16[128,640]{1,0:T(8,128)(2,1)S(1)}, bf16[128,640]{1,0:T(8,128)(2,1)S(1)}, u32[]{:S(2)}, u32[]{:S(2)}) %collective-permute-start.16) | collective-permute-done | bytes 163872 | tf_op jit(solution)/shard_map/ppermute | solution.py:52
  103.2 16.2 %all_gather.3 = bf16[512,896]{1,0:T(8,128)(2,1)S(1)} all-gather(bf16[128,896]{1,0:T(8,128)(2,1)S(1)} %add_convert_fusion), channel_id=1, replica_groups=mesh['zh'=2,'x'=4,'y'=4,'z'=4,'c'=2] {'z'}, dimensions={0}, use_global_device_ids=true | all-gather | bytes 1146880 | tf_op jit(solution)/shard_map/all_gather | solution.py:416
  120.0 8.4 %collective-permute-start.24 = (bf16[4,32,896]{2,1,0:T(8,128)(2,1)S(1)}, bf16[4,32,896]{2,1,0:T(8,128)(2,1)S(1)}, u32[]{:S(2)}, u32[]{:S(2)}) collective-permute-start(bf16[4,32,896]{2,1,0:T(8,128)(2,1)S(1)} %get-tuple-element.75), channel_id=1, source_target_pairs={{0,1},{1,0},{8,9},{9,8},{16,17},{17,16},{24,25},{25,24},{2,3},{3,2... | collective-permute-start | bytes 688136 | tf_op jit(solution)/shard_map/ppermute | solution.py:44
  129.7 5.1 %collective-permute-start.26 = (bf16[2,32,896]{2,1,0:T(8,128)(2,1)S(1)}, bf16[2,32,896]{2,1,0:T(8,128)(2,1)S(1)}, u32[]{:S(2)}, u32[]{:S(2)}) collective-permute-start(bf16[2,32,896]{2,1,0:T(8,128)(2,1)S(1)} %get-tuple-element.74), channel_id=1, source_target_pairs={{0,16},{1,17},{8,24},{9,25},{16,0},{17,1},{24,8},{25,9},{2,18},{3,... | collective-permute-start | bytes 344072 | tf_op jit(solution)/shard_map/ppermute | solution.py:44
  136.8 3.3 %collective-permute-done.26.refs_3_ = bf16[2,32,896]{2,1,0:T(8,128)(2,1)S(1)} collective-permute-done((bf16[2,32,896]{2,1,0:T(8,128)(2,1)S(1)}, bf16[2,32,896]{2,1,0:T(8,128)(2,1)S(1)}, u32[]{:S(2)}, u32[]{:S(2)}) %collective-permute-start.26) | collective-permute-done | bytes 114720 | tf_op jit(solution)/shard_map/ppermute | solution.py:44
  140.2 3.0 %adamw.1 = (f32[32,7168]{1,0:T(8,128)}, bf16[32,7168]{1,0:T(8,128)(2,1)}, bf16[32,7168]{1,0:T(8,128)(2,1)}) custom-call(s32[8,32]{1,0:T(8,128)S(1)} %copy-done.15, bf16[2,32,896]{2,1,0:T(8,128)(2,1)S(1)} %get-tuple-element.72.refs_1_, bf16[2,32,896]{2,1,0:T(8,128)(2,1)S(1)} %collective-permute-done.25.refs_2_, ...), custom_call_target="tpu_custom_call" | custom-call | tf_op jit(solution)/shard_map/adamw/pallas_call | solution.py:345
  (95 shorter events, 25.7 us)
Async XLA Ops:
  8.1 35.2 %collective-permute-start = (bf16[256,2304]{1,0:T(8,128)(2,1)}, bf16[256,2304]{1,0:T(8,128)(2,1)S(1)}, u32[]{:S(2)}, u32[]{:S(2)}) collective-permute-start(bf16[256,2304]{1,0:T(8,128)(2,1)} %get-tuple-element.38), channel_id=1, source_target_pairs={{0,8},{1,9},{8,16},{9,17},{16,24},{17,25},{24,0},{25,1},{2,10},{3,... | collective-permute-start | bytes 3538952 | tf_op jit(solution)/shard_map/ppermute | solution.py:44
  8.1 41.9 %collective-permute-start.1 = (bf16[256,2304]{1,0:T(8,128)(2,1)}, bf16[256,2304]{1,0:T(8,128)(2,1)}, u32[]{:S(2)}, u32[]{:S(2)}) collective-permute-start(bf16[256,2304]{1,0:T(8,128)(2,1)} %get-tuple-element.39), channel_id=1, source_target_pairs={{0,24},{1,25},{8,0},{9,1},{16,8},{17,9},{24,16},{25,17},{2,26},{3,... | collective-permute-start | bytes 3538952 | tf_op jit(solution)/shard_map/ppermute | solution.py:44
  16.8 9.3 %collective-permute-start.3 = (bf16[128,1024]{1,0:T(8,128)(2,1)}, bf16[128,1024]{1,0:T(8,128)(2,1)}, u32[]{:S(2)}, u32[]{:S(2)}) collective-permute-start(bf16[128,1024]{1,0:T(8,128)(2,1)} %get-tuple-element.44), channel_id=1, source_target_pairs={{0,2},{128,134},{2,4},{130,128},{4,6},{132,130},{6,0},{134,132},{1... | collective-permute-start | bytes 786440 | tf_op jit(solution)/shard_map/ppermute | solution.py:52
  16.8 14.9 %collective-permute-start.9 = (bf16[128,1024]{1,0:T(8,128)(2,1)}, bf16[128,1024]{1,0:T(8,128)(2,1)}, u32[]{:S(2)}, u32[]{:S(2)}) collective-permute-start(bf16[128,1024]{1,0:T(8,128)(2,1)} %get-tuple-element.57), channel_id=1, source_target_pairs={{0,2},{128,134},{2,4},{130,128},{4,6},{132,130},{6,0},{134,132},{1... | collective-permute-start | bytes 786440 | tf_op jit(solution)/shard_map/ppermute | solution.py:52
  20.8 34.9 %collective-permute-start.7 = (bf16[256,1280]{1,0:T(8,128)(2,1)}, bf16[256,1280]{1,0:T(8,128)(2,1)S(1)}, u32[]{:S(2)}, u32[]{:S(2)}) collective-permute-start(bf16[256,1280]{1,0:T(8,128)(2,1)} %get-tuple-element.48), channel_id=1, source_target_pairs={{0,16},{1,17},{8,24},{9,25},{16,0},{17,1},{24,8},{25,9},{2,18},{3,... | collective-permute-start | bytes 1966088 | tf_op jit(solution)/shard_map/ppermute | solution.py:44
  28.1 7.2 %collective-permute-start.4 = (bf16[128,1024]{1,0:T(8,128)(2,1)S(1)}, bf16[128,1024]{1,0:T(8,128)(2,1)S(1)}, u32[]{:S(2)}, u32[]{:S(2)}) collective-permute-start(bf16[128,1024]{1,0:T(8,128)(2,1)S(1)} %add.241), channel_id=1, source_target_pairs={{0,2},{128,134},{2,4},{130,128},{4,6},{132,130},{6,0},{134,132},{1... | collective-permute-start | bytes 786440 | tf_op jit(solution)/shard_map/ppermute | solution.py:52
  32.8 10.3 %collective-permute-start.10 = (bf16[128,1024]{1,0:T(8,128)(2,1)S(1)}, bf16[128,1024]{1,0:T(8,128)(2,1)S(1)}, u32[]{:S(2)}, u32[]{:S(2)}) collective-permute-start(bf16[128,1024]{1,0:T(8,128)(2,1)S(1)} %add.243), channel_id=1, source_target_pairs={{0,2},{128,134},{2,4},{130,128},{4,6},{132,130},{6,0},{134,132},{1... | collective-permute-start | bytes 786440 | tf_op jit(solution)/shard_map/ppermute | solution.py:52
  35.4 19.6 %collective-permute-start.12 = (bf16[128,1024]{1,0:T(8,128)(2,1)S(1)}, bf16[128,1024]{1,0:T(8,128)(2,1)S(1)}, u32[]{:S(2)}, u32[]{:S(2)}) collective-permute-start(bf16[128,1024]{1,0:T(8,128)(2,1)S(1)} %add.242.after_ref), channel_id=1, source_target_pairs={{0,2},{128,134},{2,4},{130,128},{4,6},{132,130},{6,0},{134,132},{1... | collective-permute-start | bytes 786440 | tf_op jit(solution)/shard_map/ppermute | solution.py:52
  43.1 11.8 %collective-permute-start.11 = (bf16[128,1024]{1,0:T(8,128)(2,1)S(1)}, bf16[128,1024]{1,0:T(8,128)(2,1)S(1)}, u32[]{:S(2)}, u32[]{:S(2)}) collective-permute-start(bf16[128,1024]{1,0:T(8,128)(2,1)S(1)} %add.244), channel_id=1, source_target_pairs={{0,2},{128,134},{2,4},{130,128},{4,6},{132,130},{6,0},{134,132},{1... | collective-permute-start | bytes 786440 | tf_op jit(solution)/shard_map/ppermute | solution.py:52
  51.0 8.9 %collective-permute-start.5 = (bf16[256,512]{1,0:T(8,128)(2,1)S(1)}, bf16[256,512]{1,0:T(8,128)(2,1)S(1)}, u32[]{:S(2)}, u32[]{:S(2)}) collective-permute-start(bf16[256,512]{1,0:T(8,128)(2,1)S(1)} %get-tuple-element.45), channel_id=1, source_target_pairs={{0,8},{1,9},{8,16},{9,17},{16,24},{17,25},{24,0},{25,1},{2,10},{3,... | collective-permute-start | bytes 786440 | tf_op jit(solution)/shard_map/ppermute | solution.py:44
  51.1 8.8 %collective-permute-start.6 = (bf16[256,512]{1,0:T(8,128)(2,1)S(1)}, bf16[256,512]{1,0:T(8,128)(2,1)S(1)}, u32[]{:S(2)}, u32[]{:S(2)}) collective-permute-start(bf16[256,512]{1,0:T(8,128)(2,1)S(1)} %get-tuple-element.46), channel_id=1, source_target_pairs={{0,24},{1,25},{8,0},{9,1},{16,8},{17,9},{24,16},{25,17},{2,26},{3,... | collective-permute-start | bytes 786440 | tf_op jit(solution)/shard_map/ppermute | solution.py:44
  69.4 12.3 %collective-permute-start.8 = (bf16[512,640]{1,0:T(8,128)(2,1)}, bf16[512,640]{1,0:T(8,128)(2,1)S(1)}, u32[]{:S(2)}, u32[]{:S(2)}) collective-permute-start(bf16[512,640]{1,0:T(8,128)(2,1)} %get-tuple-element.50), channel_id=1, source_target_pairs={{0,1},{1,0},{8,9},{9,8},{16,17},{17,16},{24,25},{25,24},{2,3},{3,2... | collective-permute-start | bytes 1966088 | tf_op jit(solution)/shard_map/ppermute | solution.py:44
  69.6 7.2 %collective-permute-start.20 = (bf16[128,640]{1,0:T(8,128)(2,1)S(1)}, bf16[128,640]{1,0:T(8,128)(2,1)S(1)}, u32[]{:S(2)}, u32[]{:S(2)}) collective-permute-start(bf16[128,640]{1,0:T(8,128)(2,1)S(1)} %add.245.refs_2_), channel_id=1, source_target_pairs={{0,2},{128,134},{2,4},{130,128},{4,6},{132,130},{6,0},{134,132},{1... | collective-permute-start | bytes 491528 | tf_op jit(solution)/shard_map/ppermute | solution.py:52
  76.9 11.3 %collective-permute-start.17 = (bf16[256,256]{1,0:T(8,128)(2,1)}, bf16[256,256]{1,0:T(8,128)(2,1)S(1)}, u32[]{:S(2)}, u32[]{:S(2)}) collective-permute-start(bf16[256,256]{1,0:T(8,128)(2,1)} %get-tuple-element.62), channel_id=1, source_target_pairs={{0,8},{1,9},{8,16},{9,17},{16,24},{17,25},{24,0},{25,1},{2,10},{3,... | collective-permute-start | bytes 393224 | tf_op jit(solution)/shard_map/ppermute | solution.py:44
  77.9 10.4 %collective-permute-start.18 = (bf16[256,256]{1,0:T(8,128)(2,1)}, bf16[256,256]{1,0:T(8,128)(2,1)S(1)}, u32[]{:S(2)}, u32[]{:S(2)}) collective-permute-start(bf16[256,256]{1,0:T(8,128)(2,1)} %get-tuple-element.63), channel_id=1, source_target_pairs={{0,16},{1,17},{8,24},{9,25},{16,0},{17,1},{24,8},{25,9},{2,18},{3,... | collective-permute-start | bytes 393224 | tf_op jit(solution)/shard_map/ppermute | solution.py:44
  81.1 7.2 %collective-permute-start.19 = (bf16[256,256]{1,0:T(8,128)(2,1)}, bf16[256,256]{1,0:T(8,128)(2,1)S(1)}, u32[]{:S(2)}, u32[]{:S(2)}) collective-permute-start(bf16[256,256]{1,0:T(8,128)(2,1)} %get-tuple-element.64), channel_id=1, source_target_pairs={{0,24},{1,25},{8,0},{9,1},{16,8},{17,9},{24,16},{25,17},{2,26},{3,... | collective-permute-start | bytes 393224 | tf_op jit(solution)/shard_map/ppermute | solution.py:44
  81.8 6.3 %collective-permute-start.14 = (bf16[128,640]{1,0:T(8,128)(2,1)S(1)}, bf16[128,640]{1,0:T(8,128)(2,1)S(1)}, u32[]{:S(2)}, u32[]{:S(2)}) collective-permute-start(bf16[128,640]{1,0:T(8,128)(2,1)S(1)} %add.246), channel_id=1, source_target_pairs={{0,2},{128,134},{2,4},{130,128},{4,6},{132,130},{6,0},{134,132},{1... | collective-permute-start | bytes 491528 | tf_op jit(solution)/shard_map/ppermute | solution.py:52
  83.0 7.7 %collective-permute-start.22 = (bf16[128,640]{1,0:T(8,128)(2,1)S(1)}, bf16[128,640]{1,0:T(8,128)(2,1)S(1)}, u32[]{:S(2)}, u32[]{:S(2)}) collective-permute-start(bf16[128,640]{1,0:T(8,128)(2,1)S(1)} %add.251), channel_id=1, source_target_pairs={{0,2},{128,134},{2,4},{130,128},{4,6},{132,130},{6,0},{134,132},{1... | collective-permute-start | bytes 491528 | tf_op jit(solution)/shard_map/ppermute | solution.py:52
  88.2 7.5 %collective-permute-start.15 = (bf16[128,640]{1,0:T(8,128)(2,1)S(1)}, bf16[128,640]{1,0:T(8,128)(2,1)S(1)}, u32[]{:S(2)}, u32[]{:S(2)}) collective-permute-start(bf16[128,640]{1,0:T(8,128)(2,1)S(1)} %add.247), channel_id=1, source_target_pairs={{0,2},{128,134},{2,4},{130,128},{4,6},{132,130},{6,0},{134,132},{1... | collective-permute-start | bytes 491528 | tf_op jit(solution)/shard_map/ppermute | solution.py:52
  90.8 12.4 %collective-permute-start.23 = (bf16[128,896]{1,0:T(8,128)(2,1)S(1)}, bf16[128,896]{1,0:T(8,128)(2,1)S(1)}, u32[]{:S(2)}, u32[]{:S(2)}) collective-permute-start(bf16[128,896]{1,0:T(8,128)(2,1)S(1)} %add.252), channel_id=1, source_target_pairs={{0,230},{2,228},{4,226},{6,224},{32,198},{34,196},{36,194},{38,192... | collective-permute-start | bytes 688136 | tf_op jit(solution)/shard_map/ppermute | solution.py:63
  95.8 7.3 %collective-permute-start.16 = (bf16[128,640]{1,0:T(8,128)(2,1)S(1)}, bf16[128,640]{1,0:T(8,128)(2,1)S(1)}, u32[]{:S(2)}, u32[]{:S(2)}) collective-permute-start(bf16[128,640]{1,0:T(8,128)(2,1)S(1)} %add.248), channel_id=1, source_target_pairs={{0,2},{128,134},{2,4},{130,128},{4,6},{132,130},{6,0},{134,132},{1... | collective-permute-start | bytes 491528 | tf_op jit(solution)/shard_map/ppermute | solution.py:52
  120.0 9.6 %collective-permute-start.24 = (bf16[4,32,896]{2,1,0:T(8,128)(2,1)S(1)}, bf16[4,32,896]{2,1,0:T(8,128)(2,1)S(1)}, u32[]{:S(2)}, u32[]{:S(2)}) collective-permute-start(bf16[4,32,896]{2,1,0:T(8,128)(2,1)S(1)} %get-tuple-element.75), channel_id=1, source_target_pairs={{0,1},{1,0},{8,9},{9,8},{16,17},{17,16},{24,25},{25,24},{2,3},{3,2... | collective-permute-start | bytes 688136 | tf_op jit(solution)/shard_map/ppermute | solution.py:44
  129.6 7.2 %collective-permute-start.25 = (bf16[2,32,896]{2,1,0:T(8,128)(2,1)S(1)}, bf16[2,32,896]{2,1,0:T(8,128)(2,1)S(1)}, u32[]{:S(2)}, u32[]{:S(2)}) collective-permute-start(bf16[2,32,896]{2,1,0:T(8,128)(2,1)S(1)} %get-tuple-element.73), channel_id=1, source_target_pairs={{0,8},{1,9},{8,16},{9,17},{16,24},{17,25},{24,0},{25,1},{2,10},{3,... | collective-permute-start | bytes 344072 | tf_op jit(solution)/shard_map/ppermute | solution.py:44
  129.7 10.4 %collective-permute-start.26 = (bf16[2,32,896]{2,1,0:T(8,128)(2,1)S(1)}, bf16[2,32,896]{2,1,0:T(8,128)(2,1)S(1)}, u32[]{:S(2)}, u32[]{:S(2)}) collective-permute-start(bf16[2,32,896]{2,1,0:T(8,128)(2,1)S(1)} %get-tuple-element.74), channel_id=1, source_target_pairs={{0,16},{1,17},{8,24},{9,25},{16,0},{17,1},{24,8},{25,9},{2,18},{3,... | collective-permute-start | bytes 344072 | tf_op jit(solution)/shard_map/ppermute | solution.py:44
  (20 other events, 152.4 us)

commit v3 on v2

--- a/solution.py
+++ b/solution.py
@@ -96,6 +96,14 @@
     live = live_ref[zh * 4 + x, (y * NZ + z) * NC + c]
     rank = jnp.where(zh == 0, z, NZ - 1 - z)
     keep = lax.broadcasted_iota(jnp.int32, (128, rows), 1) < live
+    pairs = [
+        (near_ref.at[0], up_hbm.at[:, width:]),
+        (near_ref.at[1], down_hbm.at[:, width:]),
+        (late_ref.at[1], swap_hbm.at[:, width:]),
+        (late_ref.at[0], late_hbm),
+    ]
+    pairs += [(turned_ref, out.at[:, :width]) for out in (up_hbm, down_hbm, swap_hbm, own_hbm)]
+    stores = [pltpu.make_async_copy(a, b, out_sem.at[i]) for i, (a, b) in enumerate(pairs)]
     for own in range(2):
         half = zh if own else 1 - zh
         for step in range(NZ):
@@ -106,12 +114,15 @@
             at = own * NZ + step
             down, across = slice(at % 2 * 128, (at % 2 + 1) * 128), at // 2 * rows
             turned_ref[down, across:across + rows] = turned
-    for copy in loads[2:]:
+        if own == 0:
+            for copy in loads[2:]:
+                copy.wait()
+            for copy in stores[:4]:
+                copy.start()
+    for copy in stores[4:]:
+        copy.start()
+    for copy in stores:
         copy.wait()
-    pairs = [(turned_ref, own_hbm), (late_ref.at[0], late_hbm)]
-    for out, grad in ((swap_hbm, late_ref.at[1]), (up_hbm, near_ref.at[0]), (down_hbm, near_ref.at[1])):
-        pairs += [(turned_ref, out.at[:, :width]), (grad, out.at[:, width:])]
-    run([pltpu.make_async_copy(a, b, out_sem.at[i]) for i, (a, b) in enumerate(pairs)])
 
 
 def prepare(live_tokens, hidden, grad):
@@ -365,7 +376,8 @@
     block = jnp.minimum(starts[:, None] + slot[None, :], hblk - 1)
     per = hblk // NZ
     chunk = block // per
-    chunk = jnp.where(lax.axis_index("zh") == 0, chunk, NZ - 1 - chunk)
+    rank = jnp.where(lax.axis_index("zh") == 0, z, NZ - 1 - z)
+    chunk = (rank + NZ - chunk) % NZ
     place = chunk * per + block % per
     rows = place[:, :, None] * BLK + jnp.arange(BLK, dtype=jnp.int32)
     rows = rows.reshape(-1)
@@ -413,7 +425,7 @@
                 after = [total]
         sums.append(total)
     tile = (sums[1] + send_mirror(sums[0]).astype(f32)).astype(bf16)
-    gathered = lax.all_gather(tile, "z", axis=0, tiled=True)
+    gathered = jnp.concatenate([tile] + [send_ring(tile, d) for d in range(1, NZ)], 0)
     picked = jnp.dot(choice, gathered, preferred_element_type=f32).astype(bf16)
     picked = picked.reshape(NY, NC, slots, COLS)
     both = jnp.stack([picked[:, 0], send_group(picked[:, 1], 0, 1)], 1)

time: 144 us -> 140 us (0.972)
  the two profiles are of different devices: /device:TPU:1 before, /device:TPU:48 now
where the time goes in v3:
time: 140 us
  waiting for transfers between devices  64.4 us (46%)
  starting transfers between devices  46.1 us (33%)
  Pallas kernels  22.3 us (16%)
  local copies, waits for them, and re-layouts  5.42 us (4%)
    ppermute x15, waiting for transfers between devices, send_ring(): return lax.ppermute(value, ('zh', 'z'), pairs)  34.7 us
    ppermute x15, starting transfers between devices, send_ring(): return lax.ppermute(value, ('zh', 'z'), pairs)  27 us
    ppermute x15, waiting for transfers between devices, send_group(): return lax.ppermute(value, ('y', 'c'), pairs)  22.5 us
    ppermute x15, starting transfers between devices, send_group(): return lax.ppermute(value, ('y', 'c'), pairs)  11.9 us
    ppermute x1, starting transfers between devices, send_mirror(): return lax.ppermute(value, ('zh', 'x', 'z'), pairs)  7.22 us
    ppermute x1, waiting for transfers between devices, send_mirror(): return lax.ppermute(value, ('zh', 'x', 'z'), pairs)  7.15 us
    pallas_call x2, Pallas kernels, product(): pl.pallas_call(functools.partial(product_kernel, part, len(after)), out_s...  6.55 us
    unnamed x28, local copies, waits for them, and re-layouts  5.19 us
  transfers between devices with their start and end apart: 31, of which 21 were waited for; matrix products, arithmetic and copies ran while one was open for 0% of the time, Pallas kernels for 9%

profile of v3, /device:TPU:48, one launch (start us, length us, event | category | flops | bytes accessed | tf_op | source)
XLA Modules:
  0.0 140.0 jit_solution(11149014423407173915)
XLA Ops:
  0.6 4.1 %prepare.1 = (bf16[256,1024]{1,0:T(8,128)(2,1)}, bf16[256,2304]{1,0:T(8,128)(2,1)}, bf16[256,2304]{1,0:T(8,128)(2,1)}, bf16[256,2048]{1,0:T(8,128)(2,1)}, bf16[256,1024]{1,0:T(8,128)(2,1)}) custom-call(s32[8,32]{1,0:T(8,128)} %live_hbm.1, bf16[256,1024]{1,0:T(8,128)(2,1)} %hidden_hbm.1, bf16[256,7168]{1,0:T(8,128)(2,1)} %grad_hbm.3), custom_call_target="tpu_custom_call" | custom-call | tf_op jit(solution)/shard_map/prepare/pallas_call | solution.py:132
  17.6 2.4 %pack.1 = (bf16[256,1280]{1,0:T(8,128)(2,1)}, bf16[256,1280]{1,0:T(8,128)(2,1)}) custom-call(bf16[256,7168]{1,0:T(8,128)(2,1)} %grad_hbm.3, bf16[256,1024]{1,0:T(8,128)(2,1)} %get-tuple-element.37.own_ref.after_ref.refs_0_), custom_call_target="tpu_custom_call" | custom-call | tf_op jit(solution)/shard_map/pack/pallas_call | solution.py:165
  20.9 2.3 %collective-permute-done.3.refs_1_ = bf16[128,1024]{1,0:T(8,128)(2,1)} collective-permute-done((bf16[128,1024]{1,0:T(8,128)(2,1)}, bf16[128,1024]{1,0:T(8,128)(2,1)}, u32[]{:S(2)}, u32[]{:S(2)}) %collective-permute-start.3) | collective-permute-done | bytes 262176 | tf_op jit(solution)/shard_map/ppermute | solution.py:52
  29.3 2.6 %collective-permute-start.10 = (bf16[128,1024]{1,0:T(8,128)(2,1)S(1)}, bf16[128,1024]{1,0:T(8,128)(2,1)S(1)}, u32[]{:S(2)}, u32[]{:S(2)}) collective-permute-start(bf16[128,1024]{1,0:T(8,128)(2,1)S(1)} %add.255), channel_id=1, source_target_pairs={{0,2},{128,134},{2,4},{130,128},{4,6},{132,130},{6,0},{134,132},{1... | collective-permute-start | bytes 786440 | tf_op jit(solution)/shard_map/ppermute | solution.py:52
  31.9 2.6 %collective-permute-done.4.refs_1_ = bf16[128,1024]{1,0:T(8,128)(2,1)S(1)} collective-permute-done((bf16[128,1024]{1,0:T(8,128)(2,1)S(1)}, bf16[128,1024]{1,0:T(8,128)(2,1)S(1)}, u32[]{:S(2)}, u32[]{:S(2)}) %collective-permute-start.4) | collective-permute-done | bytes 262176 | tf_op jit(solution)/shard_map/ppermute | solution.py:52
  36.6 3.5 %collective-permute-done.10.refs_1_ = bf16[128,1024]{1,0:T(8,128)(2,1)S(1)} collective-permute-done((bf16[128,1024]{1,0:T(8,128)(2,1)S(1)}, bf16[128,1024]{1,0:T(8,128)(2,1)S(1)}, u32[]{:S(2)}, u32[]{:S(2)}) %collective-permute-start.10) | collective-permute-done | bytes 262176 | tf_op jit(solution)/shard_map/ppermute | solution.py:52
  40.2 2.1 %collective-permute-start.11 = (bf16[128,1024]{1,0:T(8,128)(2,1)S(1)}, bf16[128,1024]{1,0:T(8,128)(2,1)S(1)}, u32[]{:S(2)}, u32[]{:S(2)}) collective-permute-start(bf16[128,1024]{1,0:T(8,128)(2,1)S(1)} %add.256), channel_id=1, source_target_pairs={{0,2},{128,134},{2,4},{130,128},{4,6},{132,130},{6,0},{134,132},{1... | collective-permute-start | bytes 786440 | tf_op jit(solution)/shard_map/ppermute | solution.py:52
  42.2 4.8 %collective-permute-done.up_ref.refs_1_.refs_6_ = bf16[256,2304]{1,0:T(8,128)(2,1)S(1)} collective-permute-done((bf16[256,2304]{1,0:T(8,128)(2,1)}, bf16[256,2304]{1,0:T(8,128)(2,1)S(1)}, u32[]{:S(2)}, u32[]{:S(2)}) %collective-permute-start) | collective-permute-done | bytes 1179680 | tf_op jit(solution)/shard_map/ppermute | solution.py:44
  48.1 2.6 %collective-permute-start.5 = (bf16[256,512]{1,0:T(8,128)(2,1)S(1)}, bf16[256,512]{1,0:T(8,128)(2,1)S(1)}, u32[]{:S(2)}, u32[]{:S(2)}) collective-permute-start(bf16[256,512]{1,0:T(8,128)(2,1)S(1)} %get-tuple-element.45), channel_id=1, source_target_pairs={{0,8},{1,9},{8,16},{9,17},{16,24},{17,25},{24,0},{25,1},{2,10},{3,... | collective-permute-start | bytes 786440 | tf_op jit(solution)/shard_map/ppermute | solution.py:44
  51.5 3.1 %collective-permute-done.5.refs_2_ = bf16[256,512]{1,0:T(8,128)(2,1)S(1)} collective-permute-done((bf16[256,512]{1,0:T(8,128)(2,1)S(1)}, bf16[256,512]{1,0:T(8,128)(2,1)S(1)}, u32[]{:S(2)}, u32[]{:S(2)}) %collective-permute-start.5) | collective-permute-done | bytes 262176 | tf_op jit(solution)/shard_map/ppermute | solution.py:44
  54.6 2.5 %collective-permute-done.6.refs_4_ = bf16[256,512]{1,0:T(8,128)(2,1)S(1)} collective-permute-done((bf16[256,512]{1,0:T(8,128)(2,1)S(1)}, bf16[256,512]{1,0:T(8,128)(2,1)S(1)}, u32[]{:S(2)}, u32[]{:S(2)}) %collective-permute-start.6) | collective-permute-done | bytes 262176 | tf_op jit(solution)/shard_map/ppermute | solution.py:44
  57.1 3.3 %product.3 = (bf16[128,640]{1,0:T(8,128)(2,1)S(1)}, bf16[128,640]{1,0:T(8,128)(2,1)S(1)}, bf16[128,640]{1,0:T(8,128)(2,1)S(1)}, bf16[128,640]{1,0:T(8,128)(2,1)S(1)}, bf16[512,640]{1,0:T(8,128)(2,1)S(1)}) custom-call(bf16[256,1024]{1,0:T(8,128)(2,1)S(1)} %copy-done.1, bf16[256,2304]{1,0:T(8,128)(2,1)S(1)} %collective-permute-done.up_ref.refs_1_.refs_6_, ...), custom_call_target="tpu_custom_call" | custom-call | flops 1342177280 | bytes 4980736 | tf_op jit(solution)/shard_map/product/pallas_call | solution.py:285
  60.5 3.3 %product.2 = (bf16[128,640]{1,0:T(8,128)(2,1)S(1)}, bf16[128,640]{1,0:T(8,128)(2,1)S(1)}, bf16[128,640]{1,0:T(8,128)(2,1)S(1)}, bf16[128,640]{1,0:T(8,128)(2,1)S(1)}, bf16[512,640]{1,0:T(8,128)(2,1)S(1)}) custom-call(bf16[256,1024]{1,0:T(8,128)(2,1)S(1)} %copy-done.1, bf16[256,2304]{1,0:T(8,128)(2,1)S(1)} %collective-permute-done.up_ref.refs_1_.refs_6_, ...), custom_call_target="tpu_custom_call" | custom-call | flops 1342177280 | bytes 4980736 | tf_op jit(solution)/shard_map/product/pallas_call | solution.py:285
  68.4 4.2 %collective-permute-done.20.refs_2_ = bf16[128,640]{1,0:T(8,128)(2,1)S(1)} collective-permute-done((bf16[128,640]{1,0:T(8,128)(2,1)S(1)}, bf16[128,640]{1,0:T(8,128)(2,1)S(1)}, u32[]{:S(2)}, u32[]{:S(2)}) %collective-permute-start.20) | collective-permute-done | bytes 163872 | tf_op jit(solution)/shard_map/ppermute | solution.py:52
  77.1 3.5 %collective-permute-done.21.refs_2_ = bf16[128,640]{1,0:T(8,128)(2,1)S(1)} collective-permute-done((bf16[128,640]{1,0:T(8,128)(2,1)S(1)}, bf16[128,640]{1,0:T(8,128)(2,1)S(1)}, u32[]{:S(2)}, u32[]{:S(2)}) %collective-permute-start.21) | collective-permute-done | bytes 163872 | tf_op jit(solution)/shard_map/ppermute | solution.py:52
  84.3 2.5 %collective-permute-start.16 = (bf16[128,640]{1,0:T(8,128)(2,1)S(1)}, bf16[128,640]{1,0:T(8,128)(2,1)S(1)}, u32[]{:S(2)}, u32[]{:S(2)}) collective-permute-start(bf16[128,640]{1,0:T(8,128)(2,1)S(1)} %add.260), channel_id=1, source_target_pairs={{0,2},{128,134},{2,4},{130,128},{4,6},{132,130},{6,0},{134,132},{1... | collective-permute-start | bytes 491528 | tf_op jit(solution)/shard_map/ppermute | solution.py:52
  86.9 2.1 %collective-permute-done.18.refs_5_ = bf16[256,256]{1,0:T(8,128)(2,1)S(1)} collective-permute-done((bf16[256,256]{1,0:T(8,128)(2,1)S(1)}, bf16[256,256]{1,0:T(8,128)(2,1)S(1)}, u32[]{:S(2)}, u32[]{:S(2)}) %collective-permute-start.18) | collective-permute-done | bytes 131104 | tf_op jit(solution)/shard_map/ppermute | solution.py:44
  89.4 7.2 %collective-permute-start.23 = (bf16[128,896]{1,0:T(8,128)(2,1)S(1)}, bf16[128,896]{1,0:T(8,128)(2,1)S(1)}, u32[]{:S(2)}, u32[]{:S(2)}) collective-permute-start(bf16[128,896]{1,0:T(8,128)(2,1)S(1)} %add.264), channel_id=1, source_target_pairs={{0,230},{2,228},{4,226},{6,224},{32,198},{34,196},{36,194},{38,192... | collective-permute-start | bytes 688136 | tf_op jit(solution)/shard_map/ppermute | solution.py:63
  97.0 7.2 %collective-permute-done.23 = bf16[128,896]{1,0:T(8,128)(2,1)S(1)} collective-permute-done((bf16[128,896]{1,0:T(8,128)(2,1)S(1)}, bf16[128,896]{1,0:T(8,128)(2,1)S(1)}, u32[]{:S(2)}, u32[]{:S(2)}) %collective-permute-start.23) | collective-permute-done | bytes 229408 | tf_op jit(solution)/shard_map/ppermute | solution.py:63
  104.5 4.9 %collective-permute-start.25 = (bf16[128,896]{1,0:T(8,128)(2,1)S(1)}, bf16[128,896]{1,0:T(8,128)(2,1)S(1)}, u32[]{:S(2)}, u32[]{:S(2)}) collective-permute-start(bf16[128,896]{1,0:T(8,128)(2,1)S(1)} %add_convert_fusion), channel_id=1, source_target_pairs={{0,4},{128,132},{2,6},{130,134},{4,0},{132,128},{6,2},{134,130},{1... | collective-permute-start | bytes 688136 | tf_op jit(solution)/shard_map/ppermute | solution.py:52
  109.7 3.9 %collective-permute-done.24 = bf16[128,896]{1,0:T(8,128)(2,1)S(1)} collective-permute-done((bf16[128,896]{1,0:T(8,128)(2,1)S(1)}, bf16[128,896]{1,0:T(8,128)(2,1)S(1)}, u32[]{:S(2)}, u32[]{:S(2)}) %collective-permute-start.24) | collective-permute-done | bytes 229408 | tf_op jit(solution)/shard_map/ppermute | solution.py:52
  113.6 10.9 %collective-permute-done.25 = bf16[128,896]{1,0:T(8,128)(2,1)S(1)} collective-permute-done((bf16[128,896]{1,0:T(8,128)(2,1)S(1)}, bf16[128,896]{1,0:T(8,128)(2,1)S(1)}, u32[]{:S(2)}, u32[]{:S(2)}) %collective-permute-start.25) | collective-permute-done | bytes 229408 | tf_op jit(solution)/shard_map/ppermute | solution.py:52
  129.7 5.6 %collective-permute-done.28.refs_2_ = bf16[2,32,896]{2,1,0:T(8,128)(2,1)S(1)} collective-permute-done((bf16[2,32,896]{2,1,0:T(8,128)(2,1)S(1)}, bf16[2,32,896]{2,1,0:T(8,128)(2,1)S(1)}, u32[]{:S(2)}, u32[]{:S(2)}) %collective-permute-start.28) | collective-permute-done | bytes 114720 | tf_op jit(solution)/shard_map/ppermute | solution.py:44
  137.1 3.0 %adamw.1 = (f32[32,7168]{1,0:T(8,128)}, bf16[32,7168]{1,0:T(8,128)(2,1)}, bf16[32,7168]{1,0:T(8,128)(2,1)}) custom-call(s32[8,32]{1,0:T(8,128)S(1)} %copy-done.13, bf16[2,32,896]{2,1,0:T(8,128)(2,1)S(1)} %get-tuple-element.72.refs_1_, bf16[2,32,896]{2,1,0:T(8,128)(2,1)S(1)} %collective-permute-done.28.refs_2_, ...), custom_call_target="tpu_custom_call" | custom-call | tf_op jit(solution)/shard_map/adamw/pallas_call | solution.py:356
  (96 shorter events, 45.1 us)
Async XLA Ops:
  4.8 42.2 %collective-permute-start = (bf16[256,2304]{1,0:T(8,128)(2,1)}, bf16[256,2304]{1,0:T(8,128)(2,1)S(1)}, u32[]{:S(2)}, u32[]{:S(2)}) collective-permute-start(bf16[256,2304]{1,0:T(8,128)(2,1)} %get-tuple-element.38), channel_id=1, source_target_pairs={{0,8},{1,9},{8,16},{9,17},{16,24},{17,25},{24,0},{25,1},{2,10},{3,... | collective-permute-start | bytes 3538952 | tf_op jit(solution)/shard_map/ppermute | solution.py:44
  6.2 40.9 %collective-permute-start.1 = (bf16[256,2304]{1,0:T(8,128)(2,1)}, bf16[256,2304]{1,0:T(8,128)(2,1)}, u32[]{:S(2)}, u32[]{:S(2)}) collective-permute-start(bf16[256,2304]{1,0:T(8,128)(2,1)} %get-tuple-element.39), channel_id=1, source_target_pairs={{0,24},{1,25},{8,0},{9,1},{16,8},{17,9},{24,16},{25,17},{2,26},{3,... | collective-permute-start | bytes 3538952 | tf_op jit(solution)/shard_map/ppermute | solution.py:44
  13.8 9.5 %collective-permute-start.3 = (bf16[128,1024]{1,0:T(8,128)(2,1)}, bf16[128,1024]{1,0:T(8,128)(2,1)}, u32[]{:S(2)}, u32[]{:S(2)}) collective-permute-start(bf16[128,1024]{1,0:T(8,128)(2,1)} %get-tuple-element.44), channel_id=1, source_target_pairs={{0,2},{128,134},{2,4},{130,128},{4,6},{132,130},{6,0},{134,132},{1... | collective-permute-start | bytes 786440 | tf_op jit(solution)/shard_map/ppermute | solution.py:52
  15.7 12.6 %collective-permute-start.9 = (bf16[128,1024]{1,0:T(8,128)(2,1)}, bf16[128,1024]{1,0:T(8,128)(2,1)}, u32[]{:S(2)}, u32[]{:S(2)}) collective-permute-start(bf16[128,1024]{1,0:T(8,128)(2,1)} %get-tuple-element.57), channel_id=1, source_target_pairs={{0,2},{128,134},{2,4},{130,128},{4,6},{132,130},{6,0},{134,132},{1... | collective-permute-start | bytes 786440 | tf_op jit(solution)/shard_map/ppermute | solution.py:52
  20.0 31.4 %collective-permute-start.7 = (bf16[256,1280]{1,0:T(8,128)(2,1)}, bf16[256,1280]{1,0:T(8,128)(2,1)S(1)}, u32[]{:S(2)}, u32[]{:S(2)}) collective-permute-start(bf16[256,1280]{1,0:T(8,128)(2,1)} %get-tuple-element.48), channel_id=1, source_target_pairs={{0,16},{1,17},{8,24},{9,25},{16,0},{17,1},{24,8},{25,9},{2,18},{3,... | collective-permute-start | bytes 1966088 | tf_op jit(solution)/shard_map/ppermute | solution.py:44
  25.2 9.2 %collective-permute-start.4 = (bf16[128,1024]{1,0:T(8,128)(2,1)S(1)}, bf16[128,1024]{1,0:T(8,128)(2,1)S(1)}, u32[]{:S(2)}, u32[]{:S(2)}) collective-permute-start(bf16[128,1024]{1,0:T(8,128)(2,1)S(1)} %add.253), channel_id=1, source_target_pairs={{0,2},{128,134},{2,4},{130,128},{4,6},{132,130},{6,0},{134,132},{1... | collective-permute-start | bytes 786440 | tf_op jit(solution)/shard_map/ppermute | solution.py:52
  29.3 10.8 %collective-permute-start.10 = (bf16[128,1024]{1,0:T(8,128)(2,1)S(1)}, bf16[128,1024]{1,0:T(8,128)(2,1)S(1)}, u32[]{:S(2)}, u32[]{:S(2)}) collective-permute-start(bf16[128,1024]{1,0:T(8,128)(2,1)S(1)} %add.255), channel_id=1, source_target_pairs={{0,2},{128,134},{2,4},{130,128},{4,6},{132,130},{6,0},{134,132},{1... | collective-permute-start | bytes 786440 | tf_op jit(solution)/shard_map/ppermute | solution.py:52
  34.5 16.2 %collective-permute-start.12 = (bf16[128,1024]{1,0:T(8,128)(2,1)S(1)}, bf16[128,1024]{1,0:T(8,128)(2,1)S(1)}, u32[]{:S(2)}, u32[]{:S(2)}) collective-permute-start(bf16[128,1024]{1,0:T(8,128)(2,1)S(1)} %add.254.after_ref), channel_id=1, source_target_pairs={{0,2},{128,134},{2,4},{130,128},{4,6},{132,130},{6,0},{134,132},{1... | collective-permute-start | bytes 786440 | tf_op jit(solution)/shard_map/ppermute | solution.py:52
  40.2 10.5 %collective-permute-start.11 = (bf16[128,1024]{1,0:T(8,128)(2,1)S(1)}, bf16[128,1024]{1,0:T(8,128)(2,1)S(1)}, u32[]{:S(2)}, u32[]{:S(2)}) collective-permute-start(bf16[128,1024]{1,0:T(8,128)(2,1)S(1)} %add.256), channel_id=1, source_target_pairs={{0,2},{128,134},{2,4},{130,128},{4,6},{132,130},{6,0},{134,132},{1... | collective-permute-start | bytes 786440 | tf_op jit(solution)/shard_map/ppermute | solution.py:52
  48.1 6.5 %collective-permute-start.5 = (bf16[256,512]{1,0:T(8,128)(2,1)S(1)}, bf16[256,512]{1,0:T(8,128)(2,1)S(1)}, u32[]{:S(2)}, u32[]{:S(2)}) collective-permute-start(bf16[256,512]{1,0:T(8,128)(2,1)S(1)} %get-tuple-element.45), channel_id=1, source_target_pairs={{0,8},{1,9},{8,16},{9,17},{16,24},{17,25},{24,0},{25,1},{2,10},{3,... | collective-permute-start | bytes 786440 | tf_op jit(solution)/shard_map/ppermute | solution.py:44
  64.4 8.2 %collective-permute-start.20 = (bf16[128,640]{1,0:T(8,128)(2,1)S(1)}, bf16[128,640]{1,0:T(8,128)(2,1)S(1)}, u32[]{:S(2)}, u32[]{:S(2)}) collective-permute-start(bf16[128,640]{1,0:T(8,128)(2,1)S(1)} %add.257.refs_2_), channel_id=1, source_target_pairs={{0,2},{128,134},{2,4},{130,128},{4,6},{132,130},{6,0},{134,132},{1... | collective-permute-start | bytes 491528 | tf_op jit(solution)/shard_map/ppermute | solution.py:52
  66.4 9.1 %collective-permute-start.14 = (bf16[128,640]{1,0:T(8,128)(2,1)S(1)}, bf16[128,640]{1,0:T(8,128)(2,1)S(1)}, u32[]{:S(2)}, u32[]{:S(2)}) collective-permute-start(bf16[128,640]{1,0:T(8,128)(2,1)S(1)} %add.258), channel_id=1, source_target_pairs={{0,2},{128,134},{2,4},{130,128},{4,6},{132,130},{6,0},{134,132},{1... | collective-permute-start | bytes 491528 | tf_op jit(solution)/shard_map/ppermute | solution.py:52
  72.6 7.9 %collective-permute-start.21 = (bf16[128,640]{1,0:T(8,128)(2,1)S(1)}, bf16[128,640]{1,0:T(8,128)(2,1)S(1)}, u32[]{:S(2)}, u32[]{:S(2)}) collective-permute-start(bf16[128,640]{1,0:T(8,128)(2,1)S(1)} %add.262), channel_id=1, source_target_pairs={{0,2},{128,134},{2,4},{130,128},{4,6},{132,130},{6,0},{134,132},{1... | collective-permute-start | bytes 491528 | tf_op jit(solution)/shard_map/ppermute | solution.py:52
  75.5 8.7 %collective-permute-start.15 = (bf16[128,640]{1,0:T(8,128)(2,1)S(1)}, bf16[128,640]{1,0:T(8,128)(2,1)S(1)}, u32[]{:S(2)}, u32[]{:S(2)}) collective-permute-start(bf16[128,640]{1,0:T(8,128)(2,1)S(1)} %add.259), channel_id=1, source_target_pairs={{0,2},{128,134},{2,4},{130,128},{4,6},{132,130},{6,0},{134,132},{1... | collective-permute-start | bytes 491528 | tf_op jit(solution)/shard_map/ppermute | solution.py:52
  80.6 8.7 %collective-permute-start.22 = (bf16[128,640]{1,0:T(8,128)(2,1)S(1)}, bf16[128,640]{1,0:T(8,128)(2,1)S(1)}, u32[]{:S(2)}, u32[]{:S(2)}) collective-permute-start(bf16[128,640]{1,0:T(8,128)(2,1)S(1)} %add.263), channel_id=1, source_target_pairs={{0,2},{128,134},{2,4},{130,128},{4,6},{132,130},{6,0},{134,132},{1... | collective-permute-start | bytes 491528 | tf_op jit(solution)/shard_map/ppermute | solution.py:52
  82.6 6.8 %collective-permute-start.19 = (bf16[256,256]{1,0:T(8,128)(2,1)S(1)}, bf16[256,256]{1,0:T(8,128)(2,1)S(1)}, u32[]{:S(2)}, u32[]{:S(2)}) collective-permute-start(bf16[256,256]{1,0:T(8,128)(2,1)S(1)} %get-tuple-element.64), channel_id=1, source_target_pairs={{0,24},{1,25},{8,0},{9,1},{16,8},{17,9},{24,16},{25,17},{2,26},{3,... | collective-permute-start | bytes 393224 | tf_op jit(solution)/shard_map/ppermute | solution.py:44
  84.3 12.6 %collective-permute-start.16 = (bf16[128,640]{1,0:T(8,128)(2,1)S(1)}, bf16[128,640]{1,0:T(8,128)(2,1)S(1)}, u32[]{:S(2)}, u32[]{:S(2)}) collective-permute-start(bf16[128,640]{1,0:T(8,128)(2,1)S(1)} %add.260), channel_id=1, source_target_pairs={{0,2},{128,134},{2,4},{130,128},{4,6},{132,130},{6,0},{134,132},{1... | collective-permute-start | bytes 491528 | tf_op jit(solution)/shard_map/ppermute | solution.py:52
  89.4 14.8 %collective-permute-start.23 = (bf16[128,896]{1,0:T(8,128)(2,1)S(1)}, bf16[128,896]{1,0:T(8,128)(2,1)S(1)}, u32[]{:S(2)}, u32[]{:S(2)}) collective-permute-start(bf16[128,896]{1,0:T(8,128)(2,1)S(1)} %add.264), channel_id=1, source_target_pairs={{0,230},{2,228},{4,226},{6,224},{32,198},{34,196},{36,194},{38,192... | collective-permute-start | bytes 688136 | tf_op jit(solution)/shard_map/ppermute | solution.py:63
  104.2 9.4 %collective-permute-start.24 = (bf16[128,896]{1,0:T(8,128)(2,1)S(1)}, bf16[128,896]{1,0:T(8,128)(2,1)S(1)}, u32[]{:S(2)}, u32[]{:S(2)}) collective-permute-start(bf16[128,896]{1,0:T(8,128)(2,1)S(1)} %add_convert_fusion), channel_id=1, source_target_pairs={{0,2},{128,134},{2,4},{130,128},{4,6},{132,130},{6,0},{134,132},{1... | collective-permute-start | bytes 688136 | tf_op jit(solution)/shard_map/ppermute | solution.py:52
  104.5 20.0 %collective-permute-start.25 = (bf16[128,896]{1,0:T(8,128)(2,1)S(1)}, bf16[128,896]{1,0:T(8,128)(2,1)S(1)}, u32[]{:S(2)}, u32[]{:S(2)}) collective-permute-start(bf16[128,896]{1,0:T(8,128)(2,1)S(1)} %add_convert_fusion), channel_id=1, source_target_pairs={{0,4},{128,132},{2,6},{130,134},{4,0},{132,128},{6,2},{134,130},{1... | collective-permute-start | bytes 688136 | tf_op jit(solution)/shard_map/ppermute | solution.py:52
  109.5 15.8 %collective-permute-start.26 = (bf16[128,896]{1,0:T(8,128)(2,1)S(1)}, bf16[128,896]{1,0:T(8,128)(2,1)S(1)}, u32[]{:S(2)}, u32[]{:S(2)}) collective-permute-start(bf16[128,896]{1,0:T(8,128)(2,1)S(1)} %add_convert_fusion), channel_id=1, source_target_pairs={{0,6},{128,130},{2,0},{130,132},{4,2},{132,134},{6,4},{134,128},{1... | collective-permute-start | bytes 688136 | tf_op jit(solution)/shard_map/ppermute | solution.py:52
  127.5 7.7 %collective-permute-start.28 = (bf16[2,32,896]{2,1,0:T(8,128)(2,1)S(1)}, bf16[2,32,896]{2,1,0:T(8,128)(2,1)S(1)}, u32[]{:S(2)}, u32[]{:S(2)}) collective-permute-start(bf16[2,32,896]{2,1,0:T(8,128)(2,1)S(1)} %get-tuple-element.73), channel_id=1, source_target_pairs={{0,8},{1,9},{8,16},{9,17},{16,24},{17,25},{24,0},{25,1},{2,10},{3,... | collective-permute-start | bytes 344072 | tf_op jit(solution)/shard_map/ppermute | solution.py:44
  128.1 7.1 %collective-permute-start.29 = (bf16[2,32,896]{2,1,0:T(8,128)(2,1)S(1)}, bf16[2,32,896]{2,1,0:T(8,128)(2,1)S(1)}, u32[]{:S(2)}, u32[]{:S(2)}) collective-permute-start(bf16[2,32,896]{2,1,0:T(8,128)(2,1)S(1)} %get-tuple-element.74), channel_id=1, source_target_pairs={{0,16},{1,17},{8,24},{9,25},{16,0},{17,1},{24,8},{25,9},{2,18},{3,... | collective-permute-start | bytes 344072 | tf_op jit(solution)/shard_map/ppermute | solution.py:44
  128.1 9.0 %collective-permute-start.30 = (bf16[2,32,896]{2,1,0:T(8,128)(2,1)S(1)}, bf16[2,32,896]{2,1,0:T(8,128)(2,1)S(1)}, u32[]{:S(2)}, u32[]{:S(2)}) collective-permute-start(bf16[2,32,896]{2,1,0:T(8,128)(2,1)S(1)} %get-tuple-element.71), channel_id=1, source_target_pairs={{0,24},{1,25},{8,0},{9,1},{16,8},{17,9},{24,16},{25,17},{2,26},{3,... | collective-permute-start | bytes 344072 | tf_op jit(solution)/shard_map/ppermute | solution.py:44
  (21 other events, 151.3 us)

commit v4 on v3

--- a/solution.py
+++ b/solution.py
@@ -50,6 +50,13 @@
         pairs.append((z, (z + steps) % NZ))
         pairs.append((NZ + z, NZ + (z + NZ - steps) % NZ))
     return lax.ppermute(value, ("zh", "z"), pairs)
+
+
+def gather(tile):
+    half = tile.shape[0] // 2
+    up, down = send_ring(tile, 1), send_ring(tile, NZ - 1)
+    far = jnp.concatenate([send_ring(up[:half], 1), send_ring(down[half:], NZ - 1)], 0)
+    return jnp.concatenate([tile, up, far, down], 0)
 
 
 def send_mirror(value):
@@ -258,23 +265,34 @@
     outs, other_ref, (left, right, sem) = refs[:NZ], refs[NZ], refs[NZ + 1:]
     depth, width = hidden[0].shape
     rows, lead = outs[0].shape[0], part * width // 2
-    pairs = []
+    first, second = [], []
     for dy in range(NY):
         if dy == 2:
             piece = hidden[NY] if part else hidden[2]
         else:
             piece = hidden[dy].at[:, lead:lead + width // 2]
-        pairs.append((piece, left.at[dy]))
-        first = grads[dy].shape[1] - NC * EARLY
-        pairs.append((grads[dy].at[:, first:], right.at[dy * depth:(dy + 1) * depth, :]))
-    run([pltpu.make_async_copy(a, b, sem.at[i]) for i, (a, b) in enumerate(pairs)])
+        first.append((piece, left.at[dy]))
+        start = grads[dy].shape[1] - NC * EARLY
+        rows_of = right.at[dy * depth:(dy + 1) * depth]
+        first.append((grads[dy].at[:, start + EARLY:], rows_of.at[:, EARLY:]))
+        second.append((grads[dy].at[:, start:start + EARLY], rows_of.at[:, :EARLY]))
+    copies = [pltpu.make_async_copy(a, b, sem.at[i]) for i, (a, b) in enumerate(first + second)]
+    for copy in copies:
+        copy.start()
+    for copy in copies[:2 * NY]:
+        copy.wait()
+    blocks = []
     for pair in range(NZ // 2):
         at = slice(pair * depth, (pair + 1) * depth)
-        block = jnp.concatenate([left[i, :, at] for i in range(NY)], 1)
-        total = jnp.dot(block, right[...], preferred_element_type=f32)
+        blocks.append(jnp.concatenate([left[i, :, at] for i in range(NY)], 1))
+        total = jnp.dot(blocks[pair], right[:, EARLY:], preferred_element_type=f32)
+        other_ref[pair * 2 * rows:(pair + 1) * 2 * rows, :] = total.astype(bf16)
+    for copy in copies[2 * NY:]:
+        copy.wait()
+    for pair in range(NZ // 2):
+        total = jnp.dot(blocks[pair], right[:, :EARLY], preferred_element_type=f32)
         for i in range(2):
-            outs[pair * 2 + i][...] = total[i * rows:(i + 1) * rows, :EARLY].astype(bf16)
-        other_ref[pair * 2 * rows:(pair + 1) * 2 * rows, :] = total[:, EARLY:].astype(bf16)
+            outs[pair * 2 + i][...] = total[i * rows:(i + 1) * rows].astype(bf16)
 
 
 def product(part, hidden, grads, after):
@@ -290,7 +308,7 @@
         scratch_shapes=[
             pltpu.VMEM((NY, tokens, width // 2), bf16),
             pltpu.VMEM((depth, NC * EARLY), bf16),
-            pltpu.SemaphoreType.DMA((2 * NY,)),
+            pltpu.SemaphoreType.DMA((3 * NY,)),
         ],
         compiler_params=PARAMS,
         cost_estimate=pl.CostEstimate(
@@ -417,7 +435,7 @@
         for step in range(NZ):
             terms = [(parts[step], 0), (sibling, step * 128)] + moved
             if step < NZ - 1:
-                total = add(terms, bf16, after if part and not step else ())
+                total = add(terms, bf16)
                 moved = [(send_ring(total, 1), 0)]
             else:
                 total = add(terms, f32 if part else bf16, (), late, part * 128)
@@ -425,7 +443,7 @@
                 after = [total]
         sums.append(total)
     tile = (sums[1] + send_mirror(sums[0]).astype(f32)).astype(bf16)
-    gathered = jnp.concatenate([tile] + [send_ring(tile, d) for d in range(1, NZ)], 0)
+    gathered = gather(tile)
     picked = jnp.dot(choice, gathered, preferred_element_type=f32).astype(bf16)
     picked = picked.reshape(NY, NC, slots, COLS)
     both = jnp.stack([picked[:, 0], send_group(picked[:, 1], 0, 1)], 1)

time: 140 us -> 140 us (level)
  the two profiles are of different devices: /device:TPU:48 before, /device:TPU:1 now
where the time goes in v4:
time: 140 us
  waiting for transfers between devices  63.3 us (45%)
  starting transfers between devices  46.6 us (33%)
  Pallas kernels  22.3 us (16%)
  local copies, waits for them, and re-layouts  5.52 us (4%)
    ppermute x16, waiting for transfers between devices, send_ring(): return lax.ppermute(value, ('zh', 'z'), pairs)  36.5 us
    ppermute x15, starting transfers between devices, send_group(): return lax.ppermute(value, ('y', 'c'), pairs)  33.2 us
    ppermute x15, waiting for transfers between devices, send_group(): return lax.ppermute(value, ('y', 'c'), pairs)  20.4 us
    ppermute x16, starting transfers between devices, send_ring(): return lax.ppermute(value, ('zh', 'z'), pairs)  8.59 us
    pallas_call x2, Pallas kernels, product(): pl.pallas_call(functools.partial(product_kernel, part, len(after)), out_s...  6.56 us
    ppermute x1, waiting for transfers between devices, send_mirror(): return lax.ppermute(value, ('zh', 'x', 'z'), pairs)  6.36 us
    unnamed x31, local copies, waits for them, and re-layouts  5.24 us
    ppermute x1, starting transfers between devices, send_mirror(): return lax.ppermute(value, ('zh', 'x', 'z'), pairs)  4.78 us
  transfers between devices with their start and end apart: 32, of which 21 were waited for; matrix products, arithmetic and copies ran while one was open for 0% of the time, Pallas kernels for 9%

profile of v4, /device:TPU:1, one launch (start us, length us, event | category | flops | bytes accessed | tf_op | source)
XLA Modules:
  0.0 139.7 jit_solution(7445406921009653043)
XLA Ops:
  0.6 4.1 %prepare.1 = (bf16[256,1024]{1,0:T(8,128)(2,1)}, bf16[256,2304]{1,0:T(8,128)(2,1)}, bf16[256,2304]{1,0:T(8,128)(2,1)}, bf16[256,2048]{1,0:T(8,128)(2,1)}, bf16[256,1024]{1,0:T(8,128)(2,1)}) custom-call(s32[8,32]{1,0:T(8,128)} %live_hbm.1, bf16[256,1024]{1,0:T(8,128)(2,1)} %hidden_hbm.1, bf16[256,7168]{1,0:T(8,128)(2,1)} %grad_hbm.3), custom_call_target="tpu_custom_call" | custom-call | tf_op jit(solution)/shard_map/prepare/pallas_call | solution.py:139
  4.7 3.3 %collective-permute-start.2 = (bf16[256,2048]{1,0:T(8,128)(2,1)}, bf16[256,2048]{1,0:T(8,128)(2,1)S(1)}, u32[]{:S(2)}, u32[]{:S(2)}) collective-permute-start(bf16[256,2048]{1,0:T(8,128)(2,1)} %get-tuple-element.41), channel_id=1, source_target_pairs={{0,1},{1,0},{8,9},{9,8},{16,17},{17,16},{24,25},{25,24},{2,3},{3,2... | collective-permute-start | bytes 3145736 | tf_op jit(solution)/shard_map/ppermute | solution.py:44
  8.1 2.7 %collective-permute-start.1 = (bf16[256,2304]{1,0:T(8,128)(2,1)}, bf16[256,2304]{1,0:T(8,128)(2,1)}, u32[]{:S(2)}, u32[]{:S(2)}) collective-permute-start(bf16[256,2304]{1,0:T(8,128)(2,1)} %get-tuple-element.39), channel_id=1, source_target_pairs={{0,24},{1,25},{8,0},{9,1},{16,8},{17,9},{24,16},{25,17},{2,26},{3,... | collective-permute-start | bytes 3538952 | tf_op jit(solution)/shard_map/ppermute | solution.py:44
  20.8 2.8 %collective-permute-start.7 = (bf16[256,1280]{1,0:T(8,128)(2,1)}, bf16[256,1280]{1,0:T(8,128)(2,1)S(1)}, u32[]{:S(2)}, u32[]{:S(2)}) collective-permute-start(bf16[256,1280]{1,0:T(8,128)(2,1)} %get-tuple-element.48), channel_id=1, source_target_pairs={{0,16},{1,17},{8,24},{9,25},{16,0},{17,1},{24,8},{25,9},{2,18},{3,... | collective-permute-start | bytes 1966088 | tf_op jit(solution)/shard_map/ppermute | solution.py:44
  28.2 3.6 %collective-permute-done.12.refs_1_ = bf16[128,1024]{1,0:T(8,128)(2,1)} collective-permute-done((bf16[128,1024]{1,0:T(8,128)(2,1)}, bf16[128,1024]{1,0:T(8,128)(2,1)}, u32[]{:S(2)}, u32[]{:S(2)}) %collective-permute-start.12) | collective-permute-done | bytes 262176 | tf_op jit(solution)/shard_map/ppermute | solution.py:52
  35.5 7.6 %collective-permute-done.13.refs_1_ = bf16[128,1024]{1,0:T(8,128)(2,1)S(1)} collective-permute-done((bf16[128,1024]{1,0:T(8,128)(2,1)S(1)}, bf16[128,1024]{1,0:T(8,128)(2,1)S(1)}, u32[]{:S(2)}, u32[]{:S(2)}) %collective-permute-start.13) | collective-permute-done | bytes 262176 | tf_op jit(solution)/shard_map/ppermute | solution.py:52
  43.3 6.7 %collective-permute-done.1.down_ref.refs_3_.refs_8_ = bf16[256,2304]{1,0:T(8,128)(2,1)} collective-permute-done((bf16[256,2304]{1,0:T(8,128)(2,1)}, bf16[256,2304]{1,0:T(8,128)(2,1)}, u32[]{:S(2)}, u32[]{:S(2)}) %collective-permute-start.1) | collective-permute-done | bytes 1179680 | tf_op jit(solution)/shard_map/ppermute | solution.py:44
  51.1 3.8 %collective-permute-start.6 = (bf16[256,512]{1,0:T(8,128)(2,1)S(1)}, bf16[256,512]{1,0:T(8,128)(2,1)S(1)}, u32[]{:S(2)}, u32[]{:S(2)}) collective-permute-start(bf16[256,512]{1,0:T(8,128)(2,1)S(1)} %get-tuple-element.46), channel_id=1, source_target_pairs={{0,24},{1,25},{8,0},{9,1},{16,8},{17,9},{24,16},{25,17},{2,26},{3,... | collective-permute-start | bytes 786440 | tf_op jit(solution)/shard_map/ppermute | solution.py:44
  55.7 4.2 %collective-permute-done.5.refs_2_ = bf16[256,512]{1,0:T(8,128)(2,1)S(1)} collective-permute-done((bf16[256,512]{1,0:T(8,128)(2,1)S(1)}, bf16[256,512]{1,0:T(8,128)(2,1)S(1)}, u32[]{:S(2)}, u32[]{:S(2)}) %collective-permute-start.5) | collective-permute-done | bytes 262176 | tf_op jit(solution)/shard_map/ppermute | solution.py:44
  60.0 3.3 %product.3 = (bf16[128,640]{1,0:T(8,128)(2,1)S(1)}, bf16[128,640]{1,0:T(8,128)(2,1)S(1)}, bf16[128,640]{1,0:T(8,128)(2,1)S(1)}, bf16[128,640]{1,0:T(8,128)(2,1)S(1)}, bf16[512,640]{1,0:T(8,128)(2,1)S(1)}) custom-call(bf16[256,1024]{1,0:T(8,128)(2,1)S(1)} %copy-done.1, bf16[256,2304]{1,0:T(8,128)(2,1)S(1)} %collective-permute-done.up_ref.refs_1_.refs_6_, ...), custom_call_target="tpu_custom_call" | custom-call | flops 1342177280 | bytes 4980736 | tf_op jit(solution)/shard_map/product/pallas_call | solution.py:303
  65.3 3.3 %product.2 = (bf16[128,640]{1,0:T(8,128)(2,1)S(1)}, bf16[128,640]{1,0:T(8,128)(2,1)S(1)}, bf16[128,640]{1,0:T(8,128)(2,1)S(1)}, bf16[128,640]{1,0:T(8,128)(2,1)S(1)}, bf16[512,640]{1,0:T(8,128)(2,1)S(1)}) custom-call(bf16[256,1024]{1,0:T(8,128)(2,1)S(1)} %copy-done.1, bf16[256,2304]{1,0:T(8,128)(2,1)S(1)} %collective-permute-done.up_ref.refs_1_.refs_6_, ...), custom_call_target="tpu_custom_call" | custom-call | flops 1342177280 | bytes 4980736 | tf_op jit(solution)/shard_map/product/pallas_call | solution.py:303
  70.9 5.0 %collective-permute-done.20.refs_2_ = bf16[128,640]{1,0:T(8,128)(2,1)S(1)} collective-permute-done((bf16[128,640]{1,0:T(8,128)(2,1)S(1)}, bf16[128,640]{1,0:T(8,128)(2,1)S(1)}, u32[]{:S(2)}, u32[]{:S(2)}) %collective-permute-start.20) | collective-permute-done | bytes 163872 | tf_op jit(solution)/shard_map/ppermute | solution.py:52
  76.1 3.4 %collective-permute-done.9.refs_2_ = bf16[128,640]{1,0:T(8,128)(2,1)S(1)} collective-permute-done((bf16[128,640]{1,0:T(8,128)(2,1)S(1)}, bf16[128,640]{1,0:T(8,128)(2,1)S(1)}, u32[]{:S(2)}, u32[]{:S(2)}) %collective-permute-start.9) | collective-permute-done | bytes 163872 | tf_op jit(solution)/shard_map/ppermute | solution.py:52
  83.1 3.3 %collective-permute-start.17 = (bf16[256,256]{1,0:T(8,128)(2,1)S(1)}, bf16[256,256]{1,0:T(8,128)(2,1)S(1)}, u32[]{:S(2)}, u32[]{:S(2)}) collective-permute-start(bf16[256,256]{1,0:T(8,128)(2,1)S(1)} %get-tuple-element.61), channel_id=1, source_target_pairs={{0,16},{1,17},{8,24},{9,25},{16,0},{17,1},{24,8},{25,9},{2,18},{3,... | collective-permute-start | bytes 393224 | tf_op jit(solution)/shard_map/ppermute | solution.py:44
  90.5 4.8 %collective-permute-start.23 = (bf16[128,896]{1,0:T(8,128)(2,1)S(1)}, bf16[128,896]{1,0:T(8,128)(2,1)S(1)}, u32[]{:S(2)}, u32[]{:S(2)}) collective-permute-start(bf16[128,896]{1,0:T(8,128)(2,1)S(1)} %add.265), channel_id=1, source_target_pairs={{0,230},{2,228},{4,226},{6,224},{32,198},{34,196},{36,194},{38,192... | collective-permute-start | bytes 688136 | tf_op jit(solution)/shard_map/ppermute | solution.py:70
  95.6 6.4 %collective-permute-done.23 = bf16[128,896]{1,0:T(8,128)(2,1)S(1)} collective-permute-done((bf16[128,896]{1,0:T(8,128)(2,1)S(1)}, bf16[128,896]{1,0:T(8,128)(2,1)S(1)}, u32[]{:S(2)}, u32[]{:S(2)}) %collective-permute-start.23) | collective-permute-done | bytes 229408 | tf_op jit(solution)/shard_map/ppermute | solution.py:70
  102.6 2.8 %collective-permute-start.26 = (bf16[128,896]{1,0:T(8,128)(2,1)S(1)}, bf16[128,896]{1,0:T(8,128)(2,1)S(1)}, u32[]{:S(2)}, u32[]{:S(2)}) collective-permute-start(bf16[128,896]{1,0:T(8,128)(2,1)S(1)} %get-tuple-element.72), channel_id=1, source_target_pairs={{0,6},{128,130},{2,0},{130,132},{4,2},{132,134},{6,4},{134,128},{1... | collective-permute-start | bytes 688136 | tf_op jit(solution)/shard_map/ppermute | solution.py:52
  105.6 3.3 %collective-permute-done.24 = bf16[128,896]{1,0:T(8,128)(2,1)S(1)} collective-permute-done((bf16[128,896]{1,0:T(8,128)(2,1)S(1)}, bf16[128,896]{1,0:T(8,128)(2,1)S(1)}, u32[]{:S(2)}, u32[]{:S(2)}) %collective-permute-start.24) | collective-permute-done | bytes 229408 | tf_op jit(solution)/shard_map/ppermute | solution.py:52
  109.9 2.7 %collective-permute-start.27 = (bf16[64,896]{1,0:T(8,128)(2,1)S(1)}, bf16[64,896]{1,0:T(8,128)(2,1)S(1)}, u32[]{:S(2)}, u32[]{:S(2)}) collective-permute-start(bf16[64,896]{1,0:T(8,128)(2,1)S(1)} %slice.33), channel_id=1, source_target_pairs={{0,6},{128,130},{2,0},{130,132},{4,2},{132,134},{6,4},{134,128},{1... | collective-permute-start | bytes 344072 | tf_op jit(solution)/shard_map/ppermute | solution.py:52
  112.7 3.4 %collective-permute-done.25 = bf16[64,896]{1,0:T(8,128)(2,1)S(1)} collective-permute-done((bf16[64,896]{1,0:T(8,128)(2,1)S(1)}, bf16[64,896]{1,0:T(8,128)(2,1)S(1)}, u32[]{:S(2)}, u32[]{:S(2)}) %collective-permute-start.25) | collective-permute-done | bytes 114720 | tf_op jit(solution)/shard_map/ppermute | solution.py:52
  118.1 7.2 %collective-permute-start.28 = (bf16[4,32,896]{2,1,0:T(8,128)(2,1)S(1)}, bf16[4,32,896]{2,1,0:T(8,128)(2,1)S(1)}, u32[]{:S(2)}, u32[]{:S(2)}) collective-permute-start(bf16[4,32,896]{2,1,0:T(8,128)(2,1)S(1)} %get-tuple-element.77), channel_id=1, source_target_pairs={{0,1},{1,0},{8,9},{9,8},{16,17},{17,16},{24,25},{25,24},{2,3},{3,2... | collective-permute-start | bytes 688136 | tf_op jit(solution)/shard_map/ppermute | solution.py:44
  127.7 3.6 %collective-permute-start.30 = (bf16[2,32,896]{2,1,0:T(8,128)(2,1)S(1)}, bf16[2,32,896]{2,1,0:T(8,128)(2,1)S(1)}, u32[]{:S(2)}, u32[]{:S(2)}) collective-permute-start(bf16[2,32,896]{2,1,0:T(8,128)(2,1)S(1)} %get-tuple-element.76), channel_id=1, source_target_pairs={{0,16},{1,17},{8,24},{9,25},{16,0},{17,1},{24,8},{25,9},{2,18},{3,... | collective-permute-start | bytes 344072 | tf_op jit(solution)/shard_map/ppermute | solution.py:44
  133.4 3.3 %collective-permute-done.30.refs_3_ = bf16[2,32,896]{2,1,0:T(8,128)(2,1)S(1)} collective-permute-done((bf16[2,32,896]{2,1,0:T(8,128)(2,1)S(1)}, bf16[2,32,896]{2,1,0:T(8,128)(2,1)S(1)}, u32[]{:S(2)}, u32[]{:S(2)}) %collective-permute-start.30) | collective-permute-done | bytes 114720 | tf_op jit(solution)/shard_map/ppermute | solution.py:44
  136.7 3.0 %adamw.1 = (f32[32,7168]{1,0:T(8,128)}, bf16[32,7168]{1,0:T(8,128)(2,1)}, bf16[32,7168]{1,0:T(8,128)(2,1)}) custom-call(s32[8,32]{1,0:T(8,128)S(1)} %copy-done.13, bf16[2,32,896]{2,1,0:T(8,128)(2,1)S(1)} %get-tuple-element.74.refs_1_, bf16[2,32,896]{2,1,0:T(8,128)(2,1)S(1)} %collective-permute-done.29.refs_2_, ...), custom_call_target="tpu_custom_call" | custom-call | tf_op jit(solution)/shard_map/adamw/pallas_call | solution.py:374
  (104 shorter events, 41.2 us)
Async XLA Ops:
  8.1 35.2 %collective-permute-start = (bf16[256,2304]{1,0:T(8,128)(2,1)}, bf16[256,2304]{1,0:T(8,128)(2,1)S(1)}, u32[]{:S(2)}, u32[]{:S(2)}) collective-permute-start(bf16[256,2304]{1,0:T(8,128)(2,1)} %get-tuple-element.38), channel_id=1, source_target_pairs={{0,8},{1,9},{8,16},{9,17},{16,24},{17,25},{24,0},{25,1},{2,10},{3,... | collective-permute-start | bytes 3538952 | tf_op jit(solution)/shard_map/ppermute | solution.py:44
  8.1 41.9 %collective-permute-start.1 = (bf16[256,2304]{1,0:T(8,128)(2,1)}, bf16[256,2304]{1,0:T(8,128)(2,1)}, u32[]{:S(2)}, u32[]{:S(2)}) collective-permute-start(bf16[256,2304]{1,0:T(8,128)(2,1)} %get-tuple-element.39), channel_id=1, source_target_pairs={{0,24},{1,25},{8,0},{9,1},{16,8},{17,9},{24,16},{25,17},{2,26},{3,... | collective-permute-start | bytes 3538952 | tf_op jit(solution)/shard_map/ppermute | solution.py:44
  16.8 9.3 %collective-permute-start.3 = (bf16[128,1024]{1,0:T(8,128)(2,1)}, bf16[128,1024]{1,0:T(8,128)(2,1)}, u32[]{:S(2)}, u32[]{:S(2)}) collective-permute-start(bf16[128,1024]{1,0:T(8,128)(2,1)} %get-tuple-element.44), channel_id=1, source_target_pairs={{0,2},{128,134},{2,4},{130,128},{4,6},{132,130},{6,0},{134,132},{1... | collective-permute-start | bytes 786440 | tf_op jit(solution)/shard_map/ppermute | solution.py:52
  16.9 14.9 %collective-permute-start.12 = (bf16[128,1024]{1,0:T(8,128)(2,1)}, bf16[128,1024]{1,0:T(8,128)(2,1)}, u32[]{:S(2)}, u32[]{:S(2)}) collective-permute-start(bf16[128,1024]{1,0:T(8,128)(2,1)} %get-tuple-element.57), channel_id=1, source_target_pairs={{0,2},{128,134},{2,4},{130,128},{4,6},{132,130},{6,0},{134,132},{1... | collective-permute-start | bytes 786440 | tf_op jit(solution)/shard_map/ppermute | solution.py:52
  20.8 34.9 %collective-permute-start.7 = (bf16[256,1280]{1,0:T(8,128)(2,1)}, bf16[256,1280]{1,0:T(8,128)(2,1)S(1)}, u32[]{:S(2)}, u32[]{:S(2)}) collective-permute-start(bf16[256,1280]{1,0:T(8,128)(2,1)} %get-tuple-element.48), channel_id=1, source_target_pairs={{0,16},{1,17},{8,24},{9,25},{16,0},{17,1},{24,8},{25,9},{2,18},{3,... | collective-permute-start | bytes 1966088 | tf_op jit(solution)/shard_map/ppermute | solution.py:44
  28.1 7.2 %collective-permute-start.4 = (bf16[128,1024]{1,0:T(8,128)(2,1)S(1)}, bf16[128,1024]{1,0:T(8,128)(2,1)S(1)}, u32[]{:S(2)}, u32[]{:S(2)}) collective-permute-start(bf16[128,1024]{1,0:T(8,128)(2,1)S(1)} %add.254), channel_id=1, source_target_pairs={{0,2},{128,134},{2,4},{130,128},{4,6},{132,130},{6,0},{134,132},{1... | collective-permute-start | bytes 786440 | tf_op jit(solution)/shard_map/ppermute | solution.py:52
  32.8 10.3 %collective-permute-start.13 = (bf16[128,1024]{1,0:T(8,128)(2,1)S(1)}, bf16[128,1024]{1,0:T(8,128)(2,1)S(1)}, u32[]{:S(2)}, u32[]{:S(2)}) collective-permute-start(bf16[128,1024]{1,0:T(8,128)(2,1)S(1)} %add.259), channel_id=1, source_target_pairs={{0,2},{128,134},{2,4},{130,128},{4,6},{132,130},{6,0},{134,132},{1... | collective-permute-start | bytes 786440 | tf_op jit(solution)/shard_map/ppermute | solution.py:52
  35.4 19.6 %collective-permute-start.15 = (bf16[128,1024]{1,0:T(8,128)(2,1)S(1)}, bf16[128,1024]{1,0:T(8,128)(2,1)S(1)}, u32[]{:S(2)}, u32[]{:S(2)}) collective-permute-start(bf16[128,1024]{1,0:T(8,128)(2,1)S(1)} %add.255.after_ref), channel_id=1, source_target_pairs={{0,2},{128,134},{2,4},{130,128},{4,6},{132,130},{6,0},{134,132},{1... | collective-permute-start | bytes 786440 | tf_op jit(solution)/shard_map/ppermute | solution.py:52
  43.2 11.8 %collective-permute-start.14 = (bf16[128,1024]{1,0:T(8,128)(2,1)S(1)}, bf16[128,1024]{1,0:T(8,128)(2,1)S(1)}, u32[]{:S(2)}, u32[]{:S(2)}) collective-permute-start(bf16[128,1024]{1,0:T(8,128)(2,1)S(1)} %add.260), channel_id=1, source_target_pairs={{0,2},{128,134},{2,4},{130,128},{4,6},{132,130},{6,0},{134,132},{1... | collective-permute-start | bytes 786440 | tf_op jit(solution)/shard_map/ppermute | solution.py:52
  51.0 8.9 %collective-permute-start.5 = (bf16[256,512]{1,0:T(8,128)(2,1)S(1)}, bf16[256,512]{1,0:T(8,128)(2,1)S(1)}, u32[]{:S(2)}, u32[]{:S(2)}) collective-permute-start(bf16[256,512]{1,0:T(8,128)(2,1)S(1)} %get-tuple-element.45), channel_id=1, source_target_pairs={{0,8},{1,9},{8,16},{9,17},{16,24},{17,25},{24,0},{25,1},{2,10},{3,... | collective-permute-start | bytes 786440 | tf_op jit(solution)/shard_map/ppermute | solution.py:44
  51.1 8.8 %collective-permute-start.6 = (bf16[256,512]{1,0:T(8,128)(2,1)S(1)}, bf16[256,512]{1,0:T(8,128)(2,1)S(1)}, u32[]{:S(2)}, u32[]{:S(2)}) collective-permute-start(bf16[256,512]{1,0:T(8,128)(2,1)S(1)} %get-tuple-element.46), channel_id=1, source_target_pairs={{0,24},{1,25},{8,0},{9,1},{16,8},{17,9},{24,16},{25,17},{2,26},{3,... | collective-permute-start | bytes 786440 | tf_op jit(solution)/shard_map/ppermute | solution.py:44
  68.8 7.2 %collective-permute-start.20 = (bf16[128,640]{1,0:T(8,128)(2,1)S(1)}, bf16[128,640]{1,0:T(8,128)(2,1)S(1)}, u32[]{:S(2)}, u32[]{:S(2)}) collective-permute-start(bf16[128,640]{1,0:T(8,128)(2,1)S(1)} %add.262), channel_id=1, source_target_pairs={{0,2},{128,134},{2,4},{130,128},{4,6},{132,130},{6,0},{134,132},{1... | collective-permute-start | bytes 491528 | tf_op jit(solution)/shard_map/ppermute | solution.py:52
  70.8 8.6 %collective-permute-start.9 = (bf16[128,640]{1,0:T(8,128)(2,1)S(1)}, bf16[128,640]{1,0:T(8,128)(2,1)S(1)}, u32[]{:S(2)}, u32[]{:S(2)}) collective-permute-start(bf16[128,640]{1,0:T(8,128)(2,1)S(1)} %add.256), channel_id=1, source_target_pairs={{0,2},{128,134},{2,4},{130,128},{4,6},{132,130},{6,0},{134,132},{1... | collective-permute-start | bytes 491528 | tf_op jit(solution)/shard_map/ppermute | solution.py:52
  79.5 8.1 %collective-permute-start.10 = (bf16[128,640]{1,0:T(8,128)(2,1)S(1)}, bf16[128,640]{1,0:T(8,128)(2,1)S(1)}, u32[]{:S(2)}, u32[]{:S(2)}) collective-permute-start(bf16[128,640]{1,0:T(8,128)(2,1)S(1)} %add.257), channel_id=1, source_target_pairs={{0,2},{128,134},{2,4},{130,128},{4,6},{132,130},{6,0},{134,132},{1... | collective-permute-start | bytes 491528 | tf_op jit(solution)/shard_map/ppermute | solution.py:52
  82.1 8.3 %collective-permute-start.22 = (bf16[128,640]{1,0:T(8,128)(2,1)S(1)}, bf16[128,640]{1,0:T(8,128)(2,1)S(1)}, u32[]{:S(2)}, u32[]{:S(2)}) collective-permute-start(bf16[128,640]{1,0:T(8,128)(2,1)S(1)} %add.264), channel_id=1, source_target_pairs={{0,2},{128,134},{2,4},{130,128},{4,6},{132,130},{6,0},{134,132},{1... | collective-permute-start | bytes 491528 | tf_op jit(solution)/shard_map/ppermute | solution.py:52
  83.1 7.2 %collective-permute-start.17 = (bf16[256,256]{1,0:T(8,128)(2,1)S(1)}, bf16[256,256]{1,0:T(8,128)(2,1)S(1)}, u32[]{:S(2)}, u32[]{:S(2)}) collective-permute-start(bf16[256,256]{1,0:T(8,128)(2,1)S(1)} %get-tuple-element.61), channel_id=1, source_target_pairs={{0,16},{1,17},{8,24},{9,25},{16,0},{17,1},{24,8},{25,9},{2,18},{3,... | collective-permute-start | bytes 393224 | tf_op jit(solution)/shard_map/ppermute | solution.py:44
  87.6 7.9 %collective-permute-start.11 = (bf16[128,640]{1,0:T(8,128)(2,1)S(1)}, bf16[128,640]{1,0:T(8,128)(2,1)S(1)}, u32[]{:S(2)}, u32[]{:S(2)}) collective-permute-start(bf16[128,640]{1,0:T(8,128)(2,1)S(1)} %add.258), channel_id=1, source_target_pairs={{0,2},{128,134},{2,4},{130,128},{4,6},{132,130},{6,0},{134,132},{1... | collective-permute-start | bytes 491528 | tf_op jit(solution)/shard_map/ppermute | solution.py:52
  90.5 11.5 %collective-permute-start.23 = (bf16[128,896]{1,0:T(8,128)(2,1)S(1)}, bf16[128,896]{1,0:T(8,128)(2,1)S(1)}, u32[]{:S(2)}, u32[]{:S(2)}) collective-permute-start(bf16[128,896]{1,0:T(8,128)(2,1)S(1)} %add.265), channel_id=1, source_target_pairs={{0,230},{2,228},{4,226},{6,224},{32,198},{34,196},{36,194},{38,192... | collective-permute-start | bytes 688136 | tf_op jit(solution)/shard_map/ppermute | solution.py:70
  102.0 6.9 %collective-permute-start.24 = (bf16[128,896]{1,0:T(8,128)(2,1)S(1)}, bf16[128,896]{1,0:T(8,128)(2,1)S(1)}, u32[]{:S(2)}, u32[]{:S(2)}) collective-permute-start(bf16[128,896]{1,0:T(8,128)(2,1)S(1)} %get-tuple-element.72), channel_id=1, source_target_pairs={{0,2},{128,134},{2,4},{130,128},{4,6},{132,130},{6,0},{134,132},{1... | collective-permute-start | bytes 688136 | tf_op jit(solution)/shard_map/ppermute | solution.py:52
  102.6 7.3 %collective-permute-start.26 = (bf16[128,896]{1,0:T(8,128)(2,1)S(1)}, bf16[128,896]{1,0:T(8,128)(2,1)S(1)}, u32[]{:S(2)}, u32[]{:S(2)}) collective-permute-start(bf16[128,896]{1,0:T(8,128)(2,1)S(1)} %get-tuple-element.72), channel_id=1, source_target_pairs={{0,6},{128,130},{2,0},{130,132},{4,2},{132,134},{6,4},{134,128},{1... | collective-permute-start | bytes 688136 | tf_op jit(solution)/shard_map/ppermute | solution.py:52
  109.0 7.1 %collective-permute-start.25 = (bf16[64,896]{1,0:T(8,128)(2,1)S(1)}, bf16[64,896]{1,0:T(8,128)(2,1)S(1)}, u32[]{:S(2)}, u32[]{:S(2)}) collective-permute-start(bf16[64,896]{1,0:T(8,128)(2,1)S(1)} %slice.32), channel_id=1, source_target_pairs={{0,2},{128,134},{2,4},{130,128},{4,6},{132,130},{6,0},{134,132},{1... | collective-permute-start | bytes 344072 | tf_op jit(solution)/shard_map/ppermute | solution.py:52
  109.9 7.6 %collective-permute-start.27 = (bf16[64,896]{1,0:T(8,128)(2,1)S(1)}, bf16[64,896]{1,0:T(8,128)(2,1)S(1)}, u32[]{:S(2)}, u32[]{:S(2)}) collective-permute-start(bf16[64,896]{1,0:T(8,128)(2,1)S(1)} %slice.33), channel_id=1, source_target_pairs={{0,6},{128,130},{2,0},{130,132},{4,2},{132,134},{6,4},{134,128},{1... | collective-permute-start | bytes 344072 | tf_op jit(solution)/shard_map/ppermute | solution.py:52
  118.1 8.3 %collective-permute-start.28 = (bf16[4,32,896]{2,1,0:T(8,128)(2,1)S(1)}, bf16[4,32,896]{2,1,0:T(8,128)(2,1)S(1)}, u32[]{:S(2)}, u32[]{:S(2)}) collective-permute-start(bf16[4,32,896]{2,1,0:T(8,128)(2,1)S(1)} %get-tuple-element.77), channel_id=1, source_target_pairs={{0,1},{1,0},{8,9},{9,8},{16,17},{17,16},{24,25},{25,24},{2,3},{3,2... | collective-permute-start | bytes 688136 | tf_op jit(solution)/shard_map/ppermute | solution.py:44
  127.7 9.0 %collective-permute-start.30 = (bf16[2,32,896]{2,1,0:T(8,128)(2,1)S(1)}, bf16[2,32,896]{2,1,0:T(8,128)(2,1)S(1)}, u32[]{:S(2)}, u32[]{:S(2)}) collective-permute-start(bf16[2,32,896]{2,1,0:T(8,128)(2,1)S(1)} %get-tuple-element.76), channel_id=1, source_target_pairs={{0,16},{1,17},{8,24},{9,25},{16,0},{17,1},{24,8},{25,9},{2,18},{3,... | collective-permute-start | bytes 344072 | tf_op jit(solution)/shard_map/ppermute | solution.py:44
  (22 other events, 152.9 us)

commit v5 on v4

--- a/solution.py
+++ b/solution.py
@@ -424,7 +424,7 @@
     )
     late = [send_group(piece, dy, 0) for dy, piece in enumerate(pieces)]
 
-    far = forward(near[0], near[1], half, steps[FORWARD])
+    far = forward(near[0], near[1], half, own)
     far = [send_group(far[0], 1, 0), send_group(far[1], 3, 0)]
     hidden = [own, near[0], far[0], near[1], far[1]]
     sums, after = [], [pieces[0]]

time: 140 us -> 140 us (level)
  no operation moved by 1% of the time
where the time goes in v5:
time: 140 us
  waiting for transfers between devices  63.2 us (45%)
  starting transfers between devices  46.6 us (33%)
  Pallas kernels  22.3 us (16%)
  local copies, waits for them, and re-layouts  5.52 us (4%)
    ppermute x16, waiting for transfers between devices, send_ring(): return lax.ppermute(value, ('zh', 'z'), pairs)  36.5 us
    ppermute x15, starting transfers between devices, send_group(): return lax.ppermute(value, ('y', 'c'), pairs)  33.2 us
    ppermute x15, waiting for transfers between devices, send_group(): return lax.ppermute(value, ('y', 'c'), pairs)  20.3 us
    ppermute x16, starting transfers between devices, send_ring(): return lax.ppermute(value, ('zh', 'z'), pairs)  8.57 us
    pallas_call x2, Pallas kernels, product(): pl.pallas_call(functools.partial(product_kernel, part, len(after)), out_s...  6.55 us
    ppermute x1, waiting for transfers between devices, send_mirror(): return lax.ppermute(value, ('zh', 'x', 'z'), pairs)  6.37 us
    unnamed x31, local copies, waits for them, and re-layouts  5.24 us
    ppermute x1, starting transfers between devices, send_mirror(): return lax.ppermute(value, ('zh', 'x', 'z'), pairs)  4.78 us
  transfers between devices with their start and end apart: 32, of which 21 were waited for; matrix products, arithmetic and copies ran while one was open for 0% of the time, Pallas kernels for 9%

profile of v5, /device:TPU:1, one launch (start us, length us, event | category | flops | bytes accessed | tf_op | source)
XLA Modules:
  0.0 139.6 jit_solution(4779242481105496935)
XLA Ops:
  0.6 4.1 %prepare.1 = (bf16[256,1024]{1,0:T(8,128)(2,1)}, bf16[256,2304]{1,0:T(8,128)(2,1)}, bf16[256,2304]{1,0:T(8,128)(2,1)}, bf16[256,2048]{1,0:T(8,128)(2,1)}, bf16[256,1024]{1,0:T(8,128)(2,1)}) custom-call(s32[8,32]{1,0:T(8,128)} %live_hbm.1, bf16[256,1024]{1,0:T(8,128)(2,1)} %hidden_hbm.1, bf16[256,7168]{1,0:T(8,128)(2,1)} %grad_hbm.3), custom_call_target="tpu_custom_call" | custom-call | tf_op jit(solution)/shard_map/prepare/pallas_call | solution.py:139
  4.8 3.3 %collective-permute-start.9 = (bf16[256,2048]{1,0:T(8,128)(2,1)}, bf16[256,2048]{1,0:T(8,128)(2,1)S(1)}, u32[]{:S(2)}, u32[]{:S(2)}) collective-permute-start(bf16[256,2048]{1,0:T(8,128)(2,1)} %get-tuple-element.50), channel_id=1, source_target_pairs={{0,1},{1,0},{8,9},{9,8},{16,17},{17,16},{24,25},{25,24},{2,3},{3,2... | collective-permute-start | bytes 3145736 | tf_op jit(solution)/shard_map/ppermute | solution.py:44
  8.1 2.7 %collective-permute-start.1 = (bf16[256,2304]{1,0:T(8,128)(2,1)}, bf16[256,2304]{1,0:T(8,128)(2,1)}, u32[]{:S(2)}, u32[]{:S(2)}) collective-permute-start(bf16[256,2304]{1,0:T(8,128)(2,1)} %get-tuple-element.39), channel_id=1, source_target_pairs={{0,24},{1,25},{8,0},{9,1},{16,8},{17,9},{24,16},{25,17},{2,26},{3,... | collective-permute-start | bytes 3538952 | tf_op jit(solution)/shard_map/ppermute | solution.py:44
  20.9 2.8 %collective-permute-start.4 = (bf16[256,1280]{1,0:T(8,128)(2,1)}, bf16[256,1280]{1,0:T(8,128)(2,1)S(1)}, u32[]{:S(2)}, u32[]{:S(2)}) collective-permute-start(bf16[256,1280]{1,0:T(8,128)(2,1)} %get-tuple-element.43), channel_id=1, source_target_pairs={{0,16},{1,17},{8,24},{9,25},{16,0},{17,1},{24,8},{25,9},{2,18},{3,... | collective-permute-start | bytes 1966088 | tf_op jit(solution)/shard_map/ppermute | solution.py:44
  28.2 3.6 %collective-permute-done.10.refs_1_ = bf16[128,1024]{1,0:T(8,128)(2,1)} collective-permute-done((bf16[128,1024]{1,0:T(8,128)(2,1)}, bf16[128,1024]{1,0:T(8,128)(2,1)}, u32[]{:S(2)}, u32[]{:S(2)}) %collective-permute-start.10) | collective-permute-done | bytes 262176 | tf_op jit(solution)/shard_map/ppermute | solution.py:52
  35.5 7.7 %collective-permute-done.11.refs_1_ = bf16[128,1024]{1,0:T(8,128)(2,1)S(1)} collective-permute-done((bf16[128,1024]{1,0:T(8,128)(2,1)S(1)}, bf16[128,1024]{1,0:T(8,128)(2,1)S(1)}, u32[]{:S(2)}, u32[]{:S(2)}) %collective-permute-start.11) | collective-permute-done | bytes 262176 | tf_op jit(solution)/shard_map/ppermute | solution.py:52
  43.3 6.7 %collective-permute-done.1.down_ref.refs_3_.refs_8_ = bf16[256,2304]{1,0:T(8,128)(2,1)} collective-permute-done((bf16[256,2304]{1,0:T(8,128)(2,1)}, bf16[256,2304]{1,0:T(8,128)(2,1)}, u32[]{:S(2)}, u32[]{:S(2)}) %collective-permute-start.1) | collective-permute-done | bytes 1179680 | tf_op jit(solution)/shard_map/ppermute | solution.py:44
  51.1 3.8 %collective-permute-start.3 = (bf16[256,512]{1,0:T(8,128)(2,1)S(1)}, bf16[256,512]{1,0:T(8,128)(2,1)S(1)}, u32[]{:S(2)}, u32[]{:S(2)}) collective-permute-start(bf16[256,512]{1,0:T(8,128)(2,1)S(1)} %get-tuple-element.41), channel_id=1, source_target_pairs={{0,24},{1,25},{8,0},{9,1},{16,8},{17,9},{24,16},{25,17},{2,26},{3,... | collective-permute-start | bytes 786440 | tf_op jit(solution)/shard_map/ppermute | solution.py:44
  55.7 4.2 %collective-permute-done.2.refs_2_ = bf16[256,512]{1,0:T(8,128)(2,1)S(1)} collective-permute-done((bf16[256,512]{1,0:T(8,128)(2,1)S(1)}, bf16[256,512]{1,0:T(8,128)(2,1)S(1)}, u32[]{:S(2)}, u32[]{:S(2)}) %collective-permute-start.2) | collective-permute-done | bytes 262176 | tf_op jit(solution)/shard_map/ppermute | solution.py:44
  59.9 3.3 %product.3 = (bf16[128,640]{1,0:T(8,128)(2,1)S(1)}, bf16[128,640]{1,0:T(8,128)(2,1)S(1)}, bf16[128,640]{1,0:T(8,128)(2,1)S(1)}, bf16[128,640]{1,0:T(8,128)(2,1)S(1)}, bf16[512,640]{1,0:T(8,128)(2,1)S(1)}) custom-call(bf16[256,1024]{1,0:T(8,128)(2,1)S(1)} %copy-done.1, bf16[256,2304]{1,0:T(8,128)(2,1)S(1)} %collective-permute-done.up_ref.refs_1_.refs_6_, ...), custom_call_target="tpu_custom_call" | custom-call | flops 1342177280 | bytes 4980736 | tf_op jit(solution)/shard_map/product/pallas_call | solution.py:303
  65.3 3.3 %product.2 = (bf16[128,640]{1,0:T(8,128)(2,1)S(1)}, bf16[128,640]{1,0:T(8,128)(2,1)S(1)}, bf16[128,640]{1,0:T(8,128)(2,1)S(1)}, bf16[128,640]{1,0:T(8,128)(2,1)S(1)}, bf16[512,640]{1,0:T(8,128)(2,1)S(1)}) custom-call(bf16[256,1024]{1,0:T(8,128)(2,1)S(1)} %copy-done.1, bf16[256,2304]{1,0:T(8,128)(2,1)S(1)} %collective-permute-done.up_ref.refs_1_.refs_6_, ...), custom_call_target="tpu_custom_call" | custom-call | flops 1342177280 | bytes 4980736 | tf_op jit(solution)/shard_map/product/pallas_call | solution.py:303
  70.9 5.0 %collective-permute-done.20.refs_2_ = bf16[128,640]{1,0:T(8,128)(2,1)S(1)} collective-permute-done((bf16[128,640]{1,0:T(8,128)(2,1)S(1)}, bf16[128,640]{1,0:T(8,128)(2,1)S(1)}, u32[]{:S(2)}, u32[]{:S(2)}) %collective-permute-start.20) | collective-permute-done | bytes 163872 | tf_op jit(solution)/shard_map/ppermute | solution.py:52
  76.0 3.4 %collective-permute-done.6.refs_2_ = bf16[128,640]{1,0:T(8,128)(2,1)S(1)} collective-permute-done((bf16[128,640]{1,0:T(8,128)(2,1)S(1)}, bf16[128,640]{1,0:T(8,128)(2,1)S(1)}, u32[]{:S(2)}, u32[]{:S(2)}) %collective-permute-start.6) | collective-permute-done | bytes 163872 | tf_op jit(solution)/shard_map/ppermute | solution.py:52
  83.1 3.3 %collective-permute-start.17 = (bf16[256,256]{1,0:T(8,128)(2,1)S(1)}, bf16[256,256]{1,0:T(8,128)(2,1)S(1)}, u32[]{:S(2)}, u32[]{:S(2)}) collective-permute-start(bf16[256,256]{1,0:T(8,128)(2,1)S(1)} %get-tuple-element.61), channel_id=1, source_target_pairs={{0,16},{1,17},{8,24},{9,25},{16,0},{17,1},{24,8},{25,9},{2,18},{3,... | collective-permute-start | bytes 393224 | tf_op jit(solution)/shard_map/ppermute | solution.py:44
  90.4 4.8 %collective-permute-start.23 = (bf16[128,896]{1,0:T(8,128)(2,1)S(1)}, bf16[128,896]{1,0:T(8,128)(2,1)S(1)}, u32[]{:S(2)}, u32[]{:S(2)}) collective-permute-start(bf16[128,896]{1,0:T(8,128)(2,1)S(1)} %add.265), channel_id=1, source_target_pairs={{0,230},{2,228},{4,226},{6,224},{32,198},{34,196},{36,194},{38,192... | collective-permute-start | bytes 688136 | tf_op jit(solution)/shard_map/ppermute | solution.py:70
  95.6 6.4 %collective-permute-done.23 = bf16[128,896]{1,0:T(8,128)(2,1)S(1)} collective-permute-done((bf16[128,896]{1,0:T(8,128)(2,1)S(1)}, bf16[128,896]{1,0:T(8,128)(2,1)S(1)}, u32[]{:S(2)}, u32[]{:S(2)}) %collective-permute-start.23) | collective-permute-done | bytes 229408 | tf_op jit(solution)/shard_map/ppermute | solution.py:70
  102.5 2.8 %collective-permute-start.26 = (bf16[128,896]{1,0:T(8,128)(2,1)S(1)}, bf16[128,896]{1,0:T(8,128)(2,1)S(1)}, u32[]{:S(2)}, u32[]{:S(2)}) collective-permute-start(bf16[128,896]{1,0:T(8,128)(2,1)S(1)} %get-tuple-element.72), channel_id=1, source_target_pairs={{0,6},{128,130},{2,0},{130,132},{4,2},{132,134},{6,4},{134,128},{1... | collective-permute-start | bytes 688136 | tf_op jit(solution)/shard_map/ppermute | solution.py:52
  105.6 3.3 %collective-permute-done.24 = bf16[128,896]{1,0:T(8,128)(2,1)S(1)} collective-permute-done((bf16[128,896]{1,0:T(8,128)(2,1)S(1)}, bf16[128,896]{1,0:T(8,128)(2,1)S(1)}, u32[]{:S(2)}, u32[]{:S(2)}) %collective-permute-start.24) | collective-permute-done | bytes 229408 | tf_op jit(solution)/shard_map/ppermute | solution.py:52
  109.8 2.7 %collective-permute-start.27 = (bf16[64,896]{1,0:T(8,128)(2,1)S(1)}, bf16[64,896]{1,0:T(8,128)(2,1)S(1)}, u32[]{:S(2)}, u32[]{:S(2)}) collective-permute-start(bf16[64,896]{1,0:T(8,128)(2,1)S(1)} %slice.33), channel_id=1, source_target_pairs={{0,6},{128,130},{2,0},{130,132},{4,2},{132,134},{6,4},{134,128},{1... | collective-permute-start | bytes 344072 | tf_op jit(solution)/shard_map/ppermute | solution.py:52
  112.6 3.4 %collective-permute-done.25 = bf16[64,896]{1,0:T(8,128)(2,1)S(1)} collective-permute-done((bf16[64,896]{1,0:T(8,128)(2,1)S(1)}, bf16[64,896]{1,0:T(8,128)(2,1)S(1)}, u32[]{:S(2)}, u32[]{:S(2)}) %collective-permute-start.25) | collective-permute-done | bytes 114720 | tf_op jit(solution)/shard_map/ppermute | solution.py:52
  118.1 7.2 %collective-permute-start.28 = (bf16[4,32,896]{2,1,0:T(8,128)(2,1)S(1)}, bf16[4,32,896]{2,1,0:T(8,128)(2,1)S(1)}, u32[]{:S(2)}, u32[]{:S(2)}) collective-permute-start(bf16[4,32,896]{2,1,0:T(8,128)(2,1)S(1)} %get-tuple-element.77), channel_id=1, source_target_pairs={{0,1},{1,0},{8,9},{9,8},{16,17},{17,16},{24,25},{25,24},{2,3},{3,2... | collective-permute-start | bytes 688136 | tf_op jit(solution)/shard_map/ppermute | solution.py:44
  127.6 3.6 %collective-permute-start.30 = (bf16[2,32,896]{2,1,0:T(8,128)(2,1)S(1)}, bf16[2,32,896]{2,1,0:T(8,128)(2,1)S(1)}, u32[]{:S(2)}, u32[]{:S(2)}) collective-permute-start(bf16[2,32,896]{2,1,0:T(8,128)(2,1)S(1)} %get-tuple-element.76), channel_id=1, source_target_pairs={{0,16},{1,17},{8,24},{9,25},{16,0},{17,1},{24,8},{25,9},{2,18},{3,... | collective-permute-start | bytes 344072 | tf_op jit(solution)/shard_map/ppermute | solution.py:44
  133.3 3.3 %collective-permute-done.30.refs_3_ = bf16[2,32,896]{2,1,0:T(8,128)(2,1)S(1)} collective-permute-done((bf16[2,32,896]{2,1,0:T(8,128)(2,1)S(1)}, bf16[2,32,896]{2,1,0:T(8,128)(2,1)S(1)}, u32[]{:S(2)}, u32[]{:S(2)}) %collective-permute-start.30) | collective-permute-done | bytes 114720 | tf_op jit(solution)/shard_map/ppermute | solution.py:44
  136.6 3.0 %adamw.1 = (f32[32,7168]{1,0:T(8,128)}, bf16[32,7168]{1,0:T(8,128)(2,1)}, bf16[32,7168]{1,0:T(8,128)(2,1)}) custom-call(s32[8,32]{1,0:T(8,128)S(1)} %copy-done.13, bf16[2,32,896]{2,1,0:T(8,128)(2,1)S(1)} %get-tuple-element.74.refs_1_, bf16[2,32,896]{2,1,0:T(8,128)(2,1)S(1)} %collective-permute-done.29.refs_2_, ...), custom_call_target="tpu_custom_call" | custom-call | tf_op jit(solution)/shard_map/adamw/pallas_call | solution.py:374
  (104 shorter events, 41.1 us)
Async XLA Ops:
  8.1 35.2 %collective-permute-start = (bf16[256,2304]{1,0:T(8,128)(2,1)}, bf16[256,2304]{1,0:T(8,128)(2,1)S(1)}, u32[]{:S(2)}, u32[]{:S(2)}) collective-permute-start(bf16[256,2304]{1,0:T(8,128)(2,1)} %get-tuple-element.38), channel_id=1, source_target_pairs={{0,8},{1,9},{8,16},{9,17},{16,24},{17,25},{24,0},{25,1},{2,10},{3,... | collective-permute-start | bytes 3538952 | tf_op jit(solution)/shard_map/ppermute | solution.py:44
  8.1 41.9 %collective-permute-start.1 = (bf16[256,2304]{1,0:T(8,128)(2,1)}, bf16[256,2304]{1,0:T(8,128)(2,1)}, u32[]{:S(2)}, u32[]{:S(2)}) collective-permute-start(bf16[256,2304]{1,0:T(8,128)(2,1)} %get-tuple-element.39), channel_id=1, source_target_pairs={{0,24},{1,25},{8,0},{9,1},{16,8},{17,9},{24,16},{25,17},{2,26},{3,... | collective-permute-start | bytes 3538952 | tf_op jit(solution)/shard_map/ppermute | solution.py:44
  16.9 9.3 %collective-permute-start.13 = (bf16[128,1024]{1,0:T(8,128)(2,1)}, bf16[128,1024]{1,0:T(8,128)(2,1)}, u32[]{:S(2)}, u32[]{:S(2)}) collective-permute-start(bf16[128,1024]{1,0:T(8,128)(2,1)} %get-tuple-element.58), channel_id=1, source_target_pairs={{0,2},{128,134},{2,4},{130,128},{4,6},{132,130},{6,0},{134,132},{1... | collective-permute-start | bytes 786440 | tf_op jit(solution)/shard_map/ppermute | solution.py:52
  16.9 14.9 %collective-permute-start.10 = (bf16[128,1024]{1,0:T(8,128)(2,1)}, bf16[128,1024]{1,0:T(8,128)(2,1)}, u32[]{:S(2)}, u32[]{:S(2)}) collective-permute-start(bf16[128,1024]{1,0:T(8,128)(2,1)} %get-tuple-element.54), channel_id=1, source_target_pairs={{0,2},{128,134},{2,4},{130,128},{4,6},{132,130},{6,0},{134,132},{1... | collective-permute-start | bytes 786440 | tf_op jit(solution)/shard_map/ppermute | solution.py:52
  20.9 34.8 %collective-permute-start.4 = (bf16[256,1280]{1,0:T(8,128)(2,1)}, bf16[256,1280]{1,0:T(8,128)(2,1)S(1)}, u32[]{:S(2)}, u32[]{:S(2)}) collective-permute-start(bf16[256,1280]{1,0:T(8,128)(2,1)} %get-tuple-element.43), channel_id=1, source_target_pairs={{0,16},{1,17},{8,24},{9,25},{16,0},{17,1},{24,8},{25,9},{2,18},{3,... | collective-permute-start | bytes 1966088 | tf_op jit(solution)/shard_map/ppermute | solution.py:44
  28.2 7.2 %collective-permute-start.14 = (bf16[128,1024]{1,0:T(8,128)(2,1)S(1)}, bf16[128,1024]{1,0:T(8,128)(2,1)S(1)}, u32[]{:S(2)}, u32[]{:S(2)}) collective-permute-start(bf16[128,1024]{1,0:T(8,128)(2,1)S(1)} %add.259), channel_id=1, source_target_pairs={{0,2},{128,134},{2,4},{130,128},{4,6},{132,130},{6,0},{134,132},{1... | collective-permute-start | bytes 786440 | tf_op jit(solution)/shard_map/ppermute | solution.py:52
  32.9 10.3 %collective-permute-start.11 = (bf16[128,1024]{1,0:T(8,128)(2,1)S(1)}, bf16[128,1024]{1,0:T(8,128)(2,1)S(1)}, u32[]{:S(2)}, u32[]{:S(2)}) collective-permute-start(bf16[128,1024]{1,0:T(8,128)(2,1)S(1)} %add.257), channel_id=1, source_target_pairs={{0,2},{128,134},{2,4},{130,128},{4,6},{132,130},{6,0},{134,132},{1... | collective-permute-start | bytes 786440 | tf_op jit(solution)/shard_map/ppermute | solution.py:52
  35.4 19.5 %collective-permute-start.15 = (bf16[128,1024]{1,0:T(8,128)(2,1)S(1)}, bf16[128,1024]{1,0:T(8,128)(2,1)S(1)}, u32[]{:S(2)}, u32[]{:S(2)}) collective-permute-start(bf16[128,1024]{1,0:T(8,128)(2,1)S(1)} %add.260), channel_id=1, source_target_pairs={{0,2},{128,134},{2,4},{130,128},{4,6},{132,130},{6,0},{134,132},{1... | collective-permute-start | bytes 786440 | tf_op jit(solution)/shard_map/ppermute | solution.py:52
  43.2 11.7 %collective-permute-start.12 = (bf16[128,1024]{1,0:T(8,128)(2,1)S(1)}, bf16[128,1024]{1,0:T(8,128)(2,1)S(1)}, u32[]{:S(2)}, u32[]{:S(2)}) collective-permute-start(bf16[128,1024]{1,0:T(8,128)(2,1)S(1)} %add.258), channel_id=1, source_target_pairs={{0,2},{128,134},{2,4},{130,128},{4,6},{132,130},{6,0},{134,132},{1... | collective-permute-start | bytes 786440 | tf_op jit(solution)/shard_map/ppermute | solution.py:52
  51.0 8.9 %collective-permute-start.2 = (bf16[256,512]{1,0:T(8,128)(2,1)S(1)}, bf16[256,512]{1,0:T(8,128)(2,1)S(1)}, u32[]{:S(2)}, u32[]{:S(2)}) collective-permute-start(bf16[256,512]{1,0:T(8,128)(2,1)S(1)} %get-tuple-element.40), channel_id=1, source_target_pairs={{0,8},{1,9},{8,16},{9,17},{16,24},{17,25},{24,0},{25,1},{2,10},{3,... | collective-permute-start | bytes 786440 | tf_op jit(solution)/shard_map/ppermute | solution.py:44
  51.1 8.8 %collective-permute-start.3 = (bf16[256,512]{1,0:T(8,128)(2,1)S(1)}, bf16[256,512]{1,0:T(8,128)(2,1)S(1)}, u32[]{:S(2)}, u32[]{:S(2)}) collective-permute-start(bf16[256,512]{1,0:T(8,128)(2,1)S(1)} %get-tuple-element.41), channel_id=1, source_target_pairs={{0,24},{1,25},{8,0},{9,1},{16,8},{17,9},{24,16},{25,17},{2,26},{3,... | collective-permute-start | bytes 786440 | tf_op jit(solution)/shard_map/ppermute | solution.py:44
  68.7 7.2 %collective-permute-start.20 = (bf16[128,640]{1,0:T(8,128)(2,1)S(1)}, bf16[128,640]{1,0:T(8,128)(2,1)S(1)}, u32[]{:S(2)}, u32[]{:S(2)}) collective-permute-start(bf16[128,640]{1,0:T(8,128)(2,1)S(1)} %add.262), channel_id=1, source_target_pairs={{0,2},{128,134},{2,4},{130,128},{4,6},{132,130},{6,0},{134,132},{1... | collective-permute-start | bytes 491528 | tf_op jit(solution)/shard_map/ppermute | solution.py:52
  70.8 8.6 %collective-permute-start.6 = (bf16[128,640]{1,0:T(8,128)(2,1)S(1)}, bf16[128,640]{1,0:T(8,128)(2,1)S(1)}, u32[]{:S(2)}, u32[]{:S(2)}) collective-permute-start(bf16[128,640]{1,0:T(8,128)(2,1)S(1)} %add.254), channel_id=1, source_target_pairs={{0,2},{128,134},{2,4},{130,128},{4,6},{132,130},{6,0},{134,132},{1... | collective-permute-start | bytes 491528 | tf_op jit(solution)/shard_map/ppermute | solution.py:52
  79.4 8.1 %collective-permute-start.7 = (bf16[128,640]{1,0:T(8,128)(2,1)S(1)}, bf16[128,640]{1,0:T(8,128)(2,1)S(1)}, u32[]{:S(2)}, u32[]{:S(2)}) collective-permute-start(bf16[128,640]{1,0:T(8,128)(2,1)S(1)} %add.255), channel_id=1, source_target_pairs={{0,2},{128,134},{2,4},{130,128},{4,6},{132,130},{6,0},{134,132},{1... | collective-permute-start | bytes 491528 | tf_op jit(solution)/shard_map/ppermute | solution.py:52
  82.0 8.3 %collective-permute-start.22 = (bf16[128,640]{1,0:T(8,128)(2,1)S(1)}, bf16[128,640]{1,0:T(8,128)(2,1)S(1)}, u32[]{:S(2)}, u32[]{:S(2)}) collective-permute-start(bf16[128,640]{1,0:T(8,128)(2,1)S(1)} %add.264), channel_id=1, source_target_pairs={{0,2},{128,134},{2,4},{130,128},{4,6},{132,130},{6,0},{134,132},{1... | collective-permute-start | bytes 491528 | tf_op jit(solution)/shard_map/ppermute | solution.py:52
  83.1 7.2 %collective-permute-start.17 = (bf16[256,256]{1,0:T(8,128)(2,1)S(1)}, bf16[256,256]{1,0:T(8,128)(2,1)S(1)}, u32[]{:S(2)}, u32[]{:S(2)}) collective-permute-start(bf16[256,256]{1,0:T(8,128)(2,1)S(1)} %get-tuple-element.61), channel_id=1, source_target_pairs={{0,16},{1,17},{8,24},{9,25},{16,0},{17,1},{24,8},{25,9},{2,18},{3,... | collective-permute-start | bytes 393224 | tf_op jit(solution)/shard_map/ppermute | solution.py:44
  87.6 7.9 %collective-permute-start.8 = (bf16[128,640]{1,0:T(8,128)(2,1)S(1)}, bf16[128,640]{1,0:T(8,128)(2,1)S(1)}, u32[]{:S(2)}, u32[]{:S(2)}) collective-permute-start(bf16[128,640]{1,0:T(8,128)(2,1)S(1)} %add.256), channel_id=1, source_target_pairs={{0,2},{128,134},{2,4},{130,128},{4,6},{132,130},{6,0},{134,132},{1... | collective-permute-start | bytes 491528 | tf_op jit(solution)/shard_map/ppermute | solution.py:52
  90.4 11.5 %collective-permute-start.23 = (bf16[128,896]{1,0:T(8,128)(2,1)S(1)}, bf16[128,896]{1,0:T(8,128)(2,1)S(1)}, u32[]{:S(2)}, u32[]{:S(2)}) collective-permute-start(bf16[128,896]{1,0:T(8,128)(2,1)S(1)} %add.265), channel_id=1, source_target_pairs={{0,230},{2,228},{4,226},{6,224},{32,198},{34,196},{36,194},{38,192... | collective-permute-start | bytes 688136 | tf_op jit(solution)/shard_map/ppermute | solution.py:70
  102.0 6.9 %collective-permute-start.24 = (bf16[128,896]{1,0:T(8,128)(2,1)S(1)}, bf16[128,896]{1,0:T(8,128)(2,1)S(1)}, u32[]{:S(2)}, u32[]{:S(2)}) collective-permute-start(bf16[128,896]{1,0:T(8,128)(2,1)S(1)} %get-tuple-element.72), channel_id=1, source_target_pairs={{0,2},{128,134},{2,4},{130,128},{4,6},{132,130},{6,0},{134,132},{1... | collective-permute-start | bytes 688136 | tf_op jit(solution)/shard_map/ppermute | solution.py:52
  102.5 7.3 %collective-permute-start.26 = (bf16[128,896]{1,0:T(8,128)(2,1)S(1)}, bf16[128,896]{1,0:T(8,128)(2,1)S(1)}, u32[]{:S(2)}, u32[]{:S(2)}) collective-permute-start(bf16[128,896]{1,0:T(8,128)(2,1)S(1)} %get-tuple-element.72), channel_id=1, source_target_pairs={{0,6},{128,130},{2,0},{130,132},{4,2},{132,134},{6,4},{134,128},{1... | collective-permute-start | bytes 688136 | tf_op jit(solution)/shard_map/ppermute | solution.py:52
  108.9 7.1 %collective-permute-start.25 = (bf16[64,896]{1,0:T(8,128)(2,1)S(1)}, bf16[64,896]{1,0:T(8,128)(2,1)S(1)}, u32[]{:S(2)}, u32[]{:S(2)}) collective-permute-start(bf16[64,896]{1,0:T(8,128)(2,1)S(1)} %slice.32), channel_id=1, source_target_pairs={{0,2},{128,134},{2,4},{130,128},{4,6},{132,130},{6,0},{134,132},{1... | collective-permute-start | bytes 344072 | tf_op jit(solution)/shard_map/ppermute | solution.py:52
  109.8 7.6 %collective-permute-start.27 = (bf16[64,896]{1,0:T(8,128)(2,1)S(1)}, bf16[64,896]{1,0:T(8,128)(2,1)S(1)}, u32[]{:S(2)}, u32[]{:S(2)}) collective-permute-start(bf16[64,896]{1,0:T(8,128)(2,1)S(1)} %slice.33), channel_id=1, source_target_pairs={{0,6},{128,130},{2,0},{130,132},{4,2},{132,134},{6,4},{134,128},{1... | collective-permute-start | bytes 344072 | tf_op jit(solution)/shard_map/ppermute | solution.py:52
  118.1 8.3 %collective-permute-start.28 = (bf16[4,32,896]{2,1,0:T(8,128)(2,1)S(1)}, bf16[4,32,896]{2,1,0:T(8,128)(2,1)S(1)}, u32[]{:S(2)}, u32[]{:S(2)}) collective-permute-start(bf16[4,32,896]{2,1,0:T(8,128)(2,1)S(1)} %get-tuple-element.77), channel_id=1, source_target_pairs={{0,1},{1,0},{8,9},{9,8},{16,17},{17,16},{24,25},{25,24},{2,3},{3,2... | collective-permute-start | bytes 688136 | tf_op jit(solution)/shard_map/ppermute | solution.py:44
  127.6 9.0 %collective-permute-start.30 = (bf16[2,32,896]{2,1,0:T(8,128)(2,1)S(1)}, bf16[2,32,896]{2,1,0:T(8,128)(2,1)S(1)}, u32[]{:S(2)}, u32[]{:S(2)}) collective-permute-start(bf16[2,32,896]{2,1,0:T(8,128)(2,1)S(1)} %get-tuple-element.76), channel_id=1, source_target_pairs={{0,16},{1,17},{8,24},{9,25},{16,0},{17,1},{24,8},{25,9},{2,18},{3,... | collective-permute-start | bytes 344072 | tf_op jit(solution)/shard_map/ppermute | solution.py:44
  (22 other events, 160.9 us)
